TPU v7x, 256 devices: a whole 4x4x8 slice. The times are simulated.
256 devices in a mesh: dp: 8 (over x, core), proto: 32 (over y, z).
Axes of the slice: x: 4, y: 4, z: 8, core: 2. Of those that a mesh axis runs over, the one named last changes fastest.
Arguments:
- features: bfloat16 [16384, 256], P('dp'), may hold values from -60 to 60
- prototypes: bfloat16 [32768, 256], P('proto'), may hold values from -50 to 50
- sibling_view: int32 [16384], P('dp'), may hold values from 0 to 2047, as said below
- q_seed: int32 [256, 32], replicated, may hold values from -8 to 7
Outputs:
- feature_grad: float32 [16384, 256], P(('dp', 'proto'))
- proto_grad: float32 [32768, 256], P('proto')
Inputs may be any that keep to these rules, and one draw needn't show every extreme that they name: Within each data group of 2048 rows the pairing is a perfect matching: sibling_view[sibling_view[b]] = b and sibling_view[b] != b.
All inputs are finite; a program needn't handle non-finite values.
Results may differ from a plain program's by a relative error of at most 0.0024.
Values sent between devices are 32-bit elements; how exact they have to be, the bound alone decides.
No kernel may reach another device: no remote copies, remote signals or barrier semaphores. Data moves between devices by JAX's collectives and lax.ppermute only.
A program may use at most 128 MiB of HBM per device.

v0:
```python
import jax
import jax.numpy as jnp
from jax import lax
from jax.sharding import PartitionSpec as P

SINK = 3


coolness_scaler = 0.1
entropic = 0.05
epsilon = 1e-06
highest = lax.Precision.HIGHEST


def normalize(value_rows):
    wide = value_rows.astype(jnp.float32)
    return (wide * lax.rsqrt(jnp.sum(wide * wide, axis=-1, keepdims=True) + epsilon)).astype(
        jnp.bfloat16
    )


def right_solve(lower_factor, value_rows):
    return lax.linalg.triangular_solve(
        lower_factor, value_rows, left_side=False, lower=True, transpose_a=True
    )


def on_device(features, prototypes, sibling_view, q_seed):
    unit_feat = normalize(features)
    unit_proto = normalize(prototypes)
    cluster_similarity = lax.dot_general(
        unit_feat, unit_proto, (((1,), (1,)), ((), ())), preferred_element_type=jnp.float32
    )
    energy = jnp.exp(cluster_similarity / entropic)
    rescaled_likelihood = jnp.exp(cluster_similarity / coolness_scaler)
    local_total = jnp.sum(rescaled_likelihood, axis=-1)
    exponent_sum = lax.psum(local_total, "proto")
    row_scale = jnp.ones((energy.shape[0],), jnp.float32)
    column_factor = jnp.ones((energy.shape[1],), jnp.float32)
    for sweep_index in range(SINK):
        col_total = lax.psum(jnp.dot(row_scale, energy, precision=highest), "dp")
        column_factor = 1.0 / col_total
        row_partial = jnp.dot(energy, column_factor, precision=highest)
        if sweep_index == 0:
            row_total = lax.psum(row_partial, "proto")
        else:
            row_total = lax.psum(row_partial, "proto")
        row_scale = 1.0 / row_total
    allotted_code = row_scale[:, None] * energy * column_factor[None, :]
    balanced_transport_plan = jnp.take(allotted_code, sibling_view, axis=0)
    guessed_allotment = rescaled_likelihood / exponent_sum[:, None]
    objective_slope_table = (
        (guessed_allotment - balanced_transport_plan) / coolness_scaler
    ).astype(jnp.bfloat16)
    feature_grad = lax.psum_scatter(
        jnp.dot(objective_slope_table, unit_proto, preferred_element_type=jnp.float32),
        "proto",
        scatter_dimension=0,
        tiled=True,
    )
    factor_scale = (
        unit_proto.shape[0]
        * lax.axis_size("proto")
        / (objective_slope_table.shape[0] * lax.axis_size("dp"))
    )
    part_grad = factor_scale * lax.dot_general(
        objective_slope_table,
        unit_feat,
        (((0,), (0,)), ((), ())),
        preferred_element_type=jnp.float32,
    )
    seed_basis = q_seed.astype(jnp.float32) * 0.125
    factor = lax.psum(jnp.dot(part_grad, seed_basis, precision=highest), "dp")
    inner_product_square = lax.psum(jnp.dot(factor.T, factor, precision=highest), "proto")
    lower_factor = jnp.linalg.cholesky(inner_product_square)
    basis = right_solve(lower_factor, factor)
    local_back = lax.dot_general(part_grad, basis, (((0,), (0,)), ((), ())), precision=highest)
    right_factor = lax.psum(local_back, ("dp", "proto"))
    proto_grad = jnp.dot(basis, right_factor.T, precision=highest)
    return (feature_grad, proto_grad)


def solution(mesh):
    return jax.shard_map(
        on_device,
        mesh=mesh,
        in_specs=(P("dp", None), P("proto", None), P("dp"), P()),
        out_specs=(P(("dp", "proto"), None), P("proto", None)),
        check_vma=False,
    )
```

profile of v0, /device:TPU:32, one launch (start us, length us, event | category | flops | bytes accessed | tf_op | source)
XLA Modules:
  0.0 738.1 jit_solution(9955854958041470952)
XLA Ops:
  8.0 0.0 all-reduce.3.cloned.1.call-start
  8.0 0.7 fusion.25
  8.7 0.7 compare_and_fusion
  9.4 1.6 fusion.7
  11.0 1.3 fusion.9
  12.3 3.0 fusion
  15.3 0.0 copy-start
  15.3 3.2 copy-done
  18.6 7.0 fusion.6
  25.6 14.6 %psum.71 = f32[1024]{0:T(1024)S(1)} all-reduce(f32[1024]{0:T(1024)S(1)} %bitcast.45), channel_id=1, replica_groups=mesh['dp'=8,'proto'=32] {'dp'}, use_global_device_ids=true, to_apply=%region_4.0 | all-reduce | flops 1024 | bytes 8192 | tf_op jit(solution)/shard_map/psum | solution.py:41
  40.2 7.5 %fusion.5 = f32[1,2048]{1,0:T(1,128)S(1)} fusion(f32[1024,1]{0,1:T(1,128)S(1)} %bitcast.41, f32[2048,1024]{0,1:T(8,128)} %copy-done), kind=kOutput, calls=%fused_computation.12 | convolution fusion | flops 27262976 | bytes 8400896 | tf_op jit(solution)/shard_map/dot_general | solution.py:43
  47.7 74.9 %psum.72 = f32[2048]{0:T(1024)S(1)} all-reduce(f32[2048]{0:T(1024)S(1)} %bitcast.37), channel_id=1, replica_groups=mesh['dp'=8,'proto'=32] {'proto'}, use_global_device_ids=true, to_apply=%region_5.0 | all-reduce | flops 2048 | bytes 16384 | tf_op jit(solution)/shard_map/psum | solution.py:45
  122.6 9.4 %fusion.4 = f32[1,1024]{1,0:T(1,128)S(1)} fusion(f32[2048,1]{0,1:T(1,128)S(1)} %bitcast.38, f32[2048,1024]{0,1:T(8,128)} %copy-done), kind=kOutput, calls=%fused_computation.11 | convolution fusion | flops 27262976 | bytes 8400896 | tf_op jit(solution)/shard_map/dot_general | solution.py:41
  132.0 12.4 %psum.73 = f32[1024]{0:T(1024)S(1)} all-reduce(f32[1024]{0:T(1024)S(1)} %bitcast.42), channel_id=1, replica_groups=mesh['dp'=8,'proto'=32] {'dp'}, use_global_device_ids=true, to_apply=%region_6.0 | all-reduce | flops 1024 | bytes 8192 | tf_op jit(solution)/shard_map/psum | solution.py:41
  144.4 7.5 %fusion.3 = f32[1,2048]{1,0:T(1,128)S(1)} fusion(f32[1024,1]{0,1:T(1,128)S(1)} %bitcast.43, f32[2048,1024]{0,1:T(8,128)} %copy-done), kind=kOutput, calls=%fused_computation.10 | convolution fusion | flops 27262976 | bytes 8400896 | tf_op jit(solution)/shard_map/dot_general | solution.py:43
  151.9 75.0 %psum.74 = f32[2048]{0:T(1024)S(1)} all-reduce(f32[2048]{0:T(1024)S(1)} %bitcast.39), channel_id=1, replica_groups=mesh['dp'=8,'proto'=32] {'proto'}, use_global_device_ids=true, to_apply=%region_7.0 | all-reduce | flops 2048 | bytes 16384 | tf_op jit(solution)/shard_map/psum | solution.py:47
  226.9 9.4 %fusion.2 = f32[1,1024]{1,0:T(1,128)S(1)} fusion(f32[2048,1]{0,1:T(1,128)S(1)} %bitcast.40, f32[2048,1024]{0,1:T(8,128)} %copy-done), kind=kOutput, calls=%fused_computation.9 | convolution fusion | flops 27262976 | bytes 8400896 | tf_op jit(solution)/shard_map/dot_general | solution.py:41
  236.2 12.4 %psum.75 = f32[1024]{0:T(1024)S(1)} all-reduce(f32[1024]{0:T(1024)S(1)} %bitcast.44), channel_id=1, replica_groups=mesh['dp'=8,'proto'=32] {'dp'}, use_global_device_ids=true, to_apply=%region_8.0 | all-reduce | flops 1024 | bytes 8192 | tf_op jit(solution)/shard_map/psum | solution.py:41
  248.7 7.5 %fusion.1 = f32[1,2048]{1,0:T(1,128)S(1)} fusion(f32[1024,1]{0,1:T(1,128)S(1)} %bitcast.35, f32[2048,1024]{0,1:T(8,128)} %copy-done), kind=kOutput, calls=%fused_computation.8 | convolution fusion | flops 27262976 | bytes 8400896 | tf_op jit(solution)/shard_map/dot_general | solution.py:43
  256.1 134.5 %all-reduce = (f32[2048]{0:T(1024)S(1)}, f32[2048]{0:T(1024)S(1)}) all-reduce(f32[2048]{0:T(1024)S(1)} %bitcast.36, f32[2048]{0:T(1024)S(1)} %get-tuple-element.4), channel_id=1, replica_groups=mesh['dp'=8,'proto'=32] {'proto'}, use_global_device_ids=true, to_apply=%region_9.0 | all-reduce | flops 4096 | bytes 32768 | tf_op jit(solution)/shard_map/psum | solution.py:47
  390.7 6.3 multiply_multiply_fusion
  397.0 9.3 %copy.6 = f32[2048,1024]{1,0:T(8,128)} copy(f32[2048,1024]{0,1:T(8,128)} %multiply_multiply_fusion) | data formatting | bytes 16777216 | tf_op jit(solution)/shard_map/mul | solution.py:49
  406.2 15.2 %gather_fusion = f32[2048,1024]{1,0:T(8,128)} fusion(f32[2048,1024]{1,0:T(8,128)} %copy.6, s32[2048]{0:T(1024)S(1)} %fusion.25), kind=kCustom, calls=%fused_computation | custom fusion | bytes 16785408 | tf_op jit(solution)/shard_map/jit(_take)/gather | solution.py:50
  421.4 9.1 %copy.7 = f32[2048,1024]{0,1:T(8,128)} copy(f32[2048,1024]{1,0:T(8,128)} %gather_fusion) | data formatting | bytes 16777216 | tf_op jit(solution)/shard_map/jit(_take)/gather | solution.py:50
  430.5 0.0 copy-start.1
  430.5 0.0 copy-start.4
  430.5 7.1 multiply_convert_fusion
  437.6 0.0 copy-done.1
  437.6 0.0 copy-start.2
  437.7 0.0 copy-start.3
  437.7 1.4 convolution_multiply_fusion
  439.0 0.5 copy-done.2
  439.6 0.0 copy-done.4
  439.6 1.7 fusion.17
  441.3 0.0 all-reduce.3.cloned.1.call-update
  441.3 0.0 reduce-scatter.2.cloned.1.call-start
  441.4 0.0 copy-done.3
  441.4 5.1 fusion.14
  446.4 0.0 reduce-scatter.2.cloned.1.call-update
  446.5 55.6 %all-reduce.3.cloned.1.call-done = f32[1024,32]{0,1:T(8,128)} async-done(((f32[1024,32]{0,1:T(8,128)}), f32[1024,32]{0,1:T(8,128)}) %all-reduce.3.cloned.1.call-update) | async-done | bytes 131088 | tf_op jit(solution)/shard_map/psum | solution.py:73
  502.1 1.2 fusion.35
  503.3 138.4 %psum.78 = f32[32,32]{0,1:T(8,128)S(1)} all-reduce(f32[32,32]{0,1:T(8,128)S(1)} %fusion.35), channel_id=1, replica_groups=mesh['dp'=8,'proto'=32] {'proto'}, use_global_device_ids=true, to_apply=%region_12.13 | all-reduce | flops 1024 | bytes 8192 | tf_op jit(solution)/shard_map/psum | solution.py:74
  641.8 0.1 copy.9
  641.9 2.9 cholesky.16
  644.8 0.6 compare_reduce_fusion
  645.5 0.7 fusion.20
  646.1 2.4 custom-call.6
  648.5 1.2 fusion.21
  649.8 1.8 fusion.36
  651.6 77.0 %psum.79 = f32[256,32]{1,0:T(8,128)S(1)} all-reduce(f32[256,32]{1,0:T(8,128)S(1)} %fusion.36), channel_id=1, replica_groups=mesh['dp'=8,'proto'=32] {'dp','proto'}, use_global_device_ids=true, to_apply=%region_15.16 | all-reduce | flops 8192 | bytes 65536 | tf_op jit(solution)/shard_map/psum | solution.py:78
  728.6 2.0 fusion.37
  730.6 0.0 reduce-scatter.2.cloned.1.call-done
  (10 shorter events, 0.1 us)
Async XLA Ops:
  8.0 494.1 %all-reduce.3.cloned.1.call-start = ((), (), s32[]{:S(2)}) async-start(), calls=%async_computation.2 | async-start | bytes 262144 | tf_op jit(solution)/shard_map/psum | solution.py:73
  15.3 3.2 copy-start
  430.5 7.1 copy-start.1
  430.5 9.1 %copy-start.4 = (s32[256,32]{0,1:T(8,128)S(1)}, s32[256,32]{0,1:T(8,128)}, u32[]{:S(2)}) copy-start(s32[256,32]{0,1:T(8,128)} %param.7) | copy-start | bytes 98308
  437.6 1.9 copy-start.2
  437.7 3.7 copy-start.3
  441.3 289.3 %reduce-scatter.2.cloned.1.call-start = ((), (), s32[]{:S(2)}) async-start(), calls=%async_computation.1 | async-start | bytes 2162688 | tf_op jit(solution)/shard_map/reduce_scatter | solution.py:55
Sparse Core Ops, SparseCore 0:
  441.4 60.6 all-reduce.2
Sparse Core Ops, SparseCore 1:
  446.5 211.6 reduce-scatter.1
where the time goes:
time: 740 us; the launch traced here: 738 us
  blocking collectives  539 us (73%)
  matrix products  65.6 us (9%)
  waiting for transfers between devices  55.7 us (8%)
  local copies, waits for them, and re-layouts  37.4 us (5%)
  other arithmetic  24.4 us (3%)
  between operations  15.6 us (2%)
    psum x3, blocking collectives, on_device(): row_total = lax.psum(row_partial, 'proto')  284 us
    psum x1, blocking collectives, on_device(): lax.psum(jnp.dot(factor.T, factor, precision=highest), 'proto')  138 us
    psum x1, blocking collectives, on_device(): right_factor = lax.psum(local_back, ('dp', 'proto'))  77 us
    psum x1, waiting for transfers between devices, on_device(): factor = lax.psum(jnp.dot(part_grad, seed_basis, precision=highest), 'dp')  55.6 us
    psum x3, blocking collectives, on_device(): col_total = lax.psum(jnp.dot(row_scale, energy, precision=highest), 'dp')  39.5 us
    dot_general x3, matrix products, on_device(): col_total = lax.psum(jnp.dot(row_scale, energy, precision=highest), 'dp')  25.7 us
    gather x2, local copies, waits for them, and re-layouts, on_device(): balanced_transport_plan = jnp.take(allotted_code, sibling_view, axis=0)  24.3 us
    dot_general x3, matrix products, on_device(): row_partial = jnp.dot(energy, column_factor, precision=highest)  22.4 us
  transfers between devices with their start and end apart: 2, of which 1 were waited for; matrix products, arithmetic and copies ran while one was open for 2% of the time, Pallas kernels for 0%

commit v1 on v0

v1 whole, which is shorter than its diff:
```python
import jax
import jax.numpy as jnp
from jax import lax
from jax.sharding import Mesh, PartitionSpec as P

SINK = 3
epsilon = 1e-06
highest = lax.Precision.HIGHEST


def normalize(value_rows):
    wide = value_rows.astype(jnp.float32)
    return (wide * lax.rsqrt(jnp.sum(wide * wide, axis=-1, keepdims=True) + epsilon)).astype(
        jnp.bfloat16
    )


def sum_over(value, axes):
    copies = jnp.broadcast_to(value[None], (lax.axis_size(axes),) + value.shape)
    return jnp.sum(lax.all_to_all(copies, axes, 0, 0), axis=0)


def sum_core(value):
    return value + lax.ppermute(value, "c", [(0, 1), (1, 0)])


def scatter_over(value, axes):
    count = lax.axis_size(axes)
    parts = value.reshape((count, value.shape[0] // count) + value.shape[1:])
    return jnp.sum(lax.all_to_all(parts, axes, 0, 0), axis=0)


def on_device(features, prototypes, sibling_view, q_seed):
    unit_feat = normalize(features)
    unit_proto = normalize(prototypes)
    rows, feat = unit_feat.shape
    protos = unit_proto.shape[0]
    total_rows = rows * lax.axis_size(("x", "c"))
    total_protos = protos * lax.axis_size(("y", "z"))

    def scores(block):
        return lax.dot_general(
            block, unit_proto, (((1,), (1,)), ((), ())), preferred_element_type=jnp.float32
        )

    likelihood = jnp.exp(scores(unit_feat) / 0.1)
    energy = likelihood * likelihood
    local_total = jnp.sum(likelihood, axis=-1)
    sibling_feat = jnp.take(unit_feat, sibling_view, axis=0)
    sibling_energy = jnp.exp(scores(sibling_feat) / 0.05)

    col_part = jnp.sum(energy, axis=0)
    for sweep in range(SINK):
        col_total = sum_over(col_part.reshape(-1, 128), ("x", "c")).reshape(-1)
        column_factor = 1.0 / col_total
        if sweep < SINK - 1:
            row_part = jnp.sum(energy * column_factor[None, :], axis=1)
            row_total = sum_over(row_part.reshape(-1, 128), ("y", "z")).reshape(-1)
            row_scale = 1.0 / row_total
            col_part = jnp.sum(energy * row_scale[:, None], axis=0)
        else:
            row_part = jnp.sum(sibling_energy * column_factor[None, :], axis=1)
            both = jnp.concatenate([row_part, local_total]).reshape(-1, 128)
            both = sum_over(both, ("y", "z")).reshape(2, rows)
            sibling_scale = 1.0 / both[0]
            exponent_sum = both[1]
    target = sibling_scale[:, None] * sibling_energy * column_factor[None, :]
    predicted = likelihood / exponent_sum[:, None]
    gradient = ((predicted - target) / 0.1).astype(jnp.bfloat16)

    part_grad = (total_protos / total_rows) * lax.dot_general(
        gradient, unit_feat, (((0,), (0,)), ((), ())), preferred_element_type=jnp.float32
    )
    seed_basis = q_seed.astype(jnp.float32) * 0.125
    factor = jnp.dot(part_grad, seed_basis, precision=highest)
    rank = factor.shape[1]
    factor = sum_core(factor.reshape(-1, 128))
    factor = sum_over(factor, "x").reshape(protos, rank)
    mixed = lax.dot_general(part_grad, factor, (((0,), (0,)), ((), ())), precision=highest)
    mixed = sum_core(mixed.reshape(-1, 128))
    mixed = sum_over(mixed, ("x", "y"))
    mixed = sum_over(mixed, "z").reshape(feat, rank)
    gramian = lax.dot_general(seed_basis, mixed, (((0,), (0,)), ((), ())), precision=highest)
    lower_factor = jnp.linalg.cholesky(0.5 * (gramian + gramian.T))
    half = lax.linalg.triangular_solve(lower_factor, mixed.T, left_side=True, lower=True)
    weights = lax.linalg.triangular_solve(
        lower_factor, half, left_side=True, lower=True, transpose_a=True
    )
    proto_grad = jnp.dot(factor, weights, precision=highest)

    row_grad = jnp.dot(gradient, unit_proto, preferred_element_type=jnp.float32)
    feature_grad = scatter_over(scatter_over(row_grad, "y"), "z")
    return (feature_grad, proto_grad)


def solution(mesh):
    wide, tall = mesh.shape["dp"], mesh.shape["proto"]
    fine = Mesh(mesh.devices.reshape(wide // 2, 2, 4, tall // 4), ("x", "c", "y", "z"))
    dp, proto = ("x", "c"), ("y", "z")
    return jax.shard_map(
        on_device,
        mesh=fine,
        in_specs=(P(dp, None), P(proto, None), P(dp), P()),
        out_specs=(P(dp + proto, None), P(proto, None)),
        check_vma=False,
    )
```

time: 740 us -> 234 us (0.32)
  blocking collectives: 539 us -> 92.3 us
  matrix products: 65.6 us -> 21.6 us
  local copies, waits for them, and re-layouts: 37.4 us -> 10.9 us
  starting transfers between devices: 0.08 us -> 20.7 us
  other arithmetic: 24.4 us -> 39.6 us
  between operations: 15.6 us -> 1 us
  waiting for transfers between devices: 55.7 us -> 44.9 us
    psum x8 -> x0, blocking collectives: 539 us -> none  [the longest x3 284 us: on_device(): row_total = lax.psum(row_partial, 'proto')]
    all_to_all x0 -> x6, blocking collectives: none -> 92.3 us  [sum_over(): return jnp.sum(lax.all_to_all(copies, axes, 0, 0), axis=0)]
    psum x1 -> x0, waiting for transfers between devices: 55.6 us -> none  [on_device(): factor = lax.psum(jnp.dot(part_grad, seed_basis, precision=highest), 'dp')]
    dot_general x13 -> x8, matrix products: 64.3 us -> 21.2 us  [the longest x2 10.1 us: scores(): lax.dot_general(block, unit_proto, (((1,), (1,)), ((), ())), preferred_el...]
    all_to_all x0 -> x5, waiting for transfers between devices: none -> 42.4 us  [the longest x2 26 us: scatter_over(): return jnp.sum(lax.all_to_all(parts, axes, 0, 0), axis=0)]
    reduce_sum x0 -> x15, other arithmetic: none -> 20.9 us  [the longest x2 10.2 us: on_device(): row_part = jnp.sum(energy * column_factor[None, :], axis=1)]
    all_to_all x0 -> x5, starting transfers between devices: none -> 20.5 us  [the longest x3 11.8 us: sum_over(): return jnp.sum(lax.all_to_all(copies, axes, 0, 0), axis=0)]
    gather x2 -> x1, local copies, waits for them, and re-layouts: 24.3 us -> 7.5 us  [on_device(): sibling_feat = jnp.take(unit_feat, sibling_view, axis=0)]
  transfers between devices with their start and end apart: 2 -> 7, of which waited for: 1 -> 6; matrix products, arithmetic and copies ran while one was open for 2% -> 9% of each run, Pallas kernels for 0% -> 0%
where the time goes in v1:
time: 234 us; the launch traced here: 231 us
  blocking collectives  92.3 us (39%)
  waiting for transfers between devices  44.9 us (19%)
  other arithmetic  39.6 us (17%)
  matrix products  21.6 us (9%)
  starting transfers between devices  20.7 us (9%)
  local copies, waits for them, and re-layouts  10.9 us (5%)
    all_to_all x6, blocking collectives, sum_over(): return jnp.sum(lax.all_to_all(copies, axes, 0, 0), axis=0)  92.3 us
    all_to_all x2, waiting for transfers between devices, scatter_over(): return jnp.sum(lax.all_to_all(parts, axes, 0, 0), axis=0)  26 us
    all_to_all x3, waiting for transfers between devices, sum_over(): return jnp.sum(lax.all_to_all(copies, axes, 0, 0), axis=0)  16.4 us
    all_to_all x3, starting transfers between devices, sum_over(): return jnp.sum(lax.all_to_all(copies, axes, 0, 0), axis=0)  11.8 us
    reduce_sum x2, other arithmetic, on_device(): row_part = jnp.sum(energy * column_factor[None, :], axis=1)  10.2 us
    dot_general x2, matrix products, scores(): lax.dot_general(block, unit_proto, (((1,), (1,)), ((), ())), preferred_el...  10.1 us
    reduce_sum x2, other arithmetic, on_device(): col_part = jnp.sum(energy * row_scale[:, None], axis=0)  8.9 us
    all_to_all x2, starting transfers between devices, scatter_over(): return jnp.sum(lax.all_to_all(parts, axes, 0, 0), axis=0)  8.69 us
  transfers between devices with their start and end apart: 7, of which 6 were waited for; matrix products, arithmetic and copies ran while one was open for 9% of the time, Pallas kernels for 0%

profile of v1, /device:TPU:32, one launch (start us, length us, event | category | flops | bytes accessed | tf_op | source)
XLA Modules:
  0.0 231.0 jit_solution(9981072955788542693)
XLA Ops:
  0.6 1.3 fusion.5
  1.9 1.6 fusion.3
  3.5 1.6 fusion.4
  5.1 5.9 %fusion.2 = (f32[1024]{0:T(1024)S(1)}, f32[2048,1024]{1,0:T(8,128)}) fusion(bf16[2048,256]{1,0:T(8,128)(2,1)S(1)} %fusion.4, bf16[1024,256]{1,0:T(8,128)(2,1)} %param.5, f32[1024]{0:T(1024)S(1)} %add_rsqrt_fusion.1), kind=kOutput, calls=%fused_computation.13 | convolution fusion | flops 1080818688 | bytes 9969664 | tf_op jit(solution)/shard_map/dot_general | solution.py:42
  11.0 9.5 %all_to_all.55 = f32[8,8,128]{2,1,0:T(8,128)S(1)} all-to-all(f32[8,8,128]{2,1,0:T(8,128)S(1)} %broadcast_in_dim.45), channel_id=1, replica_groups=mesh['x'=4,'c'=2,'y'=4,'z'=8] {'x','c'}, dimensions={0} | all-to-all | bytes 65536 | tf_op jit(solution)/shard_map/all_to_all | solution.py:20
  20.5 5.1 %multiply_reduce_fusion.4 = f32[2048]{0:T(1024)S(1)} fusion(f32[1024]{0:T(1024)S(1)} %divide_bitcast_fusion.4, f32[2048,1024]{1,0:T(8,128)} %get-tuple-element.7), kind=kLoop, calls=%fused_computation.6 | loop fusion | flops 8386560 | bytes 8400896 | tf_op jit(solution)/shard_map/reduce_sum | solution.py:57
  25.6 23.4 %all_to_all.56 = f32[32,16,128]{2,1,0:T(8,128)S(1)} all-to-all(f32[32,16,128]{2,1,0:T(8,128)S(1)} %broadcast_in_dim.87), channel_id=1, replica_groups=mesh['x'=4,'c'=2,'y'=4,'z'=8] {'y','z'}, dimensions={0} | all-to-all | bytes 524288 | tf_op jit(solution)/shard_map/all_to_all | solution.py:20
  49.1 0.0 copy-start.3
  49.1 4.3 %multiply_reduce_fusion.3 = f32[1024]{0:T(1024)S(1)} fusion(f32[2048]{0:T(1024)S(1)} %divide_bitcast_fusion.1, f32[2048,1024]{1,0:T(8,128)} %get-tuple-element.7), kind=kLoop, calls=%fused_computation.5 | loop fusion | flops 8387584 | bytes 8400896 | tf_op jit(solution)/shard_map/reduce_sum | solution.py:60
  53.4 7.8 %all_to_all.57 = f32[8,8,128]{2,1,0:T(8,128)S(1)} all-to-all(f32[8,8,128]{2,1,0:T(8,128)S(1)} %broadcast_in_dim.89), channel_id=1, replica_groups=mesh['x'=4,'c'=2,'y'=4,'z'=8] {'x','c'}, dimensions={0} | all-to-all | bytes 65536 | tf_op jit(solution)/shard_map/all_to_all | solution.py:20
  61.2 5.1 %multiply_reduce_fusion.2 = f32[2048]{0:T(1024)S(1)} fusion(f32[1024]{0:T(1024)S(1)} %divide_bitcast_fusion.3, f32[2048,1024]{1,0:T(8,128)} %get-tuple-element.7), kind=kLoop, calls=%fused_computation.4 | loop fusion | flops 8386560 | bytes 8400896 | tf_op jit(solution)/shard_map/reduce_sum | solution.py:57
  66.3 0.7 broadcast_in_dim.91
  67.1 4.6 %all-to-all-start.3 = ((f32[32,16,128]{2,1,0:T(8,128)}), f32[32,16,128]{2,1,0:T(8,128)S(1)}, u32[]{:S(2)}, u32[]{:S(2)}) async-start(f32[32,16,128]{2,1,0:T(8,128)} %broadcast_in_dim.91), calls=%async_computation.3 | async-start | bytes 524288 | tf_op jit(solution)/shard_map/all_to_all | solution.py:20
  71.6 0.0 copy-done.3
  71.7 12.2 %all-to-all-done.3 = f32[32,16,128]{2,1,0:T(8,128)S(1)} async-done(((f32[32,16,128]{2,1,0:T(8,128)}), f32[32,16,128]{2,1,0:T(8,128)S(1)}, u32[]{:S(2)}, u32[]{:S(2)}) %all-to-all-start.3) | async-done | bytes 262176 | tf_op jit(solution)/shard_map/all_to_all | solution.py:20
  83.9 0.0 copy-start.1
  83.9 4.6 %multiply_reduce_fusion.1 = (f32[1024]{0:T(1024)S(1)}, f32[2048]{0:T(1024)S(1)}) fusion(f32[2048]{0:T(1024)S(1)} %divide_bitcast_fusion, f32[2048,1024]{1,0:T(8,128)} %get-tuple-element.7), kind=kLoop, calls=%fused_computation.3 | loop fusion | flops 10482688 | bytes 8409088 | tf_op jit(solution)/shard_map/reduce_sum | solution.py:60
  88.5 0.6 broadcast_in_dim.93
  89.1 3.3 %all-to-all-start.4 = ((f32[8,8,128]{2,1,0:T(8,128)}), f32[8,8,128]{2,1,0:T(8,128)S(1)}, u32[]{:S(2)}, u32[]{:S(2)}) async-start(f32[8,8,128]{2,1,0:T(8,128)} %broadcast_in_dim.93), calls=%async_computation.4 | async-start | bytes 65536 | tf_op jit(solution)/shard_map/all_to_all | solution.py:20
  92.5 7.5 %gather_fusion = bf16[2048,256]{1,0:T(8,128)(2,1)S(1)} fusion(bf16[2048,256]{1,0:T(8,128)(2,1)S(1)} %fusion.4, s32[2048]{0:T(1024)S(1)} %fusion.23), kind=kCustom, calls=%fused_computation | custom fusion | bytes 2105344 | tf_op jit(solution)/shard_map/jit(_take)/gather | solution.py:49
  100.0 0.0 all-to-all-done.4
  100.1 0.0 copy-done.1
  100.1 4.2 %multiply_reduce_fusion = (f32[2048]{0:T(1024)S(1)}, f32[2048,1024]{1,0:T(8,128)}) fusion(f32[1024]{0:T(1024)S(1)} %divide_bitcast_fusion.2, bf16[1024,256]{1,0:T(8,128)(2,1)S(1)} %copy-done.1, f32[1024]{0:T(1024)S(1)} %add_rsqrt_fusion.1, bf16[2048,256]{1,0:T(8,128)(2,1)S(1)} %gather_fusion, pred[2048]{0:T(1024)(128)(4,1)S(1)} %compare_and_fusion), kind=kOutput, calls=%fused_computation.2 | convolution fusion | flops 1081341952 | bytes 9979904 | tf_op jit(solution)/shard_map/dot_general | solution.py:42
  104.3 0.1 broadcast_in_dim.94
  104.3 22.6 %all_to_all.58 = f32[32,32,128]{2,1,0:T(8,128)S(1)} all-to-all(f32[32,32,128]{2,1,0:T(8,128)S(1)} %broadcast_in_dim.94), channel_id=1, replica_groups=mesh['x'=4,'c'=2,'y'=4,'z'=8] {'y','z'}, dimensions={0} | all-to-all | bytes 1048576 | tf_op jit(solution)/shard_map/all_to_all | solution.py:20
  127.0 7.5 %multiply_convert_fusion = bf16[2048,1024]{1,0:T(8,128)(2,1)S(1)} fusion(f32[2048,1024]{1,0:T(8,128)} %get-tuple-element.9, f32[2048,1024]{1,0:T(8,128)} %get-tuple-element.7, f32[2048]{0:T(1024)S(1)} %get-tuple-element.5, f32[2048]{0:T(1024)S(1)} %get-tuple-element.4, f32[1024]{0:T(1024)S(1)} %divide_bitcast_fusion.2), kind=kLoop, calls=%fused_computation.1 | loop fusion | flops 16777216 | bytes 20992000 | tf_op jit(solution)/shard_map/convert_element_type | solution.py:69
  134.5 0.0 copy-start
  134.5 0.0 copy-start.2
  134.5 1.3 convolution_multiply_fusion
  135.8 0.6 copy-done
  136.4 0.0 copy-done.2
  136.4 1.0 fusion.12
  137.4 0.2 reshape.116
  137.5 0.1 collective-permute-start
  137.7 1.3 collective-permute-done
  139.0 14.0 %all_to_all.59 = f32[4,256,128]{2,1,0:T(8,128)S(1)} all-to-all(f32[4,256,128]{2,1,0:T(8,128)S(1)} %broadcast_in_dim.95), channel_id=1, replica_groups=mesh['x'=4,'c'=2,'y'=4,'z'=8] {'x'}, dimensions={0} | all-to-all | bytes 1048576 | tf_op jit(solution)/shard_map/all_to_all | solution.py:20
  153.1 0.2 reshape.117
  153.3 1.8 fusion.32
  155.1 0.1 reshape.118
  155.2 0.1 collective-permute-start.1
  155.3 1.2 collective-permute-done.1
  156.5 15.0 %all_to_all.60 = f32[16,64,128]{2,1,0:T(8,128)S(1)} all-to-all(f32[16,64,128]{2,1,0:T(8,128)S(1)} %broadcast_in_dim.96), channel_id=1, replica_groups=mesh['x'=4,'c'=2,'y'=4,'z'=8] {'x','y'}, dimensions={0} | all-to-all | bytes 1048576 | tf_op jit(solution)/shard_map/all_to_all | solution.py:20
  171.5 0.7 broadcast_in_dim.97
  172.3 3.9 %all-to-all-start.10 = ((f32[8,64,128]{2,1,0:T(8,128)}), f32[8,64,128]{2,1,0:T(8,128)S(1)}, u32[]{:S(2)}, u32[]{:S(2)}) async-start(f32[8,64,128]{2,1,0:T(8,128)} %broadcast_in_dim.97), calls=%async_computation.10 | async-start | bytes 524288 | tf_op jit(solution)/shard_map/all_to_all | solution.py:20
  176.1 4.9 %fusion.27 = f32[2048,256]{1,0:T(8,128)} fusion(bf16[2048,1024]{1,0:T(8,128)(2,1)} %copy-done, bf16[1024,256]{1,0:T(8,128)(2,1)S(1)} %copy-done.1, f32[1024]{0:T(1024)S(1)} %add_rsqrt_fusion.1), kind=kOutput, calls=%fused_computation.60 | convolution fusion | flops 1074528256 | bytes 6819840 | tf_op jit(solution)/shard_map/dot_general | solution.py:91
  181.0 4.2 %all-to-all-done.10 = f32[8,64,128]{2,1,0:T(8,128)S(1)} async-done(((f32[8,64,128]{2,1,0:T(8,128)}), f32[8,64,128]{2,1,0:T(8,128)S(1)}, u32[]{:S(2)}, u32[]{:S(2)}) %all-to-all-start.10) | async-done | bytes 262176 | tf_op jit(solution)/shard_map/all_to_all | solution.py:20
  185.2 3.6 %all-to-all-start.6 = ((f32[4,512,256]{2,1,0:T(8,128)}), f32[4,512,256]{2,1,0:T(8,128)S(1)}, u32[]{:S(2)}, u32[]{:S(2)}) async-start(f32[4,512,256]{2,1,0:T(8,128)} %bitcast.48), calls=%async_computation.6 | async-start | bytes 4194304 | tf_op jit(solution)/shard_map/all_to_all | solution.py:30
  188.8 0.1 reshape.119
  188.9 0.2 fusion.11
  189.1 0.1 copy.15
  189.2 2.9 %cholesky.16 = f32[32,32]{1,0:T(8,128)S(1)} custom-call(f32[32,32]{1,0:T(8,128)S(1)} %fusion.19), custom_call_target="Cholesky" | custom-call | tf_op jit(solution)/shard_map/jit(cholesky)/cholesky | solution.py:84
  192.2 0.6 compare_reduce_fusion
  192.8 19.6 %all-to-all-done.6 = f32[4,512,256]{2,1,0:T(8,128)S(1)} async-done(((f32[4,512,256]{2,1,0:T(8,128)}), f32[4,512,256]{2,1,0:T(8,128)S(1)}, u32[]{:S(2)}, u32[]{:S(2)}) %all-to-all-start.6) | async-done | bytes 2097184 | tf_op jit(solution)/shard_map/all_to_all | solution.py:30
  212.4 1.0 reduce_sum.195
  213.4 5.1 %all-to-all-start.7 = ((f32[8,64,256]{2,1,0:T(8,128)}), f32[8,64,256]{2,1,0:T(8,128)S(1)}, u32[]{:S(2)}, u32[]{:S(2)}) async-start(f32[8,64,256]{2,1,0:T(8,128)} %bitcast.49), calls=%async_computation.7 | async-start | bytes 1048576 | tf_op jit(solution)/shard_map/all_to_all | solution.py:30
  218.4 0.7 fusion.13
  219.1 2.4 %custom-call.8 = f32[1,32,32]{1,2,0:T(8,128)S(1)} custom-call(f32[1,32,32]{2,1,0:T(8,128)S(1)} %fusion.13), custom_call_target="InvertDiagBlocksLowerTriangular" | custom-call | tf_op jit(solution)/shard_map/triangular_solve | solution.py:86
  221.5 0.3 fusion.16
  221.8 0.2 fusion.14
  222.0 1.9 fusion.33
  223.9 6.4 %all-to-all-done.7 = f32[8,64,256]{2,1,0:T(8,128)S(1)} async-done(((f32[8,64,256]{2,1,0:T(8,128)}), f32[8,64,256]{2,1,0:T(8,128)S(1)}, u32[]{:S(2)}, u32[]{:S(2)}) %all-to-all-start.7) | async-done | bytes 524320 | tf_op jit(solution)/shard_map/all_to_all | solution.py:30
  230.4 0.7 reduce_sum.196
  (29 shorter events, 0.5 us)
Async XLA Ops:
  49.1 22.6 %copy-start.3 = (s32[2048]{0:T(1024)S(1)}, s32[2048]{0:T(1024)}, u32[]{:S(2)}) copy-start(s32[2048]{0:T(1024)} %param.6) | copy-start | bytes 24580
  67.1 16.8 %all-to-all-start.3 = ((f32[32,16,128]{2,1,0:T(8,128)}), f32[32,16,128]{2,1,0:T(8,128)S(1)}, u32[]{:S(2)}, u32[]{:S(2)}) async-start(f32[32,16,128]{2,1,0:T(8,128)} %broadcast_in_dim.91), calls=%async_computation.3 | async-start | bytes 524288 | tf_op jit(solution)/shard_map/all_to_all | solution.py:20
  83.9 16.1 %copy-start.1 = (bf16[1024,256]{1,0:T(8,128)(2,1)S(1)}, bf16[1024,256]{1,0:T(8,128)(2,1)}, u32[]{:S(2)}) copy-start(bf16[1024,256]{1,0:T(8,128)(2,1)} %param.5) | copy-start | bytes 1572868
  89.1 10.9 %all-to-all-start.4 = ((f32[8,8,128]{2,1,0:T(8,128)}), f32[8,8,128]{2,1,0:T(8,128)S(1)}, u32[]{:S(2)}, u32[]{:S(2)}) async-start(f32[8,8,128]{2,1,0:T(8,128)} %broadcast_in_dim.93), calls=%async_computation.4 | async-start | bytes 65536 | tf_op jit(solution)/shard_map/all_to_all | solution.py:20
  134.5 1.9 copy-start
  134.5 1.9 copy-start.2
  137.5 1.4 collective-permute-start
  155.2 1.3 collective-permute-start.1
  172.3 12.9 %all-to-all-start.10 = ((f32[8,64,128]{2,1,0:T(8,128)}), f32[8,64,128]{2,1,0:T(8,128)S(1)}, u32[]{:S(2)}, u32[]{:S(2)}) async-start(f32[8,64,128]{2,1,0:T(8,128)} %broadcast_in_dim.97), calls=%async_computation.10 | async-start | bytes 524288 | tf_op jit(solution)/shard_map/all_to_all | solution.py:20
  185.2 27.2 %all-to-all-start.6 = ((f32[4,512,256]{2,1,0:T(8,128)}), f32[4,512,256]{2,1,0:T(8,128)S(1)}, u32[]{:S(2)}, u32[]{:S(2)}) async-start(f32[4,512,256]{2,1,0:T(8,128)} %bitcast.48), calls=%async_computation.6 | async-start | bytes 4194304 | tf_op jit(solution)/shard_map/all_to_all | solution.py:30
  213.4 17.0 %all-to-all-start.7 = ((f32[8,64,256]{2,1,0:T(8,128)}), f32[8,64,256]{2,1,0:T(8,128)S(1)}, u32[]{:S(2)}, u32[]{:S(2)}) async-start(f32[8,64,256]{2,1,0:T(8,128)} %bitcast.49), calls=%async_computation.7 | async-start | bytes 1048576 | tf_op jit(solution)/shard_map/all_to_all | solution.py:30

commit v2 on v1

v2 whole, which is shorter than its diff:
```python
import functools
import math

import jax
import jax.numpy as jnp
from jax import lax
from jax.experimental import pallas as pl
from jax.experimental.pallas import tpu as pltpu
from jax.sharding import Mesh, PartitionSpec as P

epsilon = 1e-06
highest = lax.Precision.HIGHEST
F32, BF16 = jnp.float32, jnp.bfloat16
LANES = 128
BLOCK = 256
UNROLL = 4
MIB = 1 << 20

nt = (((1,), (1,)), ((), ()))
nn = (((1,), (0,)), ((), ()))
tn = (((0,), (0,)), ((), ()))


def dot32(a, b, dims):
    return lax.dot_general(a, b, dims, precision=highest, preferred_element_type=F32)


def dot16(a, b, dims):
    return lax.dot_general(a, b, dims, preferred_element_type=F32)


def unit_rows(block):
    wide = block.astype(F32)
    return (wide * lax.rsqrt(jnp.sum(wide * wide, axis=-1, keepdims=True) + epsilon)).astype(BF16)


def across(partial):
    count = partial.shape[0] // LANES
    return jnp.concatenate(
        [jnp.sum(partial[i * LANES:(i + 1) * LANES].T, axis=0, keepdims=True) for i in range(count)],
        axis=0,
    )


def down(rows):
    return jnp.concatenate(
        [jnp.broadcast_to(rows[i:i + 1], (LANES, LANES)).T for i in range(rows.shape[0])], axis=0
    )


def tile(j):
    return slice(j * LANES, (j + 1) * LANES)


def fold(value):
    return jnp.sum(value.reshape(-1, 8, LANES), axis=0)


def copies(ref, value):
    for i in range(ref.shape[0]):
        ref[i] = value


def scores_kernel(feat, proto, sibling, seed_t, unit_feat_t, unit_proto, like, energy, col_out, total,
                  basis_t, unit_feat):
    rows, protos = feat.shape[0], proto.shape[0]
    tiles = protos // LANES
    basis_t[...] = seed_t[...].astype(F32) * 0.125
    unit_proto[...] = unit_rows(proto[...])

    def step(i, cols):
        here = pl.ds(pl.multiple_of(i * BLOCK, BLOCK), BLOCK)
        unit = unit_rows(feat[here, :])
        unit_feat[here, :] = unit
        unit_feat_t[:, here] = unit.T
        value = jnp.exp(dot16(unit, unit_proto[...], nt) * 10.0)
        like[here, :] = value
        part = value[:, tile(0)]
        for j in range(1, tiles):
            part = part + value[:, tile(j)]
        total[pl.ds(i, 1)] = across(part)[None]
        square = value * value
        return tuple(cols[j] + fold(square[:, tile(j)]) for j in range(tiles))

    cols = lax.fori_loop(
        0, rows // BLOCK, step, tuple(jnp.zeros((8, LANES), F32) for _ in range(tiles)), unroll=UNROLL
    )
    copies(col_out, jnp.concatenate([jnp.sum(c, axis=0, keepdims=True) for c in cols], axis=0))

    def other(i, carry):
        here = pl.ds(pl.multiple_of(i * BLOCK, BLOCK), BLOCK)
        row = lax.broadcasted_iota(jnp.int32, (BLOCK, LANES), 0) + i * BLOCK
        pick = [
            jnp.where(row == sibling[j:j + 1, :], 1.0, 0.0).astype(BF16) for j in range(rows // LANES)
        ]
        feats = dot16(jnp.concatenate(pick, axis=1), unit_feat[...], nn).astype(BF16)
        energy[here, :] = jnp.exp(dot16(feats, unit_proto[...], nt) * 20.0)
        return carry

    lax.fori_loop(0, rows // BLOCK, other, 0, unroll=UNROLL)


def row_kernel(squared, cols_in, table, total, row_out, sums):
    factor = 1.0 / jnp.sum(cols_in[...], axis=0)
    rows, protos = table.shape
    count = rows // LANES

    def step(i, carry):
        here = pl.ds(pl.multiple_of(i * BLOCK, BLOCK), BLOCK)
        part = None
        for j in range(protos // LANES):
            value = table[here, tile(j)]
            value = (value * value if squared else value) * factor[j:j + 1, :]
            part = value if part is None else part + value
        sums[pl.ds(i, 1)] = across(part)[None]
        return carry

    lax.fori_loop(0, rows // BLOCK, step, 0, unroll=UNROLL)
    result = sums[...].reshape(count, LANES)
    extra = row_out.shape[1] > count
    if extra:
        totals = total[...].reshape(count, LANES)
    for i in range(row_out.shape[0]):
        row_out[i, :count] = result
        if extra:
            row_out[i, count:] = totals


def column_kernel(rows_in, like, col_out, *rest):
    scale = rest[-1]
    rows, protos = like.shape
    count, tiles = rows // LANES, protos // LANES
    sums = jnp.sum(rows_in[...], axis=0)
    scale[...] = (1.0 / sums[:count]).reshape(scale.shape)
    if len(rest) > 1:
        rest[0][...] = (10.0 / sums[count:]).reshape(scale.shape)

    def step(i, cols):
        here = pl.ds(pl.multiple_of(i * BLOCK, BLOCK), BLOCK)
        weight = down(scale[pl.ds(i, 1)][0])
        out = []
        for j in range(tiles):
            value = like[here, tile(j)]
            out.append(cols[j] + fold(value * value * weight))
        return tuple(out)

    cols = lax.fori_loop(
        0, rows // BLOCK, step, tuple(jnp.zeros((8, LANES), F32) for _ in range(tiles)), unroll=UNROLL
    )
    copies(col_out, jnp.concatenate([jnp.sum(c, axis=0, keepdims=True) for c in cols], axis=0))


def gradient_kernel(like, energy, cols_in, rows_in, like_scale, unit_proto, row_grad, gradient, code_scale):
    factor = 1.0 / jnp.sum(cols_in[...], axis=0)
    code_scale[...] = (10.0 / jnp.sum(rows_in[...], axis=0)).reshape(code_scale.shape)
    rows, protos = like.shape

    def step(i, carry):
        here = pl.ds(pl.multiple_of(i * BLOCK, BLOCK), BLOCK)
        first = down(like_scale[pl.ds(i, 1)][0])
        second = down(code_scale[pl.ds(i, 1)][0])
        for j in range(protos // LANES):
            value = like[here, tile(j)] * first - energy[here, tile(j)] * factor[j:j + 1, :] * second
            gradient[here, tile(j)] = value.astype(BF16)
        row_grad[here, :] = dot16(gradient[here, :], unit_proto[...], nn)
        return carry

    lax.fori_loop(0, rows // BLOCK, step, 0, unroll=UNROLL)


def factor_kernel(ratio, gradient, unit_feat_t, basis_t, part_t, factor_t):
    for n in range(gradient.shape[1] // BLOCK):
        here = slice(n * BLOCK, (n + 1) * BLOCK)
        part = ratio * dot16(unit_feat_t[...], gradient[:, here], nn)
        part_t[:, here] = part
        factor_t[:, here] = dot32(basis_t[...], part, nn)


def mixed_kernel(part_a, part_b, part_c, part_d, part_t, factor_t, mixed_t):
    total = (part_a[...] + part_b[...]) + (part_c[...] + part_d[...])
    factor_t[...] = total
    mixed_t[...] = dot32(total, part_t[...], nt)


def merge_kernel(grads, mixed_a, mixed_b, mixed_c, mixed_d, out):
    count, total, feat = out.shape
    rank = mixed_a.shape[0]
    mixed = (mixed_a[...] + mixed_b[...]) + (mixed_c[...] + mixed_d[...])
    keep = total - rank
    for i in range(count):
        out[i, :keep] = jnp.sum(grads[:, i * keep:(i + 1) * keep], axis=0)
        out[i, keep:] = mixed


def final_kernel(sums_in, basis_t, factor_t, feature_grad, proto_grad):
    rank = basis_t.shape[0]
    keep = sums_in.shape[1] - rank
    feature_grad[...] = jnp.sum(sums_in[:, :keep], axis=0)
    mixed = jnp.sum(sums_in[:, keep:], axis=0)
    gram = dot32(basis_t[...], mixed, nt)
    left = jnp.concatenate([gram, jnp.zeros((rank, LANES - rank), F32)], axis=1)
    wide = jnp.concatenate([left, mixed], axis=1)
    row = lax.broadcasted_iota(jnp.int32, (rank, 1), 0)
    for j in range(rank):
        pivot = wide[j:j + 1, :] / wide[j:j + 1, j:j + 1]
        wide = jnp.where(row == j, pivot, wide - wide[:, j:j + 1] * pivot)
    proto_grad[...] = dot32(factor_t[...], wide[:, LANES:], tn)


def shape(*dims, dtype=F32):
    return jax.ShapeDtypeStruct(dims, dtype)


def kept(*dims, dtype=F32):
    return pltpu.VMEM(dims, dtype)


def stay(value):
    return pltpu.with_memory_space_constraint(value, pltpu.VMEM)


def call(body, outs, scratch=(), limit=24, flops=0, moved=0, name=None):
    return pl.pallas_call(
        body,
        out_shape=outs,
        scratch_shapes=scratch,
        name=name,
        compiler_params=pltpu.CompilerParams(vmem_limit_bytes=limit * MIB),
        cost_estimate=pl.CostEstimate(flops=flops, bytes_accessed=moved, transcendentals=0),
    )


def exchange(value, axes):
    return lax.all_to_all(value, axes, 0, 0)


def sum_core(value):
    return value + lax.ppermute(value, "c", [(0, 1), (1, 0)])


def shifts(value, axis):
    count = lax.axis_size(axis)
    return (value,) + tuple(
        lax.ppermute(value, axis, [(i, (i + s) % count) for i in range(count)]) for s in range(1, count)
    )


def on_device(features, prototypes, sibling_view, q_seed):
    dp, proto = ("x", "c"), ("y", "z")
    rows, feat = features.shape
    protos = prototypes.shape[0]
    rank = q_seed.shape[1]
    row_tiles, col_tiles, blocks = rows // LANES, protos // LANES, rows // BLOCK
    wide, tall = lax.axis_size(dp), lax.axis_size(proto)
    ratio = (protos * tall) / (rows * wide)
    per_block = (blocks, BLOCK // LANES, LANES)
    row_scratch = (pltpu.VMEM(per_block, F32),)

    unit_feat_t, unit_proto, like, energy, cols, total, basis_t = call(
        scores_kernel,
        (
            shape(feat, rows, dtype=BF16),
            shape(protos, feat, dtype=BF16),
            kept(rows, protos),
            kept(rows, protos),
            shape(wide, col_tiles, LANES),
            shape(*per_block),
            shape(rank, feat),
        ),
        (pltpu.VMEM((rows, feat), BF16),),
        name="scores",
    )(features, prototypes, sibling_view.reshape(row_tiles, LANES), q_seed.T)

    def row_step(squared, cols, table, extra=0):
        return call(
            functools.partial(row_kernel, squared), shape(tall, row_tiles + extra, LANES), row_scratch,
            name="rows",
        )(cols, stay(table), total)

    def column_step(sums, extra=()):
        return call(column_kernel, (shape(wide, col_tiles, LANES),) + extra, row_scratch, name="columns")(
            sums, stay(like)
        )

    cols = exchange(cols, dp)
    row_sums = exchange(row_step(True, cols, like, row_tiles), proto)
    cols, like_scale = column_step(row_sums, (shape(*per_block),))
    cols = exchange(cols, dp)
    row_sums = exchange(row_step(True, cols, like), proto)
    (cols,) = column_step(row_sums)
    cols = exchange(cols, dp)
    row_sums = exchange(row_step(False, cols, energy), proto)

    row_grad, gradient = call(
        gradient_kernel,
        (shape(rows, feat), shape(rows, protos, dtype=BF16)),
        row_scratch,
        name="gradient",
    )(stay(like), stay(energy), cols, row_sums, like_scale, unit_proto)

    grads = exchange(row_grad.reshape(lax.axis_size("y"), -1, feat), "y")
    part_t, factor_t = call(
        functools.partial(factor_kernel, ratio), (shape(feat, protos), shape(rank, protos)), name="factor",
        flops=2 * rows * protos * feat,
    )(gradient, unit_feat_t, basis_t)
    factor_t, mixed_t = call(
        mixed_kernel, (shape(rank, protos), shape(rank, feat)), name="mixed", flops=2 * rows * protos * feat
    )(*shifts(sum_core(factor_t), "x"), part_t)
    mixed_t = sum(shifts(sum_core(mixed_t), "x"))
    sums = call(merge_kernel, shape(lax.axis_size("z"), rows // tall + rank, feat), name="merge")(
        grads, *shifts(mixed_t, "y")
    )
    return call(final_kernel, (shape(rows // tall, feat), shape(protos, feat)), name="final")(
        exchange(sums, "z"), basis_t, factor_t
    )


def solution(mesh):
    wide, tall = mesh.shape["dp"], mesh.shape["proto"]
    fine = Mesh(mesh.devices.reshape(wide // 2, 2, 4, tall // 4), ("x", "c", "y", "z"))
    dp, proto = ("x", "c"), ("y", "z")
    return jax.shard_map(
        on_device,
        mesh=fine,
        in_specs=(P(dp, None), P(proto, None), P(dp), P()),
        out_specs=(P(dp + proto, None), P(proto, None)),
        check_vma=False,
    )
```

time: 234 us -> 182 us (0.78)
  other arithmetic: 39.6 us -> 0.03 us
  Pallas kernels: 0 us -> 27.8 us
  waiting for transfers between devices: 44.9 us -> 19.2 us
  matrix products: 21.6 us -> 0 us
  blocking collectives: 92.3 us -> 110 us
  starting transfers between devices: 20.7 us -> 14.3 us
    all_to_all x5 -> x1, waiting for transfers between devices: 42.4 us -> 0.01 us  [exchange(): return lax.all_to_all(value, axes, 0, 0)]
    pallas_call x0 -> x11, Pallas kernels: none -> 27.8 us  [the longest x1 10.2 us: on_device(): call(scores_kernel, (shape(feat, rows, dtype=BF16), shape(protos, feat, d...]
    reduce_sum x17 -> x0, other arithmetic: 23.8 us -> none  [the longest x2 10.2 us: on_device(): row_part = jnp.sum(energy * column_factor[None, :], axis=1)]
    dot_general x8 -> x0, matrix products: 21.2 us -> none  [the longest x2 10.1 us: scores(): lax.dot_general(block, unit_proto, (((1,), (1,)), ((), ())), preferred_el...]
    all_to_all x6 -> x7, blocking collectives: 92.3 us -> 110 us  [exchange(): return lax.all_to_all(value, axes, 0, 0)]
    all_to_all x5 -> x1, starting transfers between devices: 20.5 us -> 3.79 us  [exchange(): return lax.all_to_all(value, axes, 0, 0)]
    ppermute x0 -> x9, waiting for transfers between devices: none -> 16.6 us  [shifts(): lax.ppermute(value, axis, [(i, (i + s) % count) for i in range(count)])]
    ppermute x0 -> x9, starting transfers between devices: none -> 10.4 us  [shifts(): lax.ppermute(value, axis, [(i, (i + s) % count) for i in range(count)])]
  transfers between devices with their start and end apart: 7 -> 12, of which waited for: 6 -> 10; matrix products, arithmetic and copies ran while one was open for 9% -> 0% of each run, Pallas kernels for 0% -> 3%
where the time goes in v2:
time: 182 us; the launch traced here: 181 us
  blocking collectives  110 us (60%)
  Pallas kernels  27.8 us (15%)
  waiting for transfers between devices  19.2 us (11%)
  starting transfers between devices  14.3 us (8%)
  local copies, waits for them, and re-layouts  9.17 us (5%)
    all_to_all x7, blocking collectives, exchange(): return lax.all_to_all(value, axes, 0, 0)  110 us
    ppermute x9, waiting for transfers between devices, shifts(): lax.ppermute(value, axis, [(i, (i + s) % count) for i in range(count)])  16.6 us
    ppermute x9, starting transfers between devices, shifts(): lax.ppermute(value, axis, [(i, (i + s) % count) for i in range(count)])  10.4 us
    pallas_call x1, Pallas kernels, on_device(): call(scores_kernel, (shape(feat, rows, dtype=BF16), shape(protos, feat, d...  10.2 us
    unnamed x14, local copies, waits for them, and re-layouts  9.17 us
    pallas_call x1, Pallas kernels, on_device(): call(final_kernel, (shape(rows // tall, feat), shape(protos, feat)), name...  4.8 us
    all_to_all x1, starting transfers between devices, exchange(): return lax.all_to_all(value, axes, 0, 0)  3.79 us
  transfers between devices with their start and end apart: 12, of which 10 were waited for; matrix products, arithmetic and copies ran while one was open for 0% of the time, Pallas kernels for 3%

profile of v2, /device:TPU:32, one launch (start us, length us, event | category | flops | bytes accessed | tf_op | source)
XLA Modules:
  0.0 181.1 jit_solution(9441948024244254061)
XLA Ops:
  0.6 0.0 copy-start.3
  0.6 1.2 copy-done.3
  1.9 0.0 copy-start.4
  1.9 1.0 copy-done.4
  2.9 0.0 copy-start.5
  2.9 0.8 copy-done.5
  3.7 0.0 copy-start.6
  3.7 0.7 copy-done.6
  4.4 10.2 %scores.1 = (bf16[256,2048]{1,0:T(8,128)(2,1)S(1)}, bf16[1024,256]{1,0:T(8,128)(2,1)S(1)}, f32[2048,1024]{1,0:T(8,128)S(1)}, f32[2048,1024]{1,0:T(8,128)S(1)}, f...) custom-call(bf16[2048,256]{1,0:T(8,128)(2,1)S(1)} %copy-done.3, ...), custom_call_target="tpu_custom_call" | custom-call | tf_op jit(solution)/shard_map/scores/pallas_call | solution.py:259
  14.5 9.5 %all_to_all.40.cols_in = f32[8,8,128]{2,1,0:T(8,128)S(1)} all-to-all(f32[8,8,128]{2,1,0:T(8,128)S(1)} %get-tuple-element.19), channel_id=1, replica_groups=mesh['x'=4,'c'=2,'y'=4,'z'=8] {'x','c'}, dimensions={0} | all-to-all | bytes 65536 | tf_op jit(solution)/shard_map/all_to_all | solution.py:234
  24.1 1.0 rows.3
  25.1 28.7 %all_to_all.41.rows_in = f32[32,32,128]{2,1,0:T(8,128)S(1)} all-to-all(f32[32,32,128]{2,1,0:T(8,128)S(1)} %rows.3), channel_id=1, replica_groups=mesh['x'=4,'c'=2,'y'=4,'z'=8] {'y','z'}, dimensions={0} | all-to-all | bytes 1048576 | tf_op jit(solution)/shard_map/all_to_all | solution.py:234
  53.8 1.0 columns.2
  54.9 7.8 %all_to_all.42.cols_in = f32[8,8,128]{2,1,0:T(8,128)S(1)} all-to-all(f32[8,8,128]{2,1,0:T(8,128)S(1)} %get-tuple-element.21), channel_id=1, replica_groups=mesh['x'=4,'c'=2,'y'=4,'z'=8] {'x','c'}, dimensions={0} | all-to-all | bytes 65536 | tf_op jit(solution)/shard_map/all_to_all | solution.py:234
  62.7 1.0 rows.4
  63.7 16.9 %all_to_all.43.rows_in = f32[32,16,128]{2,1,0:T(8,128)S(1)} all-to-all(f32[32,16,128]{2,1,0:T(8,128)S(1)} %rows.4), channel_id=1, replica_groups=mesh['x'=4,'c'=2,'y'=4,'z'=8] {'y','z'}, dimensions={0} | all-to-all | bytes 524288 | tf_op jit(solution)/shard_map/all_to_all | solution.py:234
  80.6 1.0 columns.3
  81.6 7.8 %all_to_all.44.cols_in = f32[8,8,128]{2,1,0:T(8,128)S(1)} all-to-all(f32[8,8,128]{2,1,0:T(8,128)S(1)} %columns.3), channel_id=1, replica_groups=mesh['x'=4,'c'=2,'y'=4,'z'=8] {'x','c'}, dimensions={0} | all-to-all | bytes 65536 | tf_op jit(solution)/shard_map/all_to_all | solution.py:234
  89.4 0.7 rows.5
  90.1 16.6 %all_to_all.45.rows_in = f32[32,16,128]{2,1,0:T(8,128)S(1)} all-to-all(f32[32,16,128]{2,1,0:T(8,128)S(1)} %rows.5), channel_id=1, replica_groups=mesh['x'=4,'c'=2,'y'=4,'z'=8] {'y','z'}, dimensions={0} | all-to-all | bytes 524288 | tf_op jit(solution)/shard_map/all_to_all | solution.py:234
  106.7 3.3 %gradient.1 = (f32[2048,256]{1,0:T(8,128)S(1)}, bf16[2048,1024]{1,0:T(8,128)(2,1)S(1)}) custom-call(f32[2048,1024]{1,0:T(8,128)S(1)} %get-tuple-element.17.table.like, f32[2048,1024]{1,0:T(8,128)S(1)} %get-tuple-element.18.table.energy, f32[8,8,128]{2,1,0:T(8,128)S(1)} %all_to_all.44.cols_in, f32[32,16,128]{2,1,0:T(8,128)S(1)} %all_to_all.45.rows_in, ...), custom_call_target="tpu_custom_call" | custom-call | tf_op jit(solution)/shard_map/gradient/pallas_call | solution.py:294
  110.1 0.0 copy-start
  110.1 1.9 %copy-done = bf16[2048,1024]{1,0:T(8,128)(2,1)} copy-done((bf16[2048,1024]{1,0:T(8,128)(2,1)}, bf16[2048,1024]{1,0:T(8,128)(2,1)S(1)}, u32[]{:S(2)}) %copy-start) | copy-done | bytes 4194328
  112.0 0.0 copy-start.2
  112.0 1.3 copy-done.2
  113.3 3.8 %all-to-all-start.6 = ((f32[4,512,256]{2,1,0:T(8,128)}), f32[4,512,256]{2,1,0:T(8,128)S(1)}, u32[]{:S(2)}, u32[]{:S(2)}) async-start(f32[4,512,256]{2,1,0:T(8,128)} %bitcast.3), calls=%async_computation.6 | async-start | bytes 4194304 | tf_op jit(solution)/shard_map/all_to_all | solution.py:234
  117.1 0.0 copy-start.1
  117.1 2.2 %copy-done.1 = bf16[2048,1024]{1,0:T(8,128)(2,1)S(1)} copy-done((bf16[2048,1024]{1,0:T(8,128)(2,1)S(1)}, bf16[2048,1024]{1,0:T(8,128)(2,1)}, u32[]{:S(2)}) %copy-start.1) | copy-done | bytes 4194328
  119.3 3.6 %factor.1 = (f32[256,1024]{1,0:T(8,128)S(1)}, f32[32,1024]{1,0:T(8,128)S(1)}) custom-call(bf16[2048,1024]{1,0:T(8,128)(2,1)S(1)} %copy-done.1, bf16[256,2048]{1,0:T(8,128)(2,1)S(1)} %get-tuple-element.26.unit_feat_t, f32[32,256]{1,0:T(8,128)S(1)} %get-tuple-element.27.basis_t), custom_call_target="tpu_custom_call" | custom-call | flops 1073741824 | tf_op jit(solution)/shard_map/factor/pallas_call | solution.py:302
  122.9 0.0 collective-permute-start
  122.9 1.4 collective-permute-done
  124.3 1.2 collective-permute-start.3
  125.5 1.5 collective-permute-start.2
  127.0 0.0 collective-permute-start.1
  127.0 3.7 %collective-permute-done.3.part_d = f32[32,1024]{1,0:T(8,128)S(1)} collective-permute-done((f32[32,1024]{1,0:T(8,128)S(1)}, f32[32,1024]{1,0:T(8,128)S(1)}, u32[]{:S(2)}, u32[]{:S(2)}) %collective-permute-start.3) | collective-permute-done | bytes 131104 | tf_op jit(solution)/shard_map/ppermute | solution.py:244
  130.7 2.7 %collective-permute-done.2.part_c = f32[32,1024]{1,0:T(8,128)S(1)} collective-permute-done((f32[32,1024]{1,0:T(8,128)S(1)}, f32[32,1024]{1,0:T(8,128)S(1)}, u32[]{:S(2)}, u32[]{:S(2)}) %collective-permute-start.2) | collective-permute-done | bytes 131104 | tf_op jit(solution)/shard_map/ppermute | solution.py:244
  133.4 1.7 collective-permute-done.1.part_b
  135.1 1.0 mixed.1
  136.1 0.1 collective-permute-start.4
  136.2 1.2 collective-permute-done.4
  137.4 0.6 collective-permute-start.7
  138.0 1.5 collective-permute-start.6
  139.5 0.9 collective-permute-start.5
  140.3 1.2 collective-permute-done.7
  141.5 2.0 %collective-permute-done.6 = f32[32,256]{1,0:T(8,128)S(1)} collective-permute-done((f32[32,256]{1,0:T(8,128)S(1)}, f32[32,256]{1,0:T(8,128)S(1)}, u32[]{:S(2)}, u32[]{:S(2)}) %collective-permute-start.6) | collective-permute-done | bytes 32800 | tf_op jit(solution)/shard_map/ppermute | solution.py:244
  143.5 1.1 collective-permute-done.5
  144.6 3.1 %collective-permute-start.10 = (f32[32,256]{1,0:T(8,128)S(1)}, f32[32,256]{1,0:T(8,128)S(1)}, u32[]{:S(2)}, u32[]{:S(2)}) collective-permute-start(f32[32,256]{1,0:T(8,128)S(1)} %add_add_fusion.mixed_a), channel_id=1, source_target_pairs={{0,24},{8,0},{16,8},{24,16},{1,25},{9,1},{17,9},{25,17},{2,26},{10... | collective-permute-start | bytes 98312 | tf_op jit(solution)/shard_map/ppermute | solution.py:244
  147.7 0.9 collective-permute-start.9
  148.5 0.9 collective-permute-start.8
  149.4 0.0 collective-permute-done.10.mixed_d
  149.4 3.7 %collective-permute-done.9.mixed_c = f32[32,256]{1,0:T(8,128)S(1)} collective-permute-done((f32[32,256]{1,0:T(8,128)S(1)}, f32[32,256]{1,0:T(8,128)S(1)}, u32[]{:S(2)}, u32[]{:S(2)}) %collective-permute-start.9) | collective-permute-done | bytes 32800 | tf_op jit(solution)/shard_map/ppermute | solution.py:244
  153.1 0.6 collective-permute-done.8.mixed_b
  153.7 0.0 all-to-all-done.6.grads
  153.7 0.1 merge.1
  153.8 22.5 %all_to_all.46.sums_in = f32[8,96,256]{2,1,0:T(8,128)S(1)} all-to-all(f32[8,96,256]{2,1,0:T(8,128)S(1)} %merge.1), channel_id=1, replica_groups=mesh['x'=4,'c'=2,'y'=4,'z'=8] {'z'}, dimensions={0} | all-to-all | bytes 1572864 | tf_op jit(solution)/shard_map/all_to_all | solution.py:234
  176.3 4.8 %final.1 = (f32[64,256]{1,0:T(8,128)}, f32[1024,256]{1,0:T(8,128)}) custom-call(f32[8,96,256]{2,1,0:T(8,128)S(1)} %all_to_all.46.sums_in, f32[32,256]{1,0:T(8,128)S(1)} %get-tuple-element.27.basis_t, f32[32,1024]{1,0:T(8,128)S(1)} %get-tuple-element.31.factor_t), custom_call_target="tpu_custom_call" | custom-call | tf_op jit(solution)/shard_map/final/pallas_call | solution.py:313
  (3 shorter events, 0.0 us)
Async XLA Ops:
  0.6 1.2 copy-start.3
  1.9 1.0 copy-start.4
  2.9 0.8 copy-start.5
  3.7 0.7 copy-start.6
  110.1 1.9 %copy-start = (bf16[2048,1024]{1,0:T(8,128)(2,1)}, bf16[2048,1024]{1,0:T(8,128)(2,1)S(1)}, u32[]{:S(2)}) copy-start(bf16[2048,1024]{1,0:T(8,128)(2,1)S(1)} %get-tuple-element.25.gradient) | copy-start | bytes 12582916
  112.0 1.3 copy-start.2
  113.3 40.3 %all-to-all-start.6 = ((f32[4,512,256]{2,1,0:T(8,128)}), f32[4,512,256]{2,1,0:T(8,128)S(1)}, u32[]{:S(2)}, u32[]{:S(2)}) async-start(f32[4,512,256]{2,1,0:T(8,128)} %bitcast.3), calls=%async_computation.6 | async-start | bytes 4194304 | tf_op jit(solution)/shard_map/all_to_all | solution.py:234
  117.1 2.2 %copy-start.1 = (bf16[2048,1024]{1,0:T(8,128)(2,1)S(1)}, bf16[2048,1024]{1,0:T(8,128)(2,1)}, u32[]{:S(2)}) copy-start(bf16[2048,1024]{1,0:T(8,128)(2,1)} %copy-done) | copy-start | bytes 12582916
  122.9 1.4 collective-permute-start
  124.3 6.4 %collective-permute-start.3 = (f32[32,1024]{1,0:T(8,128)S(1)}, f32[32,1024]{1,0:T(8,128)S(1)}, u32[]{:S(2)}, u32[]{:S(2)}) collective-permute-start(f32[32,1024]{1,0:T(8,128)S(1)} %add.15.part_a), channel_id=1, source_target_pairs={{0,192},{64,0},{128,64},{192,128},{1,193},{65,1},{129,65},{193,129... | collective-permute-start | bytes 393224 | tf_op jit(solution)/shard_map/ppermute | solution.py:244
  125.5 7.9 %collective-permute-start.2 = (f32[32,1024]{1,0:T(8,128)S(1)}, f32[32,1024]{1,0:T(8,128)S(1)}, u32[]{:S(2)}, u32[]{:S(2)}) collective-permute-start(f32[32,1024]{1,0:T(8,128)S(1)} %add.15.part_a), channel_id=1, source_target_pairs={{0,128},{64,192},{128,0},{192,64},{1,129},{65,193},{129,1},{193,65... | collective-permute-start | bytes 393224 | tf_op jit(solution)/shard_map/ppermute | solution.py:244
  127.0 8.1 %collective-permute-start.1 = (f32[32,1024]{1,0:T(8,128)S(1)}, f32[32,1024]{1,0:T(8,128)S(1)}, u32[]{:S(2)}, u32[]{:S(2)}) collective-permute-start(f32[32,1024]{1,0:T(8,128)S(1)} %add.15.part_a), channel_id=1, source_target_pairs={{0,64},{64,128},{128,192},{192,0},{1,65},{65,129},{129,193},{193,1... | collective-permute-start | bytes 393224 | tf_op jit(solution)/shard_map/ppermute | solution.py:244
  136.1 1.3 collective-permute-start.4
  137.4 4.0 %collective-permute-start.7 = (f32[32,256]{1,0:T(8,128)S(1)}, f32[32,256]{1,0:T(8,128)S(1)}, u32[]{:S(2)}, u32[]{:S(2)}) collective-permute-start(f32[32,256]{1,0:T(8,128)S(1)} %add.16), channel_id=1, source_target_pairs={{0,192},{64,0},{128,64},{192,128},{1,193},{65,1},{129,65},{193,129... | collective-permute-start | bytes 98312 | tf_op jit(solution)/shard_map/ppermute | solution.py:244
  138.0 5.5 %collective-permute-start.6 = (f32[32,256]{1,0:T(8,128)S(1)}, f32[32,256]{1,0:T(8,128)S(1)}, u32[]{:S(2)}, u32[]{:S(2)}) collective-permute-start(f32[32,256]{1,0:T(8,128)S(1)} %add.16), channel_id=1, source_target_pairs={{0,128},{64,192},{128,0},{192,64},{1,129},{65,193},{129,1},{193,65... | collective-permute-start | bytes 98312 | tf_op jit(solution)/shard_map/ppermute | solution.py:244
  139.5 5.1 %collective-permute-start.5 = (f32[32,256]{1,0:T(8,128)S(1)}, f32[32,256]{1,0:T(8,128)S(1)}, u32[]{:S(2)}, u32[]{:S(2)}) collective-permute-start(f32[32,256]{1,0:T(8,128)S(1)} %add.16), channel_id=1, source_target_pairs={{0,64},{64,128},{128,192},{192,0},{1,65},{65,129},{129,193},{193,1... | collective-permute-start | bytes 98312 | tf_op jit(solution)/shard_map/ppermute | solution.py:244
  144.6 4.8 %collective-permute-start.10 = (f32[32,256]{1,0:T(8,128)S(1)}, f32[32,256]{1,0:T(8,128)S(1)}, u32[]{:S(2)}, u32[]{:S(2)}) collective-permute-start(f32[32,256]{1,0:T(8,128)S(1)} %add_add_fusion.mixed_a), channel_id=1, source_target_pairs={{0,24},{8,0},{16,8},{24,16},{1,25},{9,1},{17,9},{25,17},{2,26},{10... | collective-permute-start | bytes 98312 | tf_op jit(solution)/shard_map/ppermute | solution.py:244
  147.7 5.4 %collective-permute-start.9 = (f32[32,256]{1,0:T(8,128)S(1)}, f32[32,256]{1,0:T(8,128)S(1)}, u32[]{:S(2)}, u32[]{:S(2)}) collective-permute-start(f32[32,256]{1,0:T(8,128)S(1)} %add_add_fusion.mixed_a), channel_id=1, source_target_pairs={{0,16},{8,24},{16,0},{24,8},{1,17},{9,25},{17,1},{25,9},{2,18},{10... | collective-permute-start | bytes 98312 | tf_op jit(solution)/shard_map/ppermute | solution.py:244
  148.5 5.1 %collective-permute-start.8 = (f32[32,256]{1,0:T(8,128)S(1)}, f32[32,256]{1,0:T(8,128)S(1)}, u32[]{:S(2)}, u32[]{:S(2)}) collective-permute-start(f32[32,256]{1,0:T(8,128)S(1)} %add_add_fusion.mixed_a), channel_id=1, source_target_pairs={{0,8},{8,16},{16,24},{24,0},{1,9},{9,17},{17,25},{25,1},{2,10},{10... | collective-permute-start | bytes 98312 | tf_op jit(solution)/shard_map/ppermute | solution.py:244

commit v3 on v2

v3 whole, which is shorter than its diff:
```python
import functools
import math

import jax
import jax.numpy as jnp
from jax import lax
from jax.experimental import pallas as pl
from jax.experimental.pallas import tpu as pltpu
from jax.sharding import Mesh, PartitionSpec as P

epsilon = 1e-06
highest = lax.Precision.HIGHEST
F32, BF16 = jnp.float32, jnp.bfloat16
LANES = 128
BLOCK = 256
UNROLL = 4
PIVOTS = 4
MIB = 1 << 20

nt = (((1,), (1,)), ((), ()))
nn = (((1,), (0,)), ((), ()))
tn = (((0,), (0,)), ((), ()))


def dot32(a, b, dims):
    return lax.dot_general(a, b, dims, precision=highest, preferred_element_type=F32)


def dot16(a, b, dims):
    return lax.dot_general(a, b, dims, preferred_element_type=F32)


def unit_rows(block):
    wide = block.astype(F32)
    return (wide * lax.rsqrt(jnp.sum(wide * wide, axis=-1, keepdims=True) + epsilon)).astype(BF16)


def across(partial):
    count = partial.shape[0] // LANES
    return jnp.concatenate(
        [jnp.sum(partial[i * LANES:(i + 1) * LANES].T, axis=0, keepdims=True) for i in range(count)],
        axis=0,
    )


def down(rows):
    return jnp.concatenate(
        [jnp.broadcast_to(rows[i:i + 1], (LANES, LANES)).T for i in range(rows.shape[0])], axis=0
    )


def tile(j):
    return slice(j * LANES, (j + 1) * LANES)


def fold(value):
    return jnp.sum(value.reshape(-1, 8, LANES), axis=0)


def copies(ref, value):
    for i in range(ref.shape[0]):
        ref[i] = value


def scores_kernel(feat_hbm, proto_hbm, unit_feat, unit_proto, like, col_out, total, feat, proto, ready):
    rows, protos = feat.shape[0], proto.shape[0]
    tiles = protos // LANES
    proto_copy = pltpu.make_async_copy(proto_hbm, proto, ready.at[0])
    feat_copy = pltpu.make_async_copy(feat_hbm, feat, ready.at[1])
    proto_copy.start()
    feat_copy.start()
    proto_copy.wait()
    unit_proto[...] = unit_rows(proto[...])
    feat_copy.wait()

    def step(i, cols):
        here = pl.ds(pl.multiple_of(i * BLOCK, BLOCK), BLOCK)
        unit = unit_rows(feat[here, :])
        unit_feat[here, :] = unit
        value = jnp.exp(dot16(unit, unit_proto[...], nt) * 10.0)
        like[here, :] = value
        part = value[:, tile(0)]
        for j in range(1, tiles):
            part = part + value[:, tile(j)]
        total[pl.ds(i, 1)] = across(part)[None]
        square = value * value
        return tuple(cols[j] + fold(square[:, tile(j)]) for j in range(tiles))

    cols = lax.fori_loop(
        0, rows // BLOCK, step, tuple(jnp.zeros((8, LANES), F32) for _ in range(tiles)), unroll=UNROLL
    )
    col_out[...] = jnp.concatenate([jnp.sum(c, axis=0, keepdims=True) for c in cols], axis=0)


def sibling_kernel(first, unit_feat, unit_proto, sibling, after, energy, unit_feat_t):
    rows = unit_feat.shape[0]

    def step(i, carry):
        here = pl.ds(pl.multiple_of(i * BLOCK, BLOCK), BLOCK)
        there = pl.ds(pl.multiple_of(first + i * BLOCK, BLOCK), BLOCK)
        row = lax.broadcasted_iota(jnp.int32, (BLOCK, LANES), 0) + (first + i * BLOCK)
        pick = [
            jnp.where(row == sibling[j:j + 1, :], 1.0, 0.0).astype(BF16) for j in range(rows // LANES)
        ]
        feats = dot16(jnp.concatenate(pick, axis=1), unit_feat[...], nn).astype(BF16)
        energy[here, :] = jnp.exp(dot16(feats, unit_proto[...], nt) * 20.0)
        unit_feat_t[:, here] = unit_feat[there, :].T
        return carry

    lax.fori_loop(0, energy.shape[0] // BLOCK, step, 0, unroll=UNROLL)


def row_kernel(cols_in, like, total, later, row_out, sums):
    factor = 1.0 / jnp.sum(cols_in[...], axis=0)
    rows, protos = like.shape
    count = rows // LANES

    def step(i, carry):
        here = pl.ds(pl.multiple_of(i * BLOCK, BLOCK), BLOCK)
        part = None
        for j in range(protos // LANES):
            value = like[here, tile(j)]
            value = value * value * factor[j:j + 1, :]
            part = value if part is None else part + value
        sums[pl.ds(i, 1)] = across(part)[None]
        return carry

    lax.fori_loop(0, rows // BLOCK, step, 0, unroll=UNROLL)
    result = sums[...].reshape(count, LANES)
    extra = row_out.shape[1] > count
    if extra:
        totals = total[...].reshape(count, LANES)
    for i in range(row_out.shape[0]):
        row_out[i, :count] = result
        if extra:
            row_out[i, count:] = totals


def last_row_kernel(cols_in, upper, lower, like, row_out, sums):
    factor = 1.0 / jnp.sum(cols_in[...], axis=0)
    half, protos = upper.shape
    for number, table in enumerate((upper, lower)):
        for i in range(half // BLOCK):
            part = None
            for j in range(protos // LANES):
                value = table[i * BLOCK:(i + 1) * BLOCK, tile(j)] * factor[j:j + 1, :]
                part = value if part is None else part + value
            sums[number * (half // BLOCK) + i] = across(part)
    copies(row_out, sums[...].reshape(row_out.shape[1:]))


def column_kernel(rows_in, like, col_out, *rest):
    scale = rest[-1]
    rows, protos = like.shape
    count, tiles = rows // LANES, protos // LANES
    sums = jnp.sum(rows_in[...], axis=0)
    scale[...] = (1.0 / sums[:count]).reshape(scale.shape)
    if len(rest) > 1:
        rest[0][...] = (10.0 / sums[count:]).reshape(scale.shape)

    def step(i, cols):
        here = pl.ds(pl.multiple_of(i * BLOCK, BLOCK), BLOCK)
        weight = down(scale[pl.ds(i, 1)][0])
        out = []
        for j in range(tiles):
            value = like[here, tile(j)]
            out.append(cols[j] + fold(value * value * weight))
        return tuple(out)

    cols = lax.fori_loop(
        0, rows // BLOCK, step, tuple(jnp.zeros((8, LANES), F32) for _ in range(tiles)), unroll=UNROLL
    )
    result = jnp.concatenate([jnp.sum(c, axis=0, keepdims=True) for c in cols], axis=0)
    if len(col_out.shape) == 3:
        copies(col_out, result)
    else:
        col_out[...] = result


def gradient_kernel(ratio, like, upper, lower, cols_in, rows_in, like_scale, feat_t_a, feat_t_b, unit_proto, seed_t,
                    row_grad, part_t, factor_t, basis_t, code_scale, gradient, grads, sent):
    factor = 1.0 / jnp.sum(cols_in[...], axis=0)
    code_scale[...] = (10.0 / jnp.sum(rows_in[...], axis=0)).reshape(code_scale.shape)
    basis_t[...] = seed_t[...].astype(F32) * 0.125
    rows, protos = like.shape
    blocks = rows // BLOCK

    def copy(i):
        here = slice(i * BLOCK, (i + 1) * BLOCK)
        return pltpu.make_async_copy(grads.at[here], row_grad.at[here], sent.at[i])

    for i in range(blocks):
        here = slice(i * BLOCK, (i + 1) * BLOCK)
        table = upper if i < blocks // 2 else lower
        there = slice((i % (blocks // 2)) * BLOCK, (i % (blocks // 2) + 1) * BLOCK)
        first = down(like_scale[i])
        second = down(code_scale[i])
        for j in range(protos // LANES):
            value = like[here, tile(j)] * first - table[there, tile(j)] * factor[j:j + 1, :] * second
            gradient[here, tile(j)] = value.astype(BF16)
        grads[here, :] = dot16(gradient[here, :], unit_proto[...], nn)
        copy(i).start()
    for n in range(protos // BLOCK):
        here = slice(n * BLOCK, (n + 1) * BLOCK)
        part = dot16(feat_t_a[...], gradient[:rows // 2, here], nn)
        part = ratio * (part + dot16(feat_t_b[...], gradient[rows // 2:, here], nn))
        part_t[:, here] = part
        factor_t[:, here] = dot32(basis_t[...], part, nn)
    for i in range(blocks):
        copy(i).wait()


def mixed_kernel(part_a, part_b, part_c, part_d, part_t, factor_t, mixed_t):
    total = (part_a[...] + part_b[...]) + (part_c[...] + part_d[...])
    factor_t[...] = total
    mixed_t[...] = dot32(total, part_t[...], nt)


def inverse(gram):
    rank = gram.shape[0]
    row = lax.broadcasted_iota(jnp.int32, (rank, 1), 0)
    unit = (row == lax.broadcasted_iota(jnp.int32, (rank, rank), 1)).astype(F32)
    wide = jnp.concatenate([unit, gram, jnp.zeros((rank, LANES - 2 * rank), F32)], axis=1)
    for j in range(0, rank, PIVOTS):
        lines = [wide[j + t:j + t + 1, :] for t in range(PIVOTS)]
        at = [rank + j + t for t in range(PIVOTS)]
        small = [[jnp.broadcast_to(line[:, k:k + 1], (1, LANES)) for k in at] for line in lines]
        columns = [jnp.broadcast_to(wide[:, k:k + 1], (rank, LANES)) for k in at]
        for t in range(PIVOTS):
            scale = 1.0 / small[t][t]
            lines[t] = lines[t] * scale
            small[t] = [v * scale for v in small[t]]
            for u in range(PIVOTS):
                if u != t:
                    by = small[u][t]
                    lines[u] = lines[u] - by * lines[t]
                    small[u] = [v - by * w for v, w in zip(small[u], small[t])]
        reduced = wide
        for t in range(PIVOTS):
            reduced = reduced - columns[t] * lines[t]
        for t in range(PIVOTS):
            reduced = jnp.where(row == j + t, lines[t], reduced)
        wide = reduced
    return wide[:, :rank]


def final_kernel(mixed_a, mixed_b, mixed_c, mixed_d, basis_t, factor_t, proto_grad):
    mixed = (mixed_a[...] + mixed_b[...]) + (mixed_c[...] + mixed_d[...])
    weights = dot32(inverse(dot32(basis_t[...], mixed, nt)), mixed, nn)
    proto_grad[...] = dot32(factor_t[...], weights, tn)


def gather_kernel(grads, after, out):
    out[...] = jnp.sum(grads[...], axis=0)


def shape(*dims, dtype=F32):
    return jax.ShapeDtypeStruct(dims, dtype)


def kept(*dims, dtype=F32):
    return pltpu.VMEM(dims, dtype)


def stay(value):
    return pltpu.with_memory_space_constraint(value, pltpu.VMEM)


def call(body, outs, scratch=(), limit=24, flops=0, name=None, ins=None, out_specs=None):
    specs = {}
    if ins is not None:
        specs["in_specs"] = [pl.BlockSpec(memory_space=m) for m in ins]
    if out_specs is not None:
        specs["out_specs"] = tuple(pl.BlockSpec(memory_space=m) for m in out_specs)
    return pl.pallas_call(
        body,
        out_shape=outs,
        scratch_shapes=scratch,
        name=name,
        compiler_params=pltpu.CompilerParams(vmem_limit_bytes=limit * MIB),
        cost_estimate=pl.CostEstimate(flops=flops, bytes_accessed=0, transcendentals=0),
        **specs,
    )


def exchange(value, axes):
    return lax.all_to_all(value, axes, 0, 0)


def sum_core(value):
    return value + lax.ppermute(value, "c", [(0, 1), (1, 0)])


def swap(value, axis, mask):
    return lax.ppermute(value, axis, [(i, i ^ mask) for i in range(lax.axis_size(axis))])


def fours(value, axis):
    return (value,) + tuple(swap(value, axis, m) for m in (1, 3, 2))


def on_device(features, prototypes, sibling_view, q_seed):
    proto = ("y", "z")
    rows, feat = features.shape
    protos = prototypes.shape[0]
    rank = q_seed.shape[1]
    half = rows // 2
    row_tiles, col_tiles, blocks = rows // LANES, protos // LANES, rows // BLOCK
    wide, tall = lax.axis_size(("x", "c")), lax.axis_size(proto)
    deep = lax.axis_size("z")
    ratio = (protos * tall) / (rows * wide)
    per_block = (blocks, BLOCK // LANES, LANES)
    row_scratch = (pltpu.VMEM(per_block, F32),)
    V, H, A = pltpu.VMEM, pltpu.HBM, pl.ANY

    unit_feat, unit_proto, like, cols, total = call(
        scores_kernel,
        (
            shape(rows, feat, dtype=BF16),
            shape(protos, feat, dtype=BF16),
            kept(rows, protos),
            shape(col_tiles, LANES),
            shape(*per_block),
        ),
        (V((rows, feat), BF16), V((protos, feat), BF16), pltpu.SemaphoreType.DMA((2,))),
        name="scores", ins=(H, H),
    )(
        pltpu.with_memory_space_constraint(features, H),
        pltpu.with_memory_space_constraint(prototypes, H),
    )
    sibling = sibling_view.reshape(row_tiles, LANES)

    def sibling_half(first, after):
        return call(
            functools.partial(sibling_kernel, first),
            (kept(half, protos), shape(feat, half, dtype=BF16)),
            name="sibling", ins=(V, V, V, A), flops=4 * half * rows * feat,
        )(unit_feat, unit_proto, sibling, after)

    def row_step(cols, later, extra=0):
        return call(
            row_kernel, shape(tall, row_tiles + extra, LANES), row_scratch, name="rows", ins=(V, V, V, A)
        )(cols, stay(like), total, stay(later))

    def column_step(sums, out, *extra):
        return call(column_kernel, (out,) + extra, row_scratch, name="columns")(sums, stay(like))

    cols = sum_core(cols)
    upper, feat_t_a = sibling_half(0, cols)
    cols = jnp.stack(fours(cols, "x"))
    row_sums = exchange(row_step(cols, upper, row_tiles), proto)
    cols, like_scale = column_step(row_sums, shape(col_tiles, LANES), shape(*per_block))
    cols = sum_core(cols)
    lower, feat_t_b = sibling_half(half, cols)
    cols = jnp.stack(fours(cols, "x"))
    row_sums = exchange(row_step(cols, lower), proto)
    (cols,) = column_step(row_sums, shape(wide, col_tiles, LANES))
    cols = exchange(cols, ("x", "c"))
    row_sums = exchange(
        call(last_row_kernel, shape(tall, row_tiles, LANES), row_scratch, name="rows", ins=(V, V, V, A))(
            cols, stay(upper), stay(lower), stay(like)
        ),
        proto,
    )

    row_grad, part_t, factor_t, basis_t = call(
        functools.partial(gradient_kernel, ratio),
        (pltpu.HBM((rows, feat), F32), shape(feat, protos), shape(rank, protos), shape(rank, feat)),
        row_scratch
        + (V((rows, protos), BF16), V((rows, feat), F32), pltpu.SemaphoreType.DMA((blocks,))),
        name="gradient", ins=(V,) * 10, out_specs=(H, V, V, V),
    )(
        stay(like), stay(upper), stay(lower), cols, row_sums, like_scale, feat_t_a, feat_t_b, unit_proto,
        q_seed.T,
    )

    grads = exchange(row_grad.reshape(tall // deep, -1, feat), "y")
    factor_t, mixed_t = call(
        mixed_kernel, (shape(rank, protos), shape(rank, feat)), name="mixed",
    )(*fours(sum_core(factor_t), "x"), part_t)
    mixed_t = sum_core(mixed_t)
    mixed_t = sum(fours(mixed_t, "z"))
    mixed_t = mixed_t + swap(mixed_t, "z", 4)
    grads = call(gather_kernel, shape(deep * rows // tall, feat), name="gather", ins=(V, A))(grads, mixed_t)
    grads = exchange(grads.reshape(deep, rows // tall, feat), "z")
    mixed_t = sum(fours(mixed_t, "x"))
    proto_grad = call(final_kernel, shape(protos, feat), name="final")(
        *fours(mixed_t, "y"), basis_t, factor_t
    )
    return jnp.sum(grads, axis=0), proto_grad


def solution(mesh):
    wide, tall = mesh.shape["dp"], mesh.shape["proto"]
    fine = Mesh(mesh.devices.reshape(wide // 2, 2, 4, tall // 4), ("x", "c", "y", "z"))
    dp, proto = ("x", "c"), ("y", "z")
    return jax.shard_map(
        on_device,
        mesh=fine,
        in_specs=(P(dp, None), P(proto, None), P(dp), P()),
        out_specs=(P(dp + proto, None), P(proto, None)),
        check_vma=False,
    )
```

time: 182 us -> 164 us (0.901)
  blocking collectives: 110 us -> 71.7 us
  starting transfers between devices: 14.3 us -> 35.3 us
  local copies, waits for them, and re-layouts: 9.17 us -> 0.7 us
  waiting for transfers between devices: 19.2 us -> 27.4 us
    all_to_all x7 -> x4, blocking collectives: 110 us -> 71.7 us  [exchange(): return lax.all_to_all(value, axes, 0, 0)]
    ppermute x9 -> x19, starting transfers between devices: 10.4 us -> 26 us  [swap(): lax.ppermute(value, axis, [(i, i ^ mask) for i in range(lax.axis_size(axi...]
    unnamed x14 -> x6, local copies, waits for them, and re-layouts: 9.17 us -> 0.7 us
    ppermute x9 -> x19, waiting for transfers between devices: 16.6 us -> 22.6 us  [swap(): lax.ppermute(value, axis, [(i, i ^ mask) for i in range(lax.axis_size(axi...]
    all_to_all x1 -> x2, starting transfers between devices: 3.79 us -> 8.99 us  [exchange(): return lax.all_to_all(value, axes, 0, 0)]
    ppermute x2 -> x4, waiting for transfers between devices: 2.55 us -> 4.83 us  [sum_core(): return value + lax.ppermute(value, 'c', [(0, 1), (1, 0)])]
    pallas_call x11 -> x12, Pallas kernels: 27.8 us -> 27.3 us  [the longest x2 7.23 us: sibling_half(): call(functools.partial(sibling_kernel, first), (kept(half, protos), shape...]
  transfers between devices with their start and end apart: 12 -> 25, of which waited for: 10 -> 15; matrix products, arithmetic and copies ran while one was open for 0% -> 0% of each run, Pallas kernels for 3% -> 7%
where the time goes in v3:
time: 164 us
  blocking collectives  71.7 us (44%)
  starting transfers between devices  35.3 us (22%)
  waiting for transfers between devices  27.4 us (17%)
  Pallas kernels  27.3 us (17%)
    all_to_all x4, blocking collectives, exchange(): return lax.all_to_all(value, axes, 0, 0)  71.7 us
    ppermute x19, starting transfers between devices, swap(): lax.ppermute(value, axis, [(i, i ^ mask) for i in range(lax.axis_size(axi...  26 us
    ppermute x19, waiting for transfers between devices, swap(): lax.ppermute(value, axis, [(i, i ^ mask) for i in range(lax.axis_size(axi...  22.6 us
    all_to_all x2, starting transfers between devices, exchange(): return lax.all_to_all(value, axes, 0, 0)  8.99 us
    pallas_call x2, Pallas kernels, sibling_half(): call(functools.partial(sibling_kernel, first), (kept(half, protos), shape...  7.23 us
    pallas_call x1, Pallas kernels, on_device(): call(functools.partial(gradient_kernel, ratio), (pltpu.HBM((rows, feat),...  5.94 us
    ppermute x4, waiting for transfers between devices, sum_core(): return value + lax.ppermute(value, 'c', [(0, 1), (1, 0)])  4.83 us
    pallas_call x1, Pallas kernels, on_device(): call(scores_kernel, (shape(rows, feat, dtype=BF16), shape(protos, feat, d...  4 us
  transfers between devices with their start and end apart: 25, of which 15 were waited for; matrix products, arithmetic and copies ran while one was open for 0% of the time, Pallas kernels for 7%

profile of v3, /device:TPU:32, one launch (start us, length us, event | category | flops | bytes accessed | tf_op | source)
XLA Modules:
  0.0 164.0 jit_solution(12277493891723417667)
XLA Ops:
  0.6 4.0 %scores.1 = (bf16[2048,256]{1,0:T(8,128)(2,1)S(1)}, bf16[1024,256]{1,0:T(8,128)(2,1)S(1)}, f32[2048,1024]{1,0:T(8,128)S(1)}, f32[8,128]{1,0:T(8,128)S(1)}, f32[8,2,128]{2,1,0:T(2,128)S(1)}) custom-call(bf16[2048,256]{1,0:T(8,128)(2,1)} %feat_hbm.1, bf16[1024,256]{1,0:T(8,128)(2,1)} %proto_hbm.1), custom_call_target="tpu_custom_call" | custom-call | tf_op jit(solution)/shard_map/scores/pallas_call | solution.py:316
  4.6 0.1 collective-permute-start
  4.7 1.2 collective-permute-done
  5.9 3.0 %collective-permute-start.3 = (f32[8,128]{1,0:T(8,128)S(1)}, f32[8,128]{1,0:T(8,128)S(1)}, u32[]{:S(2)}, u32[]{:S(2)}) collective-permute-start(f32[8,128]{1,0:T(8,128)S(1)} %add.33.after), channel_id=1, source_target_pairs={{0,128},{64,192},{128,0},{192,64},{1,129},{65,193},{129,1},{193,65... | collective-permute-start | bytes 12296 | tf_op jit(solution)/shard_map/ppermute | solution.py:295
  8.9 1.1 collective-permute-start.2
  10.1 0.0 collective-permute-start.1
  10.1 0.7 copy-done.1
  10.8 3.6 %sibling.2 = (f32[1024,1024]{1,0:T(8,128)S(1)}, bf16[256,1024]{1,0:T(8,128)(2,1)S(1)}) custom-call(bf16[2048,256]{1,0:T(8,128)(2,1)S(1)} %get-tuple-element.20.unit_feat, bf16[1024,256]{1,0:T(8,128)(2,1)S(1)} %get-tuple-element.21.unit_proto, s32[16,128]{1,0:T(8,128)S(1)} %bitcast.15, f32[8,128]{1,0:T(8,128)S(1)} %add.33.after), custom_call_target="tpu_custom_call" | custom-call | flops 2147483648 | tf_op jit(solution)/shard_map/sibling/pallas_call | solution.py:334
  14.4 0.0 collective-permute-done.3
  14.4 0.0 collective-permute-done.2
  14.4 1.0 rows.3
  15.4 28.6 %all_to_all.30.rows_in = f32[32,32,128]{2,1,0:T(8,128)S(1)} all-to-all(f32[32,32,128]{2,1,0:T(8,128)S(1)} %rows.3), channel_id=1, replica_groups=mesh['x'=4,'c'=2,'y'=4,'z'=8] {'y','z'}, dimensions={0} | all-to-all | bytes 1048576 | tf_op jit(solution)/shard_map/all_to_all | solution.py:287
  44.0 1.0 columns.2
  45.0 0.1 collective-permute-start.4
  45.1 1.2 collective-permute-done.4
  46.3 3.3 %collective-permute-start.7 = (f32[8,128]{1,0:T(8,128)S(1)}, f32[8,128]{1,0:T(8,128)S(1)}, u32[]{:S(2)}, u32[]{:S(2)}) collective-permute-start(f32[8,128]{1,0:T(8,128)S(1)} %add.34.after), channel_id=1, source_target_pairs={{0,128},{64,192},{128,0},{192,64},{1,129},{65,193},{129,1},{193,65... | collective-permute-start | bytes 12296 | tf_op jit(solution)/shard_map/ppermute | solution.py:295
  49.6 1.1 collective-permute-start.6
  50.7 0.0 collective-permute-start.5
  50.7 3.6 %sibling.3 = (f32[1024,1024]{1,0:T(8,128)S(1)}, bf16[256,1024]{1,0:T(8,128)(2,1)S(1)}) custom-call(bf16[2048,256]{1,0:T(8,128)(2,1)S(1)} %get-tuple-element.20.unit_feat, bf16[1024,256]{1,0:T(8,128)(2,1)S(1)} %get-tuple-element.21.unit_proto, s32[16,128]{1,0:T(8,128)S(1)} %bitcast.16, f32[8,128]{1,0:T(8,128)S(1)} %add.34.after), custom_call_target="tpu_custom_call" | custom-call | flops 2147483648 | tf_op jit(solution)/shard_map/sibling/pallas_call | solution.py:334
  54.4 0.0 collective-permute-done.6
  54.4 0.0 collective-permute-done.5
  54.4 1.0 rows.4
  55.4 16.7 %all_to_all.31.rows_in = f32[32,16,128]{2,1,0:T(8,128)S(1)} all-to-all(f32[32,16,128]{2,1,0:T(8,128)S(1)} %rows.4), channel_id=1, replica_groups=mesh['x'=4,'c'=2,'y'=4,'z'=8] {'y','z'}, dimensions={0} | all-to-all | bytes 524288 | tf_op jit(solution)/shard_map/all_to_all | solution.py:287
  72.1 1.0 columns.3
  73.1 9.8 %all_to_all.32.cols_in = f32[8,8,128]{2,1,0:T(8,128)S(1)} all-to-all(f32[8,8,128]{2,1,0:T(8,128)S(1)} %columns.3), channel_id=1, replica_groups=mesh['x'=4,'c'=2,'y'=4,'z'=8] {'x','c'}, dimensions={0} | all-to-all | bytes 65536 | tf_op jit(solution)/shard_map/all_to_all | solution.py:287
  82.9 0.7 rows.5
  83.6 16.6 %all_to_all.33.rows_in = f32[32,16,128]{2,1,0:T(8,128)S(1)} all-to-all(f32[32,16,128]{2,1,0:T(8,128)S(1)} %rows.5), channel_id=1, replica_groups=mesh['x'=4,'c'=2,'y'=4,'z'=8] {'y','z'}, dimensions={0} | all-to-all | bytes 524288 | tf_op jit(solution)/shard_map/all_to_all | solution.py:287
  100.2 5.9 %gradient.1 = (f32[2048,256]{1,0:T(8,128)}, f32[256,1024]{1,0:T(8,128)S(1)}, f32[32,1024]{1,0:T(8,128)S(1)}, f32[32,256]{1,0:T(8,128)S(1)}) custom-call(f32[2048,1024]{1,0:T(8,128)S(1)} %get-tuple-element.19.like, f32[1024,1024]{1,0:T(8,128)S(1)} %get-tuple-element.23.later.upper, f32[1024,1024]{1,0:T(8,128)S(1)} %get-tuple-element.26.later.lower, ...), custom_call_target="tpu_custom_call" | custom-call | tf_op jit(solution)/shard_map/gradient/pallas_call | solution.py:366
  106.1 3.6 %all-to-all-start.4 = ((f32[4,512,256]{2,1,0:T(8,128)}), f32[4,512,256]{2,1,0:T(8,128)S(1)}, u32[]{:S(2)}, u32[]{:S(2)}) async-start(f32[4,512,256]{2,1,0:T(8,128)} %bitcast.17), calls=%async_computation.4 | async-start | bytes 4194304 | tf_op jit(solution)/shard_map/all_to_all | solution.py:287
  109.8 0.1 collective-permute-start.8
  109.9 1.3 collective-permute-done.8
  111.2 1.2 collective-permute-start.11
  112.4 2.2 %collective-permute-start.10 = (f32[32,1024]{1,0:T(8,128)S(1)}, f32[32,1024]{1,0:T(8,128)S(1)}, u32[]{:S(2)}, u32[]{:S(2)}) collective-permute-start(f32[32,1024]{1,0:T(8,128)S(1)} %add.35.part_a), channel_id=1, source_target_pairs={{0,192},{64,128},{128,64},{192,0},{1,193},{65,129},{129,65},{193,1... | collective-permute-start | bytes 393224 | tf_op jit(solution)/shard_map/ppermute | solution.py:295
  114.5 0.3 collective-permute-start.9
  114.8 4.4 %collective-permute-done.11.part_d = f32[32,1024]{1,0:T(8,128)S(1)} collective-permute-done((f32[32,1024]{1,0:T(8,128)S(1)}, f32[32,1024]{1,0:T(8,128)S(1)}, u32[]{:S(2)}, u32[]{:S(2)}) %collective-permute-start.11) | collective-permute-done | bytes 131104 | tf_op jit(solution)/shard_map/ppermute | solution.py:295
  119.2 2.0 %collective-permute-done.10.part_c = f32[32,1024]{1,0:T(8,128)S(1)} collective-permute-done((f32[32,1024]{1,0:T(8,128)S(1)}, f32[32,1024]{1,0:T(8,128)S(1)}, u32[]{:S(2)}, u32[]{:S(2)}) %collective-permute-start.10) | collective-permute-done | bytes 131104 | tf_op jit(solution)/shard_map/ppermute | solution.py:295
  121.2 1.0 mixed.1
  122.2 0.1 collective-permute-start.12
  122.3 1.2 collective-permute-done.12
  123.5 0.8 collective-permute-start.15
  124.3 1.0 collective-permute-start.14
  125.3 2.5 %collective-permute-start.13 = (f32[32,256]{1,0:T(8,128)S(1)}, f32[32,256]{1,0:T(8,128)S(1)}, u32[]{:S(2)}, u32[]{:S(2)}) collective-permute-start(f32[32,256]{1,0:T(8,128)S(1)} %add.36), channel_id=1, source_target_pairs={{0,1},{1,0},{2,3},{3,2},{4,5},{5,4},{6,7},{7,6},{8,9},{9,8},{10,11... | collective-permute-start | bytes 98312 | tf_op jit(solution)/shard_map/ppermute | solution.py:295
  127.9 0.5 collective-permute-done.15
  128.4 0.6 collective-permute-done.14
  129.0 1.2 collective-permute-done.13
  130.1 1.3 collective-permute-start.16
  131.4 6.6 %collective-permute-done.16 = f32[32,256]{1,0:T(8,128)S(1)} collective-permute-done((f32[32,256]{1,0:T(8,128)S(1)}, f32[32,256]{1,0:T(8,128)S(1)}, u32[]{:S(2)}, u32[]{:S(2)}) %collective-permute-start.16) | collective-permute-done | bytes 32800 | tf_op jit(solution)/shard_map/ppermute | solution.py:295
  138.1 0.0 all-to-all-done.4.grads
  138.1 0.9 gather.1
  138.9 5.4 %all-to-all-start.5 = ((f32[8,64,256]{2,1,0:T(8,128)}), f32[8,64,256]{2,1,0:T(8,128)S(1)}, u32[]{:S(2)}, u32[]{:S(2)}) async-start(f32[8,64,256]{2,1,0:T(8,128)} %bitcast.11), calls=%async_computation.5 | async-start | bytes 1048576 | tf_op jit(solution)/shard_map/all_to_all | solution.py:287
  144.3 1.2 collective-permute-start.19
  145.5 1.7 %collective-permute-start.18 = (f32[32,256]{1,0:T(8,128)S(1)}, f32[32,256]{1,0:T(8,128)S(1)}, u32[]{:S(2)}, u32[]{:S(2)}) collective-permute-start(f32[32,256]{1,0:T(8,128)S(1)} %add.40.after), channel_id=1, source_target_pairs={{0,192},{64,128},{128,64},{192,0},{1,193},{65,129},{129,65},{193,1... | collective-permute-start | bytes 98312 | tf_op jit(solution)/shard_map/ppermute | solution.py:295
  147.2 0.6 collective-permute-start.17
  147.8 1.9 %collective-permute-done.19 = f32[32,256]{1,0:T(8,128)S(1)} collective-permute-done((f32[32,256]{1,0:T(8,128)S(1)}, f32[32,256]{1,0:T(8,128)S(1)}, u32[]{:S(2)}, u32[]{:S(2)}) %collective-permute-start.19) | collective-permute-done | bytes 32800 | tf_op jit(solution)/shard_map/ppermute | solution.py:295
  149.7 0.9 collective-permute-done.18
  150.7 0.5 collective-permute-done.17
  151.2 3.5 %collective-permute-start.22 = (f32[32,256]{1,0:T(8,128)S(1)}, f32[32,256]{1,0:T(8,128)S(1)}, u32[]{:S(2)}, u32[]{:S(2)}) collective-permute-start(f32[32,256]{1,0:T(8,128)S(1)} %add_add_fusion.mixed_a), channel_id=1, source_target_pairs={{0,16},{8,24},{16,0},{24,8},{1,17},{9,25},{17,1},{25,9},{2,18},{10... | collective-permute-start | bytes 98312 | tf_op jit(solution)/shard_map/ppermute | solution.py:295
  154.7 1.2 collective-permute-start.21
  155.8 0.0 collective-permute-start.20
  155.8 0.8 collective-permute-done.22.mixed_d
  156.7 3.1 %collective-permute-done.21.mixed_c = f32[32,256]{1,0:T(8,128)S(1)} collective-permute-done((f32[32,256]{1,0:T(8,128)S(1)}, f32[32,256]{1,0:T(8,128)S(1)}, u32[]{:S(2)}, u32[]{:S(2)}) %collective-permute-start.21) | collective-permute-done | bytes 32800 | tf_op jit(solution)/shard_map/ppermute | solution.py:295
  159.8 3.5 %final.1 = f32[1024,256]{1,0:T(8,128)} custom-call(f32[32,256]{1,0:T(8,128)S(1)} %add_add_fusion.mixed_a, f32[32,256]{1,0:T(8,128)S(1)} %collective-permute-done.20.mixed_b, f32[32,256]{1,0:T(8,128)S(1)} %collective-permute-done.21.mixed_c, f32[32,256]{1,0:T(8,128)S(1)} %collective-permute-done.22.mixed_d, f32[32,256]{1,0:T(8,128)S(1)} %get-tuple-element.34.basis_t, ...), custom_call_target="tpu_custom_call" | custom-call | tf_op jit(solution)/shard_map/final/pallas_call | solution.py:387
  163.3 0.0 all-to-all-done.5
  163.3 0.7 reduce_sum.9
  (18 shorter events, 0.1 us)
Async XLA Ops:
  4.6 1.3 collective-permute-start
  5.9 8.5 %collective-permute-start.3 = (f32[8,128]{1,0:T(8,128)S(1)}, f32[8,128]{1,0:T(8,128)S(1)}, u32[]{:S(2)}, u32[]{:S(2)}) collective-permute-start(f32[8,128]{1,0:T(8,128)S(1)} %add.33.after), channel_id=1, source_target_pairs={{0,128},{64,192},{128,0},{192,64},{1,129},{65,193},{129,1},{193,65... | collective-permute-start | bytes 12296 | tf_op jit(solution)/shard_map/ppermute | solution.py:295
  8.9 5.5 %collective-permute-start.2 = (f32[8,128]{1,0:T(8,128)S(1)}, f32[8,128]{1,0:T(8,128)S(1)}, u32[]{:S(2)}, u32[]{:S(2)}) collective-permute-start(f32[8,128]{1,0:T(8,128)S(1)} %add.33.after), channel_id=1, source_target_pairs={{0,192},{64,128},{128,64},{192,0},{1,193},{65,129},{129,65},{193,1... | collective-permute-start | bytes 12296 | tf_op jit(solution)/shard_map/ppermute | solution.py:295
  10.1 4.3 %collective-permute-start.1 = (f32[8,128]{1,0:T(8,128)S(1)}, f32[8,128]{1,0:T(8,128)S(1)}, u32[]{:S(2)}, u32[]{:S(2)}) collective-permute-start(f32[8,128]{1,0:T(8,128)S(1)} %add.33.after), channel_id=1, source_target_pairs={{0,64},{64,0},{128,192},{192,128},{1,65},{65,1},{129,193},{193,129... | collective-permute-start | bytes 12296 | tf_op jit(solution)/shard_map/ppermute | solution.py:295
  10.1 0.7 copy-start.1
  44.0 6.7 %copy-start.2 = (s32[2048]{0:T(1024)S(1)}, s32[2048]{0:T(1024)}, u32[]{:S(2)}) copy-start(s32[2048]{0:T(1024)} %param.6) | copy-start | bytes 24580
  45.0 1.3 collective-permute-start.4
  46.3 8.1 %collective-permute-start.7 = (f32[8,128]{1,0:T(8,128)S(1)}, f32[8,128]{1,0:T(8,128)S(1)}, u32[]{:S(2)}, u32[]{:S(2)}) collective-permute-start(f32[8,128]{1,0:T(8,128)S(1)} %add.34.after), channel_id=1, source_target_pairs={{0,128},{64,192},{128,0},{192,64},{1,129},{65,193},{129,1},{193,65... | collective-permute-start | bytes 12296 | tf_op jit(solution)/shard_map/ppermute | solution.py:295
  49.6 4.8 %collective-permute-start.6 = (f32[8,128]{1,0:T(8,128)S(1)}, f32[8,128]{1,0:T(8,128)S(1)}, u32[]{:S(2)}, u32[]{:S(2)}) collective-permute-start(f32[8,128]{1,0:T(8,128)S(1)} %add.34.after), channel_id=1, source_target_pairs={{0,192},{64,128},{128,64},{192,0},{1,193},{65,129},{129,65},{193,1... | collective-permute-start | bytes 12296 | tf_op jit(solution)/shard_map/ppermute | solution.py:295
  50.7 3.7 %collective-permute-start.5 = (f32[8,128]{1,0:T(8,128)S(1)}, f32[8,128]{1,0:T(8,128)S(1)}, u32[]{:S(2)}, u32[]{:S(2)}) collective-permute-start(f32[8,128]{1,0:T(8,128)S(1)} %add.34.after), channel_id=1, source_target_pairs={{0,64},{64,0},{128,192},{192,128},{1,65},{65,1},{129,193},{193,129... | collective-permute-start | bytes 12296 | tf_op jit(solution)/shard_map/ppermute | solution.py:295
  82.9 17.3 %copy-start = (s32[256,32]{0,1:T(8,128)S(1)}, s32[256,32]{0,1:T(8,128)}, u32[]{:S(2)}) copy-start(s32[256,32]{0,1:T(8,128)} %param.7) | copy-start | bytes 98308
  106.1 31.9 %all-to-all-start.4 = ((f32[4,512,256]{2,1,0:T(8,128)}), f32[4,512,256]{2,1,0:T(8,128)S(1)}, u32[]{:S(2)}, u32[]{:S(2)}) async-start(f32[4,512,256]{2,1,0:T(8,128)} %bitcast.17), calls=%async_computation.4 | async-start | bytes 4194304 | tf_op jit(solution)/shard_map/all_to_all | solution.py:287
  109.8 1.4 collective-permute-start.8
  111.2 7.9 %collective-permute-start.11 = (f32[32,1024]{1,0:T(8,128)S(1)}, f32[32,1024]{1,0:T(8,128)S(1)}, u32[]{:S(2)}, u32[]{:S(2)}) collective-permute-start(f32[32,1024]{1,0:T(8,128)S(1)} %add.35.part_a), channel_id=1, source_target_pairs={{0,128},{64,192},{128,0},{192,64},{1,129},{65,193},{129,1},{193,65... | collective-permute-start | bytes 393224 | tf_op jit(solution)/shard_map/ppermute | solution.py:295
  112.4 8.8 %collective-permute-start.10 = (f32[32,1024]{1,0:T(8,128)S(1)}, f32[32,1024]{1,0:T(8,128)S(1)}, u32[]{:S(2)}, u32[]{:S(2)}) collective-permute-start(f32[32,1024]{1,0:T(8,128)S(1)} %add.35.part_a), channel_id=1, source_target_pairs={{0,192},{64,128},{128,64},{192,0},{1,193},{65,129},{129,65},{193,1... | collective-permute-start | bytes 393224 | tf_op jit(solution)/shard_map/ppermute | solution.py:295
  114.5 6.6 %collective-permute-start.9 = (f32[32,1024]{1,0:T(8,128)S(1)}, f32[32,1024]{1,0:T(8,128)S(1)}, u32[]{:S(2)}, u32[]{:S(2)}) collective-permute-start(f32[32,1024]{1,0:T(8,128)S(1)} %add.35.part_a), channel_id=1, source_target_pairs={{0,64},{64,0},{128,192},{192,128},{1,65},{65,1},{129,193},{193,129... | collective-permute-start | bytes 393224 | tf_op jit(solution)/shard_map/ppermute | solution.py:295
  122.2 1.3 collective-permute-start.12
  123.5 4.9 %collective-permute-start.15 = (f32[32,256]{1,0:T(8,128)S(1)}, f32[32,256]{1,0:T(8,128)S(1)}, u32[]{:S(2)}, u32[]{:S(2)}) collective-permute-start(f32[32,256]{1,0:T(8,128)S(1)} %add.36), channel_id=1, source_target_pairs={{0,2},{1,3},{2,0},{3,1},{4,6},{5,7},{6,4},{7,5},{8,10},{9,11},{10,... | collective-permute-start | bytes 98312 | tf_op jit(solution)/shard_map/ppermute | solution.py:295
  124.3 4.6 %collective-permute-start.14 = (f32[32,256]{1,0:T(8,128)S(1)}, f32[32,256]{1,0:T(8,128)S(1)}, u32[]{:S(2)}, u32[]{:S(2)}) collective-permute-start(f32[32,256]{1,0:T(8,128)S(1)} %add.36), channel_id=1, source_target_pairs={{0,3},{1,2},{2,1},{3,0},{4,7},{5,6},{6,5},{7,4},{8,11},{9,10},{10,... | collective-permute-start | bytes 98312 | tf_op jit(solution)/shard_map/ppermute | solution.py:295
  125.3 4.8 %collective-permute-start.13 = (f32[32,256]{1,0:T(8,128)S(1)}, f32[32,256]{1,0:T(8,128)S(1)}, u32[]{:S(2)}, u32[]{:S(2)}) collective-permute-start(f32[32,256]{1,0:T(8,128)S(1)} %add.36), channel_id=1, source_target_pairs={{0,1},{1,0},{2,3},{3,2},{4,5},{5,4},{6,7},{7,6},{8,9},{9,8},{10,11... | collective-permute-start | bytes 98312 | tf_op jit(solution)/shard_map/ppermute | solution.py:295
  130.1 7.9 %collective-permute-start.16 = (f32[32,256]{1,0:T(8,128)S(1)}, f32[32,256]{1,0:T(8,128)S(1)}, u32[]{:S(2)}, u32[]{:S(2)}) collective-permute-start(f32[32,256]{1,0:T(8,128)S(1)} %add_add_fusion.1), channel_id=1, source_target_pairs={{0,4},{1,5},{2,6},{3,7},{4,0},{5,1},{6,2},{7,3},{8,12},{9,13},{10,... | collective-permute-start | bytes 98312 | tf_op jit(solution)/shard_map/ppermute | solution.py:295
  138.9 24.4 %all-to-all-start.5 = ((f32[8,64,256]{2,1,0:T(8,128)}), f32[8,64,256]{2,1,0:T(8,128)S(1)}, u32[]{:S(2)}, u32[]{:S(2)}) async-start(f32[8,64,256]{2,1,0:T(8,128)} %bitcast.11), calls=%async_computation.5 | async-start | bytes 1048576 | tf_op jit(solution)/shard_map/all_to_all | solution.py:287
  144.3 5.4 %collective-permute-start.19 = (f32[32,256]{1,0:T(8,128)S(1)}, f32[32,256]{1,0:T(8,128)S(1)}, u32[]{:S(2)}, u32[]{:S(2)}) collective-permute-start(f32[32,256]{1,0:T(8,128)S(1)} %add.40.after), channel_id=1, source_target_pairs={{0,128},{64,192},{128,0},{192,64},{1,129},{65,193},{129,1},{193,65... | collective-permute-start | bytes 98312 | tf_op jit(solution)/shard_map/ppermute | solution.py:295
  145.5 5.1 %collective-permute-start.18 = (f32[32,256]{1,0:T(8,128)S(1)}, f32[32,256]{1,0:T(8,128)S(1)}, u32[]{:S(2)}, u32[]{:S(2)}) collective-permute-start(f32[32,256]{1,0:T(8,128)S(1)} %add.40.after), channel_id=1, source_target_pairs={{0,192},{64,128},{128,64},{192,0},{1,193},{65,129},{129,65},{193,1... | collective-permute-start | bytes 98312 | tf_op jit(solution)/shard_map/ppermute | solution.py:295
  147.2 3.9 %collective-permute-start.17 = (f32[32,256]{1,0:T(8,128)S(1)}, f32[32,256]{1,0:T(8,128)S(1)}, u32[]{:S(2)}, u32[]{:S(2)}) collective-permute-start(f32[32,256]{1,0:T(8,128)S(1)} %add.40.after), channel_id=1, source_target_pairs={{0,64},{64,0},{128,192},{192,128},{1,65},{65,1},{129,193},{193,129... | collective-permute-start | bytes 98312 | tf_op jit(solution)/shard_map/ppermute | solution.py:295
  151.2 5.5 %collective-permute-start.22 = (f32[32,256]{1,0:T(8,128)S(1)}, f32[32,256]{1,0:T(8,128)S(1)}, u32[]{:S(2)}, u32[]{:S(2)}) collective-permute-start(f32[32,256]{1,0:T(8,128)S(1)} %add_add_fusion.mixed_a), channel_id=1, source_target_pairs={{0,16},{8,24},{16,0},{24,8},{1,17},{9,25},{17,1},{25,9},{2,18},{10... | collective-permute-start | bytes 98312 | tf_op jit(solution)/shard_map/ppermute | solution.py:295
  154.7 5.1 %collective-permute-start.21 = (f32[32,256]{1,0:T(8,128)S(1)}, f32[32,256]{1,0:T(8,128)S(1)}, u32[]{:S(2)}, u32[]{:S(2)}) collective-permute-start(f32[32,256]{1,0:T(8,128)S(1)} %add_add_fusion.mixed_a), channel_id=1, source_target_pairs={{0,24},{8,16},{16,8},{24,0},{1,25},{9,17},{17,9},{25,1},{2,26},{10... | collective-permute-start | bytes 98312 | tf_op jit(solution)/shard_map/ppermute | solution.py:295
  155.8 4.0 %collective-permute-start.20 = (f32[32,256]{1,0:T(8,128)S(1)}, f32[32,256]{1,0:T(8,128)S(1)}, u32[]{:S(2)}, u32[]{:S(2)}) collective-permute-start(f32[32,256]{1,0:T(8,128)S(1)} %add_add_fusion.mixed_a), channel_id=1, source_target_pairs={{0,8},{8,0},{16,24},{24,16},{1,9},{9,1},{17,25},{25,17},{2,10},{10... | collective-permute-start | bytes 98312 | tf_op jit(solution)/shard_map/ppermute | solution.py:295

commit v4 on v3

--- a/solution.py
+++ b/solution.py
@@ -62,13 +62,18 @@
         ref[i] = value
 
 
-def scores_kernel(feat_hbm, proto_hbm, unit_feat, unit_proto, like, col_out, total, feat, proto, ready):
+def scores_kernel(feat_hbm, proto_hbm, sibling_hbm, seed_hbm, unit_feat, unit_proto, like, col_out, total,
+                  sibling, seed_t, feat, proto, ready):
     rows, protos = feat.shape[0], proto.shape[0]
     tiles = protos // LANES
     proto_copy = pltpu.make_async_copy(proto_hbm, proto, ready.at[0])
     feat_copy = pltpu.make_async_copy(feat_hbm, feat, ready.at[1])
+    sibling_copy = pltpu.make_async_copy(sibling_hbm, sibling, ready.at[2])
+    seed_copy = pltpu.make_async_copy(seed_hbm, seed_t, ready.at[3])
     proto_copy.start()
     feat_copy.start()
+    sibling_copy.start()
+    seed_copy.start()
     proto_copy.wait()
     unit_proto[...] = unit_rows(proto[...])
     feat_copy.wait()
@@ -90,10 +95,17 @@
         0, rows // BLOCK, step, tuple(jnp.zeros((8, LANES), F32) for _ in range(tiles)), unroll=UNROLL
     )
     col_out[...] = jnp.concatenate([jnp.sum(c, axis=0, keepdims=True) for c in cols], axis=0)
-
-
-def sibling_kernel(first, unit_feat, unit_proto, sibling, after, energy, unit_feat_t):
+    sibling_copy.wait()
+    seed_copy.wait()
+
+
+def sibling_kernel(first, unit_feat, unit_proto, sibling, seed_t, after, energy, unit_feat_t, *basis_t):
     rows = unit_feat.shape[0]
+    for out in basis_t:
+        seed = seed_t[...].astype(F32) * 0.125
+        mine = seed.shape[0] // 2
+        turned = jnp.concatenate([seed[mine:], seed[:mine]], axis=0)
+        out[...] = jnp.where(lax.axis_index("c") == 0, seed, turned)
 
     def step(i, carry):
         here = pl.ds(pl.multiple_of(i * BLOCK, BLOCK), BLOCK)
@@ -110,30 +122,35 @@
     lax.fori_loop(0, energy.shape[0] // BLOCK, step, 0, unroll=UNROLL)
 
 
-def row_kernel(cols_in, like, total, later, row_out, sums):
-    factor = 1.0 / jnp.sum(cols_in[...], axis=0)
+def flat(rows):
+    return jnp.concatenate([rows[i:i + 1] for i in range(rows.shape[0])], axis=1)
+
+
+def row_kernel(cols_in, like, rest, later, row_out):
+    factor = 1.0 / add4(*(cols_in[i] for i in range(4)))
     rows, protos = like.shape
-    count = rows // LANES
-
-    def step(i, carry):
-        here = pl.ds(pl.multiple_of(i * BLOCK, BLOCK), BLOCK)
+    sums = []
+    for i in range(rows // BLOCK):
         part = None
         for j in range(protos // LANES):
-            value = like[here, tile(j)]
+            value = like[i * BLOCK:(i + 1) * BLOCK, tile(j)]
             value = value * value * factor[j:j + 1, :]
             part = value if part is None else part + value
-        sums[pl.ds(i, 1)] = across(part)[None]
-        return carry
-
-    lax.fori_loop(0, rows // BLOCK, step, 0, unroll=UNROLL)
-    result = sums[...].reshape(count, LANES)
-    extra = row_out.shape[1] > count
-    if extra:
-        totals = total[...].reshape(count, LANES)
-    for i in range(row_out.shape[0]):
-        row_out[i, :count] = result
-        if extra:
-            row_out[i, count:] = totals
+        sums.append(flat(across(part)))
+    result = jnp.concatenate(sums, axis=1)
+    tall = row_out.shape[0]
+    piece = rows // tall
+    if rest.shape[0] == 1:
+        tails = [rest[...]] * tall
+    else:
+        totals = rest[...].reshape(rows // LANES, LANES)
+        tails = [
+            totals[q * piece // LANES:q * piece // LANES + 1, q * piece % LANES:q * piece % LANES + piece]
+            for q in range(tall)
+        ]
+        tails = [jnp.concatenate([t, jnp.zeros((1, LANES - piece), F32)], axis=1) for t in tails]
+    for q in range(tall):
+        row_out[q] = jnp.concatenate([result, tails[q]], axis=1)
 
 
 def last_row_kernel(cols_in, upper, lower, like, row_out, sums):
@@ -149,14 +166,23 @@
     copies(row_out, sums[...].reshape(row_out.shape[1:]))
 
 
-def column_kernel(rows_in, like, col_out, *rest):
-    scale = rest[-1]
+def column_kernel(finish, rows_in, like, col_out, extra, scale):
     rows, protos = like.shape
-    count, tiles = rows // LANES, protos // LANES
-    sums = jnp.sum(rows_in[...], axis=0)
-    scale[...] = (1.0 / sums[:count]).reshape(scale.shape)
-    if len(rest) > 1:
-        rest[0][...] = (10.0 / sums[count:]).reshape(scale.shape)
+    tall, tiles = rows_in.shape[0], protos // LANES
+    sums = rows_in[0]
+    for q in range(1, tall):
+        sums = sums + rows_in[q]
+    inverse_sums = 1.0 / sums[:, :rows]
+    for i in range(rows // LANES):
+        scale[i // 2, i % 2:i % 2 + 1] = inverse_sums[:, tile(i)]
+    if finish:
+        piece = rows // tall
+        for i in range(rows // LANES):
+            each = LANES // piece
+            line = [rows_in[each * i + t][:, rows:rows + piece] for t in range(each)]
+            extra[i // 2, i % 2:i % 2 + 1] = 10.0 / jnp.concatenate(line, axis=1)
+    else:
+        extra[...] = sums[:, rows:]
 
     def step(i, cols):
         here = pl.ds(pl.multiple_of(i * BLOCK, BLOCK), BLOCK)
@@ -177,17 +203,13 @@
         col_out[...] = result
 
 
-def gradient_kernel(ratio, like, upper, lower, cols_in, rows_in, like_scale, feat_t_a, feat_t_b, unit_proto, seed_t,
-                    row_grad, part_t, factor_t, basis_t, code_scale, gradient, grads, sent):
+def gradient_kernel(ratio, like, upper, lower, cols_in, rows_in, like_scale, feat_t_a, feat_t_b, basis_t,
+                    gradient, part_t, factor_mine, factor_other, code_scale):
     factor = 1.0 / jnp.sum(cols_in[...], axis=0)
     code_scale[...] = (10.0 / jnp.sum(rows_in[...], axis=0)).reshape(code_scale.shape)
-    basis_t[...] = seed_t[...].astype(F32) * 0.125
+    mine = factor_mine.shape[0]
     rows, protos = like.shape
     blocks = rows // BLOCK
-
-    def copy(i):
-        here = slice(i * BLOCK, (i + 1) * BLOCK)
-        return pltpu.make_async_copy(grads.at[here], row_grad.at[here], sent.at[i])
 
     for i in range(blocks):
         here = slice(i * BLOCK, (i + 1) * BLOCK)
@@ -198,22 +220,36 @@
         for j in range(protos // LANES):
             value = like[here, tile(j)] * first - table[there, tile(j)] * factor[j:j + 1, :] * second
             gradient[here, tile(j)] = value.astype(BF16)
-        grads[here, :] = dot16(gradient[here, :], unit_proto[...], nn)
-        copy(i).start()
     for n in range(protos // BLOCK):
         here = slice(n * BLOCK, (n + 1) * BLOCK)
         part = dot16(feat_t_a[...], gradient[:rows // 2, here], nn)
         part = ratio * (part + dot16(feat_t_b[...], gradient[rows // 2:, here], nn))
         part_t[:, here] = part
-        factor_t[:, here] = dot32(basis_t[...], part, nn)
+        both = dot32(basis_t[...], part, nn)
+        factor_mine[:, here] = both[:mine]
+        factor_other[:, here] = both[mine:]
+
+
+def row_grad_kernel(gradient, unit_proto, after, row_grad, grads, sent):
+    rows = gradient.shape[0]
+    blocks = rows // BLOCK
+
+    def copy(i):
+        here = slice(i * BLOCK, (i + 1) * BLOCK)
+        return pltpu.make_async_copy(grads.at[here], row_grad.at[here], sent.at[i])
+
+    for i in range(blocks):
+        here = slice(i * BLOCK, (i + 1) * BLOCK)
+        grads[here, :] = dot16(gradient[here, :], unit_proto[...], nn)
+        copy(i).start()
     for i in range(blocks):
         copy(i).wait()
 
 
-def mixed_kernel(part_a, part_b, part_c, part_d, part_t, factor_t, mixed_t):
-    total = (part_a[...] + part_b[...]) + (part_c[...] + part_d[...])
+def mixed_kernel(a, b, c, d, part_t, part_other, factor_t, mixed_t):
+    total = (a[...] + b[...]) + (c[...] + d[...])
     factor_t[...] = total
-    mixed_t[...] = dot32(total, part_t[...], nt)
+    mixed_t[...] = dot32(total, part_t[...] + part_other[...], nt)
 
 
 def inverse(gram):
@@ -244,10 +280,11 @@
     return wide[:, :rank]
 
 
-def final_kernel(mixed_a, mixed_b, mixed_c, mixed_d, basis_t, factor_t, proto_grad):
+def final_kernel(mixed_a, mixed_b, mixed_c, mixed_d, basis_t, factor_mine, factor_other, proto_grad):
     mixed = (mixed_a[...] + mixed_b[...]) + (mixed_c[...] + mixed_d[...])
     weights = dot32(inverse(dot32(basis_t[...], mixed, nt)), mixed, nn)
-    proto_grad[...] = dot32(factor_t[...], weights, tn)
+    factor_t = jnp.concatenate([factor_mine[...], factor_other[...]], axis=0)
+    proto_grad[...] = dot32(factor_t, weights, tn)
 
 
 def gather_kernel(grads, after, out):
@@ -291,6 +328,10 @@
     return value + lax.ppermute(value, "c", [(0, 1), (1, 0)])
 
 
+def add4(a, b, c, d):
+    return (a + b) + (c + d)
+
+
 def swap(value, axis, mask):
     return lax.ppermute(value, axis, [(i, i ^ mask) for i in range(lax.axis_size(axis))])
 
@@ -313,7 +354,7 @@
     row_scratch = (pltpu.VMEM(per_block, F32),)
     V, H, A = pltpu.VMEM, pltpu.HBM, pl.ANY
 
-    unit_feat, unit_proto, like, cols, total = call(
+    unit_feat, unit_proto, like, cols, total, sibling, seed_t = call(
         scores_kernel,
         (
             shape(rows, feat, dtype=BF16),
@@ -321,40 +362,45 @@
             kept(rows, protos),
             shape(col_tiles, LANES),
             shape(*per_block),
+            shape(row_tiles, LANES, dtype=jnp.int32),
+            shape(rank, feat, dtype=jnp.int32),
         ),
-        (V((rows, feat), BF16), V((protos, feat), BF16), pltpu.SemaphoreType.DMA((2,))),
-        name="scores", ins=(H, H),
+        (V((rows, feat), BF16), V((protos, feat), BF16), pltpu.SemaphoreType.DMA((4,))),
+        name="scores", ins=(H, H, H, H),
     )(
         pltpu.with_memory_space_constraint(features, H),
         pltpu.with_memory_space_constraint(prototypes, H),
-    )
-    sibling = sibling_view.reshape(row_tiles, LANES)
-
-    def sibling_half(first, after):
+        pltpu.with_memory_space_constraint(sibling_view.reshape(row_tiles, LANES), H),
+        pltpu.with_memory_space_constraint(q_seed.T, H),
+    )
+
+    def sibling_half(first, after, *extra):
         return call(
             functools.partial(sibling_kernel, first),
-            (kept(half, protos), shape(feat, half, dtype=BF16)),
-            name="sibling", ins=(V, V, V, A), flops=4 * half * rows * feat,
-        )(unit_feat, unit_proto, sibling, after)
-
-    def row_step(cols, later, extra=0):
-        return call(
-            row_kernel, shape(tall, row_tiles + extra, LANES), row_scratch, name="rows", ins=(V, V, V, A)
-        )(cols, stay(like), total, stay(later))
-
-    def column_step(sums, out, *extra):
-        return call(column_kernel, (out,) + extra, row_scratch, name="columns")(sums, stay(like))
+            (kept(half, protos), shape(feat, half, dtype=BF16)) + extra,
+            name="sibling", ins=(V, V, V, V, A), flops=4 * half * rows * feat,
+        )(unit_feat, unit_proto, sibling, seed_t, after)
+
+    def row_step(cols, rest, later):
+        return call(row_kernel, shape(tall, 1, rows + LANES), name="rows", ins=(V, V, V, A))(
+            cols, stay(like), rest, stay(later)
+        )
+
+    def column_step(finish, sums, *outs):
+        return call(functools.partial(column_kernel, finish), outs, row_scratch, name="columns")(
+            sums, stay(like)
+        )
 
     cols = sum_core(cols)
-    upper, feat_t_a = sibling_half(0, cols)
+    upper, feat_t_a, basis_t = sibling_half(0, cols, shape(rank, feat))
     cols = jnp.stack(fours(cols, "x"))
-    row_sums = exchange(row_step(cols, upper, row_tiles), proto)
-    cols, like_scale = column_step(row_sums, shape(col_tiles, LANES), shape(*per_block))
+    row_sums = exchange(row_step(cols, total, upper), proto)
+    cols, piece = column_step(False, row_sums, shape(col_tiles, LANES), shape(1, LANES))
     cols = sum_core(cols)
     lower, feat_t_b = sibling_half(half, cols)
     cols = jnp.stack(fours(cols, "x"))
-    row_sums = exchange(row_step(cols, lower), proto)
-    (cols,) = column_step(row_sums, shape(wide, col_tiles, LANES))
+    row_sums = exchange(row_step(cols, piece, lower), proto)
+    cols, like_scale = column_step(True, row_sums, shape(wide, col_tiles, LANES), shape(*per_block))
     cols = exchange(cols, ("x", "c"))
     row_sums = exchange(
         call(last_row_kernel, shape(tall, row_tiles, LANES), row_scratch, name="rows", ins=(V, V, V, A))(
@@ -363,29 +409,38 @@
         proto,
     )
 
-    row_grad, part_t, factor_t, basis_t = call(
+    mine = rank // 2
+    gradient, part_t, factor_mine, factor_other = call(
         functools.partial(gradient_kernel, ratio),
-        (pltpu.HBM((rows, feat), F32), shape(feat, protos), shape(rank, protos), shape(rank, feat)),
-        row_scratch
-        + (V((rows, protos), BF16), V((rows, feat), F32), pltpu.SemaphoreType.DMA((blocks,))),
-        name="gradient", ins=(V,) * 10, out_specs=(H, V, V, V),
-    )(
-        stay(like), stay(upper), stay(lower), cols, row_sums, like_scale, feat_t_a, feat_t_b, unit_proto,
-        q_seed.T,
-    )
-
+        (
+            kept(rows, protos, dtype=BF16),
+            shape(feat, protos),
+            shape(mine, protos),
+            shape(mine, protos),
+        ),
+        row_scratch,
+        name="gradient", ins=(V,) * 9, out_specs=(V,) * 4,
+    )(stay(like), stay(upper), stay(lower), cols, row_sums, like_scale, feat_t_a, feat_t_b, basis_t)
+    factor_mine = factor_mine + swap(factor_other, "c", 1)
+    (row_grad,) = call(
+        row_grad_kernel, (pltpu.HBM((rows, feat), F32),),
+        (V((rows, feat), F32), pltpu.SemaphoreType.DMA((blocks,))),
+        name="row_grad", ins=(V, V, A), out_specs=(H,), flops=2 * rows * protos * feat,
+    )(stay(gradient), unit_proto, factor_mine)
     grads = exchange(row_grad.reshape(tall // deep, -1, feat), "y")
-    factor_t, mixed_t = call(
-        mixed_kernel, (shape(rank, protos), shape(rank, feat)), name="mixed",
-    )(*fours(sum_core(factor_t), "x"), part_t)
-    mixed_t = sum_core(mixed_t)
-    mixed_t = sum(fours(mixed_t, "z"))
+
+    factor_mine, mixed_t = call(
+        mixed_kernel, (shape(mine, protos), shape(mine, feat)), name="mixed",
+    )(*fours(factor_mine, "x"), part_t, swap(part_t, "c", 1))
+    factor_other = swap(factor_mine, "c", 1)
+    mixed_t = add4(*fours(mixed_t, "z"))
     mixed_t = mixed_t + swap(mixed_t, "z", 4)
+    mixed_t = add4(*fours(mixed_t, "x"))
     grads = call(gather_kernel, shape(deep * rows // tall, feat), name="gather", ins=(V, A))(grads, mixed_t)
+    mixed_t = jnp.concatenate([mixed_t, swap(mixed_t, "c", 1)], axis=0)
     grads = exchange(grads.reshape(deep, rows // tall, feat), "z")
-    mixed_t = sum(fours(mixed_t, "x"))
     proto_grad = call(final_kernel, shape(protos, feat), name="final")(
-        *fours(mixed_t, "y"), basis_t, factor_t
+        *fours(mixed_t, "y"), basis_t, factor_mine, factor_other
     )
     return jnp.sum(grads, axis=0), proto_grad
 

time: 164 us -> 156 us (0.951)
  blocking collectives: 71.7 us -> 66.7 us
  waiting for transfers between devices: 27.4 us -> 23.8 us
    all_to_all x4, blocking collectives: 71.7 us -> 66.7 us  [exchange(): return lax.all_to_all(value, axes, 0, 0)]
    ppermute x4 -> x2, waiting for transfers between devices: 4.83 us -> 2.31 us  [sum_core(): return value + lax.ppermute(value, 'c', [(0, 1), (1, 0)])]
    ppermute x19 -> x23, waiting for transfers between devices: 22.6 us -> 21.5 us  [swap(): lax.ppermute(value, axis, [(i, i ^ mask) for i in range(lax.axis_size(axi...]
    pallas_call x6 -> x7, Pallas kernels: 11 us -> 11.9 us  [the longest x1 4.82 us: on_device(): call(functools.partial(gradient_kernel, ratio), (kept(rows, protos, dtype...]
    ppermute x19 -> x23, starting transfers between devices: 26 us -> 26.4 us  [swap(): lax.ppermute(value, axis, [(i, i ^ mask) for i in range(lax.axis_size(axi...]
  transfers between devices with their start and end apart: 25 -> 27, of which waited for: 15 -> 15; matrix products, arithmetic and copies ran while one was open for 0% -> 0% of each run, Pallas kernels for 7% -> 8%
where the time goes in v4:
time: 156 us
  blocking collectives  66.7 us (43%)
  starting transfers between devices  35.5 us (23%)
  Pallas kernels  28.2 us (18%)
  waiting for transfers between devices  23.8 us (15%)
    all_to_all x4, blocking collectives, exchange(): return lax.all_to_all(value, axes, 0, 0)  66.7 us
    ppermute x23, starting transfers between devices, swap(): lax.ppermute(value, axis, [(i, i ^ mask) for i in range(lax.axis_size(axi...  26.4 us
    ppermute x23, waiting for transfers between devices, swap(): lax.ppermute(value, axis, [(i, i ^ mask) for i in range(lax.axis_size(axi...  21.5 us
    all_to_all x2, starting transfers between devices, exchange(): return lax.all_to_all(value, axes, 0, 0)  8.86 us
    pallas_call x2, Pallas kernels, sibling_half(): call(functools.partial(sibling_kernel, first), (kept(half, protos), shape...  7.23 us
    pallas_call x1, Pallas kernels, on_device(): call(functools.partial(gradient_kernel, ratio), (kept(rows, protos, dtype...  4.82 us
    pallas_call x1, Pallas kernels, on_device(): call(scores_kernel, (shape(rows, feat, dtype=BF16), shape(protos, feat, d...  4.02 us
    pallas_call x1, Pallas kernels, on_device(): call(final_kernel, shape(protos, feat), name='final')  3.55 us
  transfers between devices with their start and end apart: 27, of which 15 were waited for; matrix products, arithmetic and copies ran while one was open for 0% of the time, Pallas kernels for 8%

profile of v4, /device:TPU:32, one launch (start us, length us, event | category | flops | bytes accessed | tf_op | source)
XLA Modules:
  0.0 155.7 jit_solution(6942995270454503820)
XLA Ops:
  0.6 4.0 %scores.1 = (bf16[2048,256]{1,0:T(8,128)(2,1)S(1)}, bf16[1024,256]{1,0:T(8,128)(2,1)S(1)}, f32[2048,1024]{1,0:T(8,128)S(1)}, f32[8,128]{1,0:T(8,128)S(1)}, f32[8...) custom-call(bf16[2048,256]{1,0:T(8,128)(2,1)} %feat_hbm.1, bf16[1024,256]{1,0:T(8,128)(2,1)} %proto_hbm.1, ...), custom_call_target="tpu_custom_call" | custom-call | tf_op jit(solution)/shard_map/scores/pallas_call | solution.py:357
  4.7 0.1 collective-permute-start
  4.8 1.2 collective-permute-done
  5.9 3.0 %collective-permute-start.3 = (f32[8,128]{1,0:T(8,128)S(1)}, f32[8,128]{1,0:T(8,128)S(1)}, u32[]{:S(2)}, u32[]{:S(2)}) collective-permute-start(f32[8,128]{1,0:T(8,128)S(1)} %add.30.after), channel_id=1, source_target_pairs={{0,128},{64,192},{128,0},{192,64},{1,129},{65,193},{129,1},{193,65... | collective-permute-start | bytes 12296 | tf_op jit(solution)/shard_map/ppermute | solution.py:336
  8.9 1.1 collective-permute-start.2
  10.1 0.0 collective-permute-start.1
  10.1 3.6 %sibling.2 = (f32[1024,1024]{1,0:T(8,128)S(1)}, bf16[256,1024]{1,0:T(8,128)(2,1)S(1)}, f32[32,256]{1,0:T(8,128)S(1)}) custom-call(bf16[2048,256]{1,0:T(8,128)(2,1)S(1)} %get-tuple-element.25.unit_feat, bf16[1024,256]{1,0:T(8,128)(2,1)S(1)} %get-tuple-element.26.unit_proto, s32[16,128]{1,0:T(8,128)S(1)} %get-tuple-element.27.sibling, ...), custom_call_target="tpu_custom_call" | custom-call | flops 2147483648 | tf_op jit(solution)/shard_map/sibling/pallas_call | solution.py:378
  13.7 0.0 collective-permute-done.2
  13.8 0.0 collective-permute-done.1
  13.8 0.9 rows.3
  14.7 23.5 %all_to_all.30.rows_in = f32[32,1,2176]{2,1,0:T(1,128)S(1)} all-to-all(f32[32,1,2176]{2,1,0:T(1,128)S(1)} %rows.3), channel_id=1, replica_groups=mesh['x'=4,'c'=2,'y'=4,'z'=8] {'y','z'}, dimensions={0} | all-to-all | bytes 557056 | tf_op jit(solution)/shard_map/all_to_all | solution.py:324
  38.2 1.0 columns.2
  39.2 0.1 collective-permute-start.4
  39.3 1.2 collective-permute-done.4
  40.5 3.3 %collective-permute-start.7 = (f32[8,128]{1,0:T(8,128)S(1)}, f32[8,128]{1,0:T(8,128)S(1)}, u32[]{:S(2)}, u32[]{:S(2)}) collective-permute-start(f32[8,128]{1,0:T(8,128)S(1)} %add.31.after), channel_id=1, source_target_pairs={{0,128},{64,192},{128,0},{192,64},{1,129},{65,193},{129,1},{193,65... | collective-permute-start | bytes 12296 | tf_op jit(solution)/shard_map/ppermute | solution.py:336
  43.8 1.1 collective-permute-start.6
  44.9 0.0 collective-permute-start.5
  44.9 3.6 %sibling.3 = (f32[1024,1024]{1,0:T(8,128)S(1)}, bf16[256,1024]{1,0:T(8,128)(2,1)S(1)}) custom-call(bf16[2048,256]{1,0:T(8,128)(2,1)S(1)} %get-tuple-element.25.unit_feat, bf16[1024,256]{1,0:T(8,128)(2,1)S(1)} %get-tuple-element.26.unit_proto, s32[16,128]{1,0:T(8,128)S(1)} %get-tuple-element.27.sibling, s32[32,256]{1,0:T(8,128)S(1)} %get-tuple-element.28.seed_t, ...), custom_call_target="tpu_custom_call" | custom-call | flops 2147483648 | tf_op jit(solution)/shard_map/sibling/pallas_call | solution.py:378
  48.5 0.0 collective-permute-done.7
  48.5 0.0 collective-permute-done.6
  48.6 0.9 rows.4
  49.5 16.8 %all_to_all.31.rows_in = f32[32,1,2176]{2,1,0:T(1,128)S(1)} all-to-all(f32[32,1,2176]{2,1,0:T(1,128)S(1)} %rows.4), channel_id=1, replica_groups=mesh['x'=4,'c'=2,'y'=4,'z'=8] {'y','z'}, dimensions={0} | all-to-all | bytes 557056 | tf_op jit(solution)/shard_map/all_to_all | solution.py:324
  66.3 1.1 columns.3
  67.3 9.8 %all_to_all.32.cols_in = f32[8,8,128]{2,1,0:T(8,128)S(1)} all-to-all(f32[8,8,128]{2,1,0:T(8,128)S(1)} %get-tuple-element.35), channel_id=1, replica_groups=mesh['x'=4,'c'=2,'y'=4,'z'=8] {'x','c'}, dimensions={0} | all-to-all | bytes 65536 | tf_op jit(solution)/shard_map/all_to_all | solution.py:324
  77.1 0.7 rows.5
  77.8 16.6 %all_to_all.33.rows_in = f32[32,16,128]{2,1,0:T(8,128)S(1)} all-to-all(f32[32,16,128]{2,1,0:T(8,128)S(1)} %rows.5), channel_id=1, replica_groups=mesh['x'=4,'c'=2,'y'=4,'z'=8] {'y','z'}, dimensions={0} | all-to-all | bytes 524288 | tf_op jit(solution)/shard_map/all_to_all | solution.py:324
  94.4 4.8 %gradient.1 = (bf16[2048,1024]{1,0:T(8,128)(2,1)S(1)}, f32[256,1024]{1,0:T(8,128)S(1)}, f32[16,1024]{1,0:T(8,128)S(1)}, f32[16,1024]{1,0:T(8,128)S(1)}) custom-call(f32[2048,1024]{1,0:T(8,128)S(1)} %get-tuple-element.24.like, f32[1024,1024]{1,0:T(8,128)S(1)} %get-tuple-element.30.later.upper, f32[1024,1024]{1,0:T(8,128)S(1)} %get-tuple-element.33.later.lower, ...), custom_call_target="tpu_custom_call" | custom-call | tf_op jit(solution)/shard_map/gradient/pallas_call | solution.py:413
  99.2 0.0 collective-permute-start.8
  99.2 1.3 collective-permute-done.8
  100.5 2.2 %row_grad.1 = f32[2048,256]{1,0:T(8,128)} custom-call(bf16[2048,1024]{1,0:T(8,128)(2,1)S(1)} %get-tuple-element.40.gradient, bf16[1024,256]{1,0:T(8,128)(2,1)S(1)} %get-tuple-element.26.unit_proto, f32[16,1024]{1,0:T(8,128)S(1)} %add.32.after.a), custom_call_target="tpu_custom_call" | custom-call | flops 1073741824 | tf_op jit(solution)/shard_map/row_grad/pallas_call | solution.py:425
  102.7 3.6 %all-to-all-start.4 = ((f32[4,512,256]{2,1,0:T(8,128)}), f32[4,512,256]{2,1,0:T(8,128)S(1)}, u32[]{:S(2)}, u32[]{:S(2)}) async-start(f32[4,512,256]{2,1,0:T(8,128)} %bitcast.14), calls=%async_computation.4 | async-start | bytes 4194304 | tf_op jit(solution)/shard_map/all_to_all | solution.py:324
  106.3 0.2 collective-permute-start.12
  106.6 1.2 collective-permute-start.11
  107.8 2.2 %collective-permute-start.10 = (f32[16,1024]{1,0:T(8,128)S(1)}, f32[16,1024]{1,0:T(8,128)S(1)}, u32[]{:S(2)}, u32[]{:S(2)}) collective-permute-start(f32[16,1024]{1,0:T(8,128)S(1)} %add.32.after.a), channel_id=1, source_target_pairs={{0,192},{64,128},{128,64},{192,0},{1,193},{65,129},{129,65},{193,1... | collective-permute-start | bytes 196616 | tf_op jit(solution)/shard_map/ppermute | solution.py:336
  110.0 0.3 collective-permute-start.9
  110.2 2.3 %collective-permute-done.11.d = f32[16,1024]{1,0:T(8,128)S(1)} collective-permute-done((f32[16,1024]{1,0:T(8,128)S(1)}, f32[16,1024]{1,0:T(8,128)S(1)}, u32[]{:S(2)}, u32[]{:S(2)}) %collective-permute-start.11) | collective-permute-done | bytes 65568 | tf_op jit(solution)/shard_map/ppermute | solution.py:336
  112.6 1.3 collective-permute-done.10.c
  113.8 0.4 collective-permute-done.9.b
  114.3 0.9 mixed.1
  115.2 0.9 collective-permute-start.15
  116.0 1.0 collective-permute-start.14
  117.1 2.5 %collective-permute-start.13 = (f32[16,256]{1,0:T(8,128)S(1)}, f32[16,256]{1,0:T(8,128)S(1)}, u32[]{:S(2)}, u32[]{:S(2)}) collective-permute-start(f32[16,256]{1,0:T(8,128)S(1)} %get-tuple-element.44), channel_id=1, source_target_pairs={{0,1},{1,0},{2,3},{3,2},{4,5},{5,4},{6,7},{7,6},{8,9},{9,8},{10,11... | collective-permute-start | bytes 49160 | tf_op jit(solution)/shard_map/ppermute | solution.py:336
  119.6 0.5 collective-permute-done.15
  120.1 0.0 collective-permute-done.14
  120.1 1.3 collective-permute-done.13
  121.5 1.3 collective-permute-start.16
  122.8 6.4 %collective-permute-done.16 = f32[16,256]{1,0:T(8,128)S(1)} collective-permute-done((f32[16,256]{1,0:T(8,128)S(1)}, f32[16,256]{1,0:T(8,128)S(1)}, u32[]{:S(2)}, u32[]{:S(2)}) %collective-permute-start.16) | collective-permute-done | bytes 16416 | tf_op jit(solution)/shard_map/ppermute | solution.py:336
  129.2 0.9 collective-permute-start.19
  130.1 2.1 %collective-permute-start.18 = (f32[16,256]{1,0:T(8,128)S(1)}, f32[16,256]{1,0:T(8,128)S(1)}, u32[]{:S(2)}, u32[]{:S(2)}) collective-permute-start(f32[16,256]{1,0:T(8,128)S(1)} %add.36), channel_id=1, source_target_pairs={{0,192},{64,128},{128,64},{192,0},{1,193},{65,129},{129,65},{193,1... | collective-permute-start | bytes 49160 | tf_op jit(solution)/shard_map/ppermute | solution.py:336
  132.2 0.6 collective-permute-start.17
  132.7 1.8 %collective-permute-done.19 = f32[16,256]{1,0:T(8,128)S(1)} collective-permute-done((f32[16,256]{1,0:T(8,128)S(1)}, f32[16,256]{1,0:T(8,128)S(1)}, u32[]{:S(2)}, u32[]{:S(2)}) %collective-permute-start.19) | collective-permute-done | bytes 16416 | tf_op jit(solution)/shard_map/ppermute | solution.py:336
  134.5 0.6 collective-permute-done.18
  135.0 0.9 collective-permute-done.17
  135.9 0.9 gather.1
  136.8 5.2 %all-to-all-start.5 = ((f32[8,64,256]{2,1,0:T(8,128)}), f32[8,64,256]{2,1,0:T(8,128)S(1)}, u32[]{:S(2)}, u32[]{:S(2)}) async-start(f32[8,64,256]{2,1,0:T(8,128)} %bitcast.11), calls=%async_computation.5 | async-start | bytes 1048576 | tf_op jit(solution)/shard_map/all_to_all | solution.py:324
  142.0 0.0 collective-permute-start.20
  142.0 0.5 collective-permute-start.24
  142.6 0.7 collective-permute-done.20
  143.2 3.1 %collective-permute-start.23 = (f32[32,256]{1,0:T(8,128)S(1)}, f32[32,256]{1,0:T(8,128)S(1)}, u32[]{:S(2)}, u32[]{:S(2)}) collective-permute-start(f32[32,256]{1,0:T(8,128)S(1)} %pad_maximum_fusion.mixed_a), channel_id=1, source_target_pairs={{0,16},{8,24},{16,0},{24,8},{1,17},{9,25},{17,1},{25,9},{2,18},{10... | collective-permute-start | bytes 98312 | tf_op jit(solution)/shard_map/ppermute | solution.py:336
  146.3 1.2 collective-permute-start.22
  147.5 1.2 collective-permute-done.23.mixed_d
  148.6 2.8 %collective-permute-done.22.mixed_c = f32[32,256]{1,0:T(8,128)S(1)} collective-permute-done((f32[32,256]{1,0:T(8,128)S(1)}, f32[32,256]{1,0:T(8,128)S(1)}, u32[]{:S(2)}, u32[]{:S(2)}) %collective-permute-start.22) | collective-permute-done | bytes 32800 | tf_op jit(solution)/shard_map/ppermute | solution.py:336
  151.4 3.5 %final.1 = f32[1024,256]{1,0:T(8,128)} custom-call(f32[32,256]{1,0:T(8,128)S(1)} %pad_maximum_fusion.mixed_a, f32[32,256]{1,0:T(8,128)S(1)} %collective-permute-done.21.mixed_b, f32[32,256]{1,0:T(8,128)S(1)} %collective-permute-done.22.mixed_c, f32[32,256]{1,0:T(8,128)S(1)} %collective-permute-done.23.mixed_d, f32[32,256]{1,0:T(8,128)S(1)} %get-tuple-element.39.basis_t, ...), custom_call_target="tpu_custom_call" | custom-call | tf_op jit(solution)/shard_map/final/pallas_call | solution.py:442
  155.0 0.7 reduce_sum.9
  (17 shorter events, 0.1 us)
Async XLA Ops:
  4.7 1.3 collective-permute-start
  5.9 7.8 %collective-permute-start.3 = (f32[8,128]{1,0:T(8,128)S(1)}, f32[8,128]{1,0:T(8,128)S(1)}, u32[]{:S(2)}, u32[]{:S(2)}) collective-permute-start(f32[8,128]{1,0:T(8,128)S(1)} %add.30.after), channel_id=1, source_target_pairs={{0,128},{64,192},{128,0},{192,64},{1,129},{65,193},{129,1},{193,65... | collective-permute-start | bytes 12296 | tf_op jit(solution)/shard_map/ppermute | solution.py:336
  8.9 4.8 %collective-permute-start.2 = (f32[8,128]{1,0:T(8,128)S(1)}, f32[8,128]{1,0:T(8,128)S(1)}, u32[]{:S(2)}, u32[]{:S(2)}) collective-permute-start(f32[8,128]{1,0:T(8,128)S(1)} %add.30.after), channel_id=1, source_target_pairs={{0,192},{64,128},{128,64},{192,0},{1,193},{65,129},{129,65},{193,1... | collective-permute-start | bytes 12296 | tf_op jit(solution)/shard_map/ppermute | solution.py:336
  10.1 3.7 %collective-permute-start.1 = (f32[8,128]{1,0:T(8,128)S(1)}, f32[8,128]{1,0:T(8,128)S(1)}, u32[]{:S(2)}, u32[]{:S(2)}) collective-permute-start(f32[8,128]{1,0:T(8,128)S(1)} %add.30.after), channel_id=1, source_target_pairs={{0,64},{64,0},{128,192},{192,128},{1,65},{65,1},{129,193},{193,129... | collective-permute-start | bytes 12296 | tf_op jit(solution)/shard_map/ppermute | solution.py:336
  39.2 1.3 collective-permute-start.4
  40.5 8.0 %collective-permute-start.7 = (f32[8,128]{1,0:T(8,128)S(1)}, f32[8,128]{1,0:T(8,128)S(1)}, u32[]{:S(2)}, u32[]{:S(2)}) collective-permute-start(f32[8,128]{1,0:T(8,128)S(1)} %add.31.after), channel_id=1, source_target_pairs={{0,128},{64,192},{128,0},{192,64},{1,129},{65,193},{129,1},{193,65... | collective-permute-start | bytes 12296 | tf_op jit(solution)/shard_map/ppermute | solution.py:336
  43.8 4.8 %collective-permute-start.6 = (f32[8,128]{1,0:T(8,128)S(1)}, f32[8,128]{1,0:T(8,128)S(1)}, u32[]{:S(2)}, u32[]{:S(2)}) collective-permute-start(f32[8,128]{1,0:T(8,128)S(1)} %add.31.after), channel_id=1, source_target_pairs={{0,192},{64,128},{128,64},{192,0},{1,193},{65,129},{129,65},{193,1... | collective-permute-start | bytes 12296 | tf_op jit(solution)/shard_map/ppermute | solution.py:336
  44.9 3.7 %collective-permute-start.5 = (f32[8,128]{1,0:T(8,128)S(1)}, f32[8,128]{1,0:T(8,128)S(1)}, u32[]{:S(2)}, u32[]{:S(2)}) collective-permute-start(f32[8,128]{1,0:T(8,128)S(1)} %add.31.after), channel_id=1, source_target_pairs={{0,64},{64,0},{128,192},{192,128},{1,65},{65,1},{129,193},{193,129... | collective-permute-start | bytes 12296 | tf_op jit(solution)/shard_map/ppermute | solution.py:336
  99.2 1.3 collective-permute-start.8
  102.7 33.2 %all-to-all-start.4 = ((f32[4,512,256]{2,1,0:T(8,128)}), f32[4,512,256]{2,1,0:T(8,128)S(1)}, u32[]{:S(2)}, u32[]{:S(2)}) async-start(f32[4,512,256]{2,1,0:T(8,128)} %bitcast.14), calls=%async_computation.4 | async-start | bytes 4194304 | tf_op jit(solution)/shard_map/all_to_all | solution.py:324
  106.3 7.9 %collective-permute-start.12 = (f32[256,1024]{1,0:T(8,128)S(1)}, f32[256,1024]{1,0:T(8,128)S(1)}, u32[]{:S(2)}, u32[]{:S(2)}) collective-permute-start(f32[256,1024]{1,0:T(8,128)S(1)} %get-tuple-element.43.part_t), channel_id=1, source_target_pairs={{0,32},{32,0},{1,33},{33,1},{2,34},{34,2},{3,35},{35,3},{4,36},{36... | collective-permute-start | bytes 3145736 | tf_op jit(solution)/shard_map/ppermute | solution.py:336
  106.6 6.0 %collective-permute-start.11 = (f32[16,1024]{1,0:T(8,128)S(1)}, f32[16,1024]{1,0:T(8,128)S(1)}, u32[]{:S(2)}, u32[]{:S(2)}) collective-permute-start(f32[16,1024]{1,0:T(8,128)S(1)} %add.32.after.a), channel_id=1, source_target_pairs={{0,128},{64,192},{128,0},{192,64},{1,129},{65,193},{129,1},{193,65... | collective-permute-start | bytes 196616 | tf_op jit(solution)/shard_map/ppermute | solution.py:336
  107.8 6.0 %collective-permute-start.10 = (f32[16,1024]{1,0:T(8,128)S(1)}, f32[16,1024]{1,0:T(8,128)S(1)}, u32[]{:S(2)}, u32[]{:S(2)}) collective-permute-start(f32[16,1024]{1,0:T(8,128)S(1)} %add.32.after.a), channel_id=1, source_target_pairs={{0,192},{64,128},{128,64},{192,0},{1,193},{65,129},{129,65},{193,1... | collective-permute-start | bytes 196616 | tf_op jit(solution)/shard_map/ppermute | solution.py:336
  110.0 4.3 %collective-permute-start.9 = (f32[16,1024]{1,0:T(8,128)S(1)}, f32[16,1024]{1,0:T(8,128)S(1)}, u32[]{:S(2)}, u32[]{:S(2)}) collective-permute-start(f32[16,1024]{1,0:T(8,128)S(1)} %add.32.after.a), channel_id=1, source_target_pairs={{0,64},{64,0},{128,192},{192,128},{1,65},{65,1},{129,193},{193,129... | collective-permute-start | bytes 196616 | tf_op jit(solution)/shard_map/ppermute | solution.py:336
  115.2 4.9 %collective-permute-start.15 = (f32[16,256]{1,0:T(8,128)S(1)}, f32[16,256]{1,0:T(8,128)S(1)}, u32[]{:S(2)}, u32[]{:S(2)}) collective-permute-start(f32[16,256]{1,0:T(8,128)S(1)} %get-tuple-element.44), channel_id=1, source_target_pairs={{0,2},{1,3},{2,0},{3,1},{4,6},{5,7},{6,4},{7,5},{8,10},{9,11},{10,... | collective-permute-start | bytes 49160 | tf_op jit(solution)/shard_map/ppermute | solution.py:336
  116.0 4.1 %collective-permute-start.14 = (f32[16,256]{1,0:T(8,128)S(1)}, f32[16,256]{1,0:T(8,128)S(1)}, u32[]{:S(2)}, u32[]{:S(2)}) collective-permute-start(f32[16,256]{1,0:T(8,128)S(1)} %get-tuple-element.44), channel_id=1, source_target_pairs={{0,3},{1,2},{2,1},{3,0},{4,7},{5,6},{6,5},{7,4},{8,11},{9,10},{10,... | collective-permute-start | bytes 49160 | tf_op jit(solution)/shard_map/ppermute | solution.py:336
  117.1 4.4 %collective-permute-start.13 = (f32[16,256]{1,0:T(8,128)S(1)}, f32[16,256]{1,0:T(8,128)S(1)}, u32[]{:S(2)}, u32[]{:S(2)}) collective-permute-start(f32[16,256]{1,0:T(8,128)S(1)} %get-tuple-element.44), channel_id=1, source_target_pairs={{0,1},{1,0},{2,3},{3,2},{4,5},{5,4},{6,7},{7,6},{8,9},{9,8},{10,11... | collective-permute-start | bytes 49160 | tf_op jit(solution)/shard_map/ppermute | solution.py:336
  121.5 7.7 %collective-permute-start.16 = (f32[16,256]{1,0:T(8,128)S(1)}, f32[16,256]{1,0:T(8,128)S(1)}, u32[]{:S(2)}, u32[]{:S(2)}) collective-permute-start(f32[16,256]{1,0:T(8,128)S(1)} %add_add_fusion.1), channel_id=1, source_target_pairs={{0,4},{1,5},{2,6},{3,7},{4,0},{5,1},{6,2},{7,3},{8,12},{9,13},{10,... | collective-permute-start | bytes 49160 | tf_op jit(solution)/shard_map/ppermute | solution.py:336
  129.2 5.2 %collective-permute-start.19 = (f32[16,256]{1,0:T(8,128)S(1)}, f32[16,256]{1,0:T(8,128)S(1)}, u32[]{:S(2)}, u32[]{:S(2)}) collective-permute-start(f32[16,256]{1,0:T(8,128)S(1)} %add.36), channel_id=1, source_target_pairs={{0,128},{64,192},{128,0},{192,64},{1,129},{65,193},{129,1},{193,65... | collective-permute-start | bytes 49160 | tf_op jit(solution)/shard_map/ppermute | solution.py:336
  130.1 4.9 %collective-permute-start.18 = (f32[16,256]{1,0:T(8,128)S(1)}, f32[16,256]{1,0:T(8,128)S(1)}, u32[]{:S(2)}, u32[]{:S(2)}) collective-permute-start(f32[16,256]{1,0:T(8,128)S(1)} %add.36), channel_id=1, source_target_pairs={{0,192},{64,128},{128,64},{192,0},{1,193},{65,129},{129,65},{193,1... | collective-permute-start | bytes 49160 | tf_op jit(solution)/shard_map/ppermute | solution.py:336
  132.2 3.7 %collective-permute-start.17 = (f32[16,256]{1,0:T(8,128)S(1)}, f32[16,256]{1,0:T(8,128)S(1)}, u32[]{:S(2)}, u32[]{:S(2)}) collective-permute-start(f32[16,256]{1,0:T(8,128)S(1)} %add.36), channel_id=1, source_target_pairs={{0,64},{64,0},{128,192},{192,128},{1,65},{65,1},{129,193},{193,129... | collective-permute-start | bytes 49160 | tf_op jit(solution)/shard_map/ppermute | solution.py:336
  136.8 18.2 %all-to-all-start.5 = ((f32[8,64,256]{2,1,0:T(8,128)}), f32[8,64,256]{2,1,0:T(8,128)S(1)}, u32[]{:S(2)}, u32[]{:S(2)}) async-start(f32[8,64,256]{2,1,0:T(8,128)} %bitcast.11), calls=%async_computation.5 | async-start | bytes 1048576 | tf_op jit(solution)/shard_map/all_to_all | solution.py:324
  142.0 1.2 collective-permute-start.20
  142.0 5.4 %collective-permute-start.24 = (f32[16,1024]{1,0:T(8,128)S(1)}, f32[16,1024]{1,0:T(8,128)S(1)}, u32[]{:S(2)}, u32[]{:S(2)}) collective-permute-start(f32[16,1024]{1,0:T(8,128)S(1)} %get-tuple-element.45.factor_mine), channel_id=1, source_target_pairs={{0,32},{32,0},{1,33},{33,1},{2,34},{34,2},{3,35},{35,3},{4,36},{36... | collective-permute-start | bytes 196616 | tf_op jit(solution)/shard_map/ppermute | solution.py:336
  143.2 5.4 %collective-permute-start.23 = (f32[32,256]{1,0:T(8,128)S(1)}, f32[32,256]{1,0:T(8,128)S(1)}, u32[]{:S(2)}, u32[]{:S(2)}) collective-permute-start(f32[32,256]{1,0:T(8,128)S(1)} %pad_maximum_fusion.mixed_a), channel_id=1, source_target_pairs={{0,16},{8,24},{16,0},{24,8},{1,17},{9,25},{17,1},{25,9},{2,18},{10... | collective-permute-start | bytes 98312 | tf_op jit(solution)/shard_map/ppermute | solution.py:336
  146.3 5.1 %collective-permute-start.22 = (f32[32,256]{1,0:T(8,128)S(1)}, f32[32,256]{1,0:T(8,128)S(1)}, u32[]{:S(2)}, u32[]{:S(2)}) collective-permute-start(f32[32,256]{1,0:T(8,128)S(1)} %pad_maximum_fusion.mixed_a), channel_id=1, source_target_pairs={{0,24},{8,16},{16,8},{24,0},{1,25},{9,17},{17,9},{25,1},{2,26},{10... | collective-permute-start | bytes 98312 | tf_op jit(solution)/shard_map/ppermute | solution.py:336
  147.5 4.0 %collective-permute-start.21 = (f32[32,256]{1,0:T(8,128)S(1)}, f32[32,256]{1,0:T(8,128)S(1)}, u32[]{:S(2)}, u32[]{:S(2)}) collective-permute-start(f32[32,256]{1,0:T(8,128)S(1)} %pad_maximum_fusion.mixed_a), channel_id=1, source_target_pairs={{0,8},{8,0},{16,24},{24,16},{1,9},{9,1},{17,25},{25,17},{2,10},{10... | collective-permute-start | bytes 98312 | tf_op jit(solution)/shard_map/ppermute | solution.py:336

commit v5 on v4

--- a/solution.py
+++ b/solution.py
@@ -13,7 +13,6 @@
 F32, BF16 = jnp.float32, jnp.bfloat16
 LANES = 128
 BLOCK = 256
-UNROLL = 4
 PIVOTS = 4
 MIB = 1 << 20
 
@@ -28,6 +27,11 @@
 
 def dot16(a, b, dims):
     return lax.dot_general(a, b, dims, preferred_element_type=F32)
+
+
+def split(value):
+    high = value.astype(BF16)
+    return high, (value - high.astype(F32)).astype(BF16)
 
 
 def unit_rows(block):
@@ -78,8 +82,9 @@
     unit_proto[...] = unit_rows(proto[...])
     feat_copy.wait()
 
-    def step(i, cols):
-        here = pl.ds(pl.multiple_of(i * BLOCK, BLOCK), BLOCK)
+    cols = [jnp.zeros((8, LANES), F32)] * tiles
+    for i in range(rows // BLOCK):
+        here = slice(i * BLOCK, (i + 1) * BLOCK)
         unit = unit_rows(feat[here, :])
         unit_feat[here, :] = unit
         value = jnp.exp(dot16(unit, unit_proto[...], nt) * 10.0)
@@ -87,13 +92,9 @@
         part = value[:, tile(0)]
         for j in range(1, tiles):
             part = part + value[:, tile(j)]
-        total[pl.ds(i, 1)] = across(part)[None]
+        total[i] = across(part)
         square = value * value
-        return tuple(cols[j] + fold(square[:, tile(j)]) for j in range(tiles))
-
-    cols = lax.fori_loop(
-        0, rows // BLOCK, step, tuple(jnp.zeros((8, LANES), F32) for _ in range(tiles)), unroll=UNROLL
-    )
+        cols = [cols[j] + fold(square[:, tile(j)]) for j in range(tiles)]
     col_out[...] = jnp.concatenate([jnp.sum(c, axis=0, keepdims=True) for c in cols], axis=0)
     sibling_copy.wait()
     seed_copy.wait()
@@ -107,9 +108,9 @@
         turned = jnp.concatenate([seed[mine:], seed[:mine]], axis=0)
         out[...] = jnp.where(lax.axis_index("c") == 0, seed, turned)
 
-    def step(i, carry):
-        here = pl.ds(pl.multiple_of(i * BLOCK, BLOCK), BLOCK)
-        there = pl.ds(pl.multiple_of(first + i * BLOCK, BLOCK), BLOCK)
+    for i in range(energy.shape[0] // BLOCK):
+        here = slice(i * BLOCK, (i + 1) * BLOCK)
+        there = slice(first + i * BLOCK, first + (i + 1) * BLOCK)
         row = lax.broadcasted_iota(jnp.int32, (BLOCK, LANES), 0) + (first + i * BLOCK)
         pick = [
             jnp.where(row == sibling[j:j + 1, :], 1.0, 0.0).astype(BF16) for j in range(rows // LANES)
@@ -117,9 +118,6 @@
         feats = dot16(jnp.concatenate(pick, axis=1), unit_feat[...], nn).astype(BF16)
         energy[here, :] = jnp.exp(dot16(feats, unit_proto[...], nt) * 20.0)
         unit_feat_t[:, here] = unit_feat[there, :].T
-        return carry
-
-    lax.fori_loop(0, energy.shape[0] // BLOCK, step, 0, unroll=UNROLL)
 
 
 def flat(rows):
@@ -154,7 +152,7 @@
 
 
 def last_row_kernel(cols_in, upper, lower, like, row_out, sums):
-    factor = 1.0 / jnp.sum(cols_in[...], axis=0)
+    factor = 1.0 / add4(*(cols_in[i] for i in range(4)))
     half, protos = upper.shape
     for number, table in enumerate((upper, lower)):
         for i in range(half // BLOCK):
@@ -184,18 +182,12 @@
     else:
         extra[...] = sums[:, rows:]
 
-    def step(i, cols):
-        here = pl.ds(pl.multiple_of(i * BLOCK, BLOCK), BLOCK)
-        weight = down(scale[pl.ds(i, 1)][0])
-        out = []
+    cols = [jnp.zeros((8, LANES), F32)] * tiles
+    for i in range(rows // BLOCK):
+        weight = down(scale[i])
         for j in range(tiles):
-            value = like[here, tile(j)]
-            out.append(cols[j] + fold(value * value * weight))
-        return tuple(out)
-
-    cols = lax.fori_loop(
-        0, rows // BLOCK, step, tuple(jnp.zeros((8, LANES), F32) for _ in range(tiles)), unroll=UNROLL
-    )
+            value = like[i * BLOCK:(i + 1) * BLOCK, tile(j)]
+            cols[j] = cols[j] + fold(value * value * weight)
     result = jnp.concatenate([jnp.sum(c, axis=0, keepdims=True) for c in cols], axis=0)
     if len(col_out.shape) == 3:
         copies(col_out, result)
@@ -203,13 +195,18 @@
         col_out[...] = result
 
 
-def gradient_kernel(ratio, like, upper, lower, cols_in, rows_in, like_scale, feat_t_a, feat_t_b, basis_t,
-                    gradient, part_t, factor_mine, factor_other, code_scale):
-    factor = 1.0 / jnp.sum(cols_in[...], axis=0)
+def gradient_kernel(ratio, like, upper, lower, cols_in, rows_in, like_scale, feat_t_a, feat_t_b, unit_proto, basis_t,
+                    row_grad, part_t, factor_mine, factor_other, code_scale, gradient, grads, sent):
+    factor = 1.0 / add4(*(cols_in[i] for i in range(4)))
     code_scale[...] = (10.0 / jnp.sum(rows_in[...], axis=0)).reshape(code_scale.shape)
     mine = factor_mine.shape[0]
+    basis = basis_t[...].astype(BF16)
     rows, protos = like.shape
     blocks = rows // BLOCK
+
+    def copy(i):
+        here = slice(i * BLOCK, (i + 1) * BLOCK)
+        return pltpu.make_async_copy(grads.at[here], row_grad.at[here], sent.at[i])
 
     for i in range(blocks):
         here = slice(i * BLOCK, (i + 1) * BLOCK)
@@ -220,28 +217,17 @@
         for j in range(protos // LANES):
             value = like[here, tile(j)] * first - table[there, tile(j)] * factor[j:j + 1, :] * second
             gradient[here, tile(j)] = value.astype(BF16)
+        grads[here, :] = dot16(gradient[here, :], unit_proto[...], nn)
+        copy(i).start()
     for n in range(protos // BLOCK):
         here = slice(n * BLOCK, (n + 1) * BLOCK)
         part = dot16(feat_t_a[...], gradient[:rows // 2, here], nn)
         part = ratio * (part + dot16(feat_t_b[...], gradient[rows // 2:, here], nn))
         part_t[:, here] = part
-        both = dot32(basis_t[...], part, nn)
+        high, low = split(part)
+        both = dot16(basis, high, nn) + dot16(basis, low, nn)
         factor_mine[:, here] = both[:mine]
         factor_other[:, here] = both[mine:]
-
-
-def row_grad_kernel(gradient, unit_proto, after, row_grad, grads, sent):
-    rows = gradient.shape[0]
-    blocks = rows // BLOCK
-
-    def copy(i):
-        here = slice(i * BLOCK, (i + 1) * BLOCK)
-        return pltpu.make_async_copy(grads.at[here], row_grad.at[here], sent.at[i])
-
-    for i in range(blocks):
-        here = slice(i * BLOCK, (i + 1) * BLOCK)
-        grads[here, :] = dot16(gradient[here, :], unit_proto[...], nn)
-        copy(i).start()
     for i in range(blocks):
         copy(i).wait()
 
@@ -249,7 +235,11 @@
 def mixed_kernel(a, b, c, d, part_t, part_other, factor_t, mixed_t):
     total = (a[...] + b[...]) + (c[...] + d[...])
     factor_t[...] = total
-    mixed_t[...] = dot32(total, part_t[...] + part_other[...], nt)
+    rank = total.shape[0]
+    part_high, part_low = split(part_t[...] + part_other[...])
+    high, low = split(total)
+    both = dot16(jnp.concatenate([high, low], axis=0), part_high, nt)
+    mixed_t[...] = both[:rank] + both[rank:] + dot16(high, part_low, nt)
 
 
 def inverse(gram):
@@ -283,8 +273,13 @@
 def final_kernel(mixed_a, mixed_b, mixed_c, mixed_d, basis_t, factor_mine, factor_other, proto_grad):
     mixed = (mixed_a[...] + mixed_b[...]) + (mixed_c[...] + mixed_d[...])
     weights = dot32(inverse(dot32(basis_t[...], mixed, nt)), mixed, nn)
-    factor_t = jnp.concatenate([factor_mine[...], factor_other[...]], axis=0)
-    proto_grad[...] = dot32(factor_t, weights, tn)
+    high, low = split(jnp.concatenate([factor_mine[...], factor_other[...]], axis=0))
+    weights_high, weights_low = split(weights)
+    proto_grad[...] = dot16(
+        jnp.concatenate([high, low, high], axis=0),
+        jnp.concatenate([weights_high, weights_high, weights_low], axis=0),
+        tn,
+    )
 
 
 def gather_kernel(grads, after, out):
@@ -400,8 +395,8 @@
     lower, feat_t_b = sibling_half(half, cols)
     cols = jnp.stack(fours(cols, "x"))
     row_sums = exchange(row_step(cols, piece, lower), proto)
-    cols, like_scale = column_step(True, row_sums, shape(wide, col_tiles, LANES), shape(*per_block))
-    cols = exchange(cols, ("x", "c"))
+    cols, like_scale = column_step(True, row_sums, shape(col_tiles, LANES), shape(*per_block))
+    cols = jnp.stack(fours(sum_core(cols), "x"))
     row_sums = exchange(
         call(last_row_kernel, shape(tall, row_tiles, LANES), row_scratch, name="rows", ins=(V, V, V, A))(
             cols, stay(upper), stay(lower), stay(like)
@@ -410,23 +405,22 @@
     )
 
     mine = rank // 2
-    gradient, part_t, factor_mine, factor_other = call(
+    row_grad, part_t, factor_mine, factor_other = call(
         functools.partial(gradient_kernel, ratio),
         (
-            kept(rows, protos, dtype=BF16),
+            pltpu.HBM((rows, feat), F32),
             shape(feat, protos),
             shape(mine, protos),
             shape(mine, protos),
         ),
-        row_scratch,
-        name="gradient", ins=(V,) * 9, out_specs=(V,) * 4,
-    )(stay(like), stay(upper), stay(lower), cols, row_sums, like_scale, feat_t_a, feat_t_b, basis_t)
-    factor_mine = factor_mine + swap(factor_other, "c", 1)
-    (row_grad,) = call(
-        row_grad_kernel, (pltpu.HBM((rows, feat), F32),),
-        (V((rows, feat), F32), pltpu.SemaphoreType.DMA((blocks,))),
-        name="row_grad", ins=(V, V, A), out_specs=(H,), flops=2 * rows * protos * feat,
-    )(stay(gradient), unit_proto, factor_mine)
+        row_scratch
+        + (V((rows, protos), BF16), V((rows, feat), F32), pltpu.SemaphoreType.DMA((blocks,))),
+        name="gradient", ins=(V,) * 10, out_specs=(H, V, V, V),
+    )(
+        stay(like), stay(upper), stay(lower), cols, row_sums, like_scale, feat_t_a, feat_t_b, unit_proto,
+        basis_t,
+    )
+    factor_mine, part_t = lax.optimization_barrier((factor_mine + swap(factor_other, "c", 1), part_t))
     grads = exchange(row_grad.reshape(tall // deep, -1, feat), "y")
 
     factor_mine, mixed_t = call(
@@ -435,10 +429,13 @@
     factor_other = swap(factor_mine, "c", 1)
     mixed_t = add4(*fours(mixed_t, "z"))
     mixed_t = mixed_t + swap(mixed_t, "z", 4)
+    mixed_other = swap(mixed_t, "c", 1)
+    grads = call(gather_kernel, shape(deep * rows // tall, feat), name="gather", ins=(V, A))(
+        grads, mixed_other
+    )
+    mixed_t = jnp.concatenate([mixed_t, mixed_other], axis=0)
+    grads = exchange(grads.reshape(deep, rows // tall, feat), "z")
     mixed_t = add4(*fours(mixed_t, "x"))
-    grads = call(gather_kernel, shape(deep * rows // tall, feat), name="gather", ins=(V, A))(grads, mixed_t)
-    mixed_t = jnp.concatenate([mixed_t, swap(mixed_t, "c", 1)], axis=0)
-    grads = exchange(grads.reshape(deep, rows // tall, feat), "z")
     proto_grad = call(final_kernel, shape(protos, feat), name="final")(
         *fours(mixed_t, "y"), basis_t, factor_mine, factor_other
     )

time: 156 us -> 153 us (0.981)
  blocking collectives: 66.7 us -> 55.9 us
  waiting for transfers between devices: 23.8 us -> 29 us
  starting transfers between devices: 35.5 us -> 40.4 us
  Pallas kernels: 28.2 us -> 25.5 us
    all_to_all x4 -> x3, blocking collectives: 66.7 us -> 55.9 us  [exchange(): return lax.all_to_all(value, axes, 0, 0)]
    ppermute x23 -> x26, starting transfers between devices: 26.4 us -> 31.3 us  [swap(): lax.ppermute(value, axis, [(i, i ^ mask) for i in range(lax.axis_size(axi...]
    ppermute x23 -> x26, waiting for transfers between devices: 21.5 us -> 25.6 us  [swap(): lax.ppermute(value, axis, [(i, i ^ mask) for i in range(lax.axis_size(axi...]
    pallas_call x2 -> x1, Pallas kernels: 7.01 us -> 5.48 us  [on_device(): call(functools.partial(gradient_kernel, ratio), (pltpu.HBM((rows, feat),...]
    ppermute x2 -> x3, waiting for transfers between devices: 2.31 us -> 3.46 us  [sum_core(): return value + lax.ppermute(value, 'c', [(0, 1), (1, 0)])]
  transfers between devices with their start and end apart: 27 -> 31, of which waited for: 15 -> 16; matrix products, arithmetic and copies ran while one was open for 0% -> 0% of each run, Pallas kernels for 8% -> 7%
where the time goes in v5:
time: 153 us; the launch traced here: 152 us
  blocking collectives  55.9 us (37%)
  starting transfers between devices  40.4 us (26%)
  waiting for transfers between devices  29 us (19%)
  Pallas kernels  25.5 us (17%)
    all_to_all x3, blocking collectives, exchange(): return lax.all_to_all(value, axes, 0, 0)  55.9 us
    ppermute x26, starting transfers between devices, swap(): lax.ppermute(value, axis, [(i, i ^ mask) for i in range(lax.axis_size(axi...  31.3 us
    ppermute x26, waiting for transfers between devices, swap(): lax.ppermute(value, axis, [(i, i ^ mask) for i in range(lax.axis_size(axi...  25.6 us
    all_to_all x2, starting transfers between devices, exchange(): return lax.all_to_all(value, axes, 0, 0)  8.86 us
    pallas_call x2, Pallas kernels, sibling_half(): call(functools.partial(sibling_kernel, first), (kept(half, protos), shape...  7.27 us
    pallas_call x1, Pallas kernels, on_device(): call(functools.partial(gradient_kernel, ratio), (pltpu.HBM((rows, feat),...  5.48 us
    pallas_call x1, Pallas kernels, on_device(): call(scores_kernel, (shape(rows, feat, dtype=BF16), shape(protos, feat, d...  4.08 us
    ppermute x3, waiting for transfers between devices, sum_core(): return value + lax.ppermute(value, 'c', [(0, 1), (1, 0)])  3.46 us
  transfers between devices with their start and end apart: 31, of which 16 were waited for; matrix products, arithmetic and copies ran while one was open for 0% of the time, Pallas kernels for 7%

profile of v5, /device:TPU:32, one launch (start us, length us, event | category | flops | bytes accessed | tf_op | source)
XLA Modules:
  0.0 152.4 jit_solution(13175460238511949096)
XLA Ops:
  0.6 4.1 %scores.1 = (bf16[2048,256]{1,0:T(8,128)(2,1)S(1)}, bf16[1024,256]{1,0:T(8,128)(2,1)S(1)}, f32[2048,1024]{1,0:T(8,128)S(1)}, f32[8,128]{1,0:T(8,128)S(1)}, f32[8...) custom-call(bf16[2048,256]{1,0:T(8,128)(2,1)} %feat_hbm.1, bf16[1024,256]{1,0:T(8,128)(2,1)} %proto_hbm.1, ...), custom_call_target="tpu_custom_call" | custom-call | tf_op jit(solution)/shard_map/scores/pallas_call | solution.py:352
  4.7 0.1 collective-permute-start
  4.8 1.2 collective-permute-done
  6.0 3.0 %collective-permute-start.3 = (f32[8,128]{1,0:T(8,128)S(1)}, f32[8,128]{1,0:T(8,128)S(1)}, u32[]{:S(2)}, u32[]{:S(2)}) collective-permute-start(f32[8,128]{1,0:T(8,128)S(1)} %add.33.after), channel_id=1, source_target_pairs={{0,128},{64,192},{128,0},{192,64},{1,129},{65,193},{129,1},{193,65... | collective-permute-start | bytes 12296 | tf_op jit(solution)/shard_map/ppermute | solution.py:331
  9.0 1.2 collective-permute-start.2
  10.1 3.6 %sibling.2 = (f32[1024,1024]{1,0:T(8,128)S(1)}, bf16[256,1024]{1,0:T(8,128)(2,1)S(1)}, f32[32,256]{1,0:T(8,128)S(1)}) custom-call(bf16[2048,256]{1,0:T(8,128)(2,1)S(1)} %get-tuple-element.27.unit_feat, bf16[1024,256]{1,0:T(8,128)(2,1)S(1)} %get-tuple-element.28.unit_proto, s32[16,128]{1,0:T(8,128)S(1)} %get-tuple-element.29.sibling, ...), custom_call_target="tpu_custom_call" | custom-call | flops 2147483648 | tf_op jit(solution)/shard_map/sibling/pallas_call | solution.py:373
  13.8 0.0 collective-permute-done.2
  13.8 0.0 collective-permute-done.1
  13.8 0.9 rows.3
  14.8 23.5 %all_to_all.25.rows_in = f32[32,1,2176]{2,1,0:T(1,128)S(1)} all-to-all(f32[32,1,2176]{2,1,0:T(1,128)S(1)} %rows.3), channel_id=1, replica_groups=mesh['x'=4,'c'=2,'y'=4,'z'=8] {'y','z'}, dimensions={0} | all-to-all | bytes 557056 | tf_op jit(solution)/shard_map/all_to_all | solution.py:319
  38.3 1.0 columns.2
  39.3 0.1 collective-permute-start.4
  39.4 1.2 collective-permute-done.4
  40.6 3.3 %collective-permute-start.7 = (f32[8,128]{1,0:T(8,128)S(1)}, f32[8,128]{1,0:T(8,128)S(1)}, u32[]{:S(2)}, u32[]{:S(2)}) collective-permute-start(f32[8,128]{1,0:T(8,128)S(1)} %add.34.after), channel_id=1, source_target_pairs={{0,128},{64,192},{128,0},{192,64},{1,129},{65,193},{129,1},{193,65... | collective-permute-start | bytes 12296 | tf_op jit(solution)/shard_map/ppermute | solution.py:331
  43.9 1.1 collective-permute-start.6
  45.0 0.0 collective-permute-start.5
  45.0 3.6 %sibling.3 = (f32[1024,1024]{1,0:T(8,128)S(1)}, bf16[256,1024]{1,0:T(8,128)(2,1)S(1)}) custom-call(bf16[2048,256]{1,0:T(8,128)(2,1)S(1)} %get-tuple-element.27.unit_feat, bf16[1024,256]{1,0:T(8,128)(2,1)S(1)} %get-tuple-element.28.unit_proto, s32[16,128]{1,0:T(8,128)S(1)} %get-tuple-element.29.sibling, s32[32,256]{1,0:T(8,128)S(1)} %get-tuple-element.30.seed_t, ...), custom_call_target="tpu_custom_call" | custom-call | flops 2147483648 | tf_op jit(solution)/shard_map/sibling/pallas_call | solution.py:373
  48.7 0.0 collective-permute-done.7
  48.7 0.0 collective-permute-done.6
  48.7 0.0 collective-permute-done.5
  48.7 0.9 rows.4
  49.6 16.8 %all_to_all.26.rows_in = f32[32,1,2176]{2,1,0:T(1,128)S(1)} all-to-all(f32[32,1,2176]{2,1,0:T(1,128)S(1)} %rows.4), channel_id=1, replica_groups=mesh['x'=4,'c'=2,'y'=4,'z'=8] {'y','z'}, dimensions={0} | all-to-all | bytes 557056 | tf_op jit(solution)/shard_map/all_to_all | solution.py:319
  66.4 1.0 columns.3
  67.4 0.1 collective-permute-start.8
  67.5 1.2 collective-permute-done.8
  68.7 3.3 %collective-permute-start.11 = (f32[8,128]{1,0:T(8,128)S(1)}, f32[8,128]{1,0:T(8,128)S(1)}, u32[]{:S(2)}, u32[]{:S(2)}) collective-permute-start(f32[8,128]{1,0:T(8,128)S(1)} %add.35), channel_id=1, source_target_pairs={{0,128},{64,192},{128,0},{192,64},{1,129},{65,193},{129,1},{193,65... | collective-permute-start | bytes 12296 | tf_op jit(solution)/shard_map/ppermute | solution.py:331
  71.9 1.1 collective-permute-start.10
  73.1 0.7 collective-permute-done.11
  73.8 3.0 %collective-permute-done.10 = f32[8,128]{1,0:T(8,128)S(1)} collective-permute-done((f32[8,128]{1,0:T(8,128)S(1)}, f32[8,128]{1,0:T(8,128)S(1)}, u32[]{:S(2)}, u32[]{:S(2)}) %collective-permute-start.10) | collective-permute-done | bytes 4128 | tf_op jit(solution)/shard_map/ppermute | solution.py:331
  76.8 0.7 rows.5
  77.4 15.6 %all_to_all.27.rows_in = f32[32,16,128]{2,1,0:T(8,128)S(1)} all-to-all(f32[32,16,128]{2,1,0:T(8,128)S(1)} %rows.5), channel_id=1, replica_groups=mesh['x'=4,'c'=2,'y'=4,'z'=8] {'y','z'}, dimensions={0} | all-to-all | bytes 524288 | tf_op jit(solution)/shard_map/all_to_all | solution.py:319
  93.0 5.5 %gradient.1 = (f32[2048,256]{1,0:T(8,128)}, f32[256,1024]{1,0:T(8,128)S(1)}, f32[16,1024]{1,0:T(8,128)S(1)}, f32[16,1024]{1,0:T(8,128)S(1)}) custom-call(f32[2048,1024]{1,0:T(8,128)S(1)} %get-tuple-element.26.like, f32[1024,1024]{1,0:T(8,128)S(1)} %get-tuple-element.32.later.upper, f32[1024,1024]{1,0:T(8,128)S(1)} %get-tuple-element.35.later.lower, ...), custom_call_target="tpu_custom_call" | custom-call | tf_op jit(solution)/shard_map/gradient/pallas_call | solution.py:408
  98.5 3.6 %all-to-all-start.3 = ((f32[4,512,256]{2,1,0:T(8,128)}), f32[4,512,256]{2,1,0:T(8,128)S(1)}, u32[]{:S(2)}, u32[]{:S(2)}) async-start(f32[4,512,256]{2,1,0:T(8,128)} %bitcast.18), calls=%async_computation.3 | async-start | bytes 4194304 | tf_op jit(solution)/shard_map/all_to_all | solution.py:319
  102.1 0.1 collective-permute-start.12
  102.2 1.2 collective-permute-done.12
  103.5 0.2 collective-permute-start.16
  103.7 1.7 %collective-permute-start.15 = (f32[16,1024]{1,0:T(8,128)S(1)}, f32[16,1024]{1,0:T(8,128)S(1)}, u32[]{:S(2)}, u32[]{:S(2)}) collective-permute-start(f32[16,1024]{1,0:T(8,128)S(1)} %add.36.a), channel_id=1, source_target_pairs={{0,128},{64,192},{128,0},{192,64},{1,129},{65,193},{129,1},{193,65... | collective-permute-start | bytes 196616 | tf_op jit(solution)/shard_map/ppermute | solution.py:331
  105.4 1.1 collective-permute-start.14
  106.5 0.7 collective-permute-start.13
  107.2 2.4 %collective-permute-done.15.d = f32[16,1024]{1,0:T(8,128)S(1)} collective-permute-done((f32[16,1024]{1,0:T(8,128)S(1)}, f32[16,1024]{1,0:T(8,128)S(1)}, u32[]{:S(2)}, u32[]{:S(2)}) %collective-permute-start.15) | collective-permute-done | bytes 65568 | tf_op jit(solution)/shard_map/ppermute | solution.py:331
  109.6 1.4 collective-permute-done.14.c
  111.0 0.4 mixed.1
  111.4 0.8 collective-permute-start.19
  112.2 1.0 collective-permute-start.18
  113.2 2.6 %collective-permute-start.17 = (f32[16,256]{1,0:T(8,128)S(1)}, f32[16,256]{1,0:T(8,128)S(1)}, u32[]{:S(2)}, u32[]{:S(2)}) collective-permute-start(f32[16,256]{1,0:T(8,128)S(1)} %get-tuple-element.48), channel_id=1, source_target_pairs={{0,1},{1,0},{2,3},{3,2},{4,5},{5,4},{6,7},{7,6},{8,9},{9,8},{10,11... | collective-permute-start | bytes 49160 | tf_op jit(solution)/shard_map/ppermute | solution.py:331
  115.8 0.4 collective-permute-done.19
  116.2 1.5 collective-permute-done.17
  117.7 1.3 collective-permute-start.20
  118.9 6.4 %collective-permute-done.20 = f32[16,256]{1,0:T(8,128)S(1)} collective-permute-done((f32[16,256]{1,0:T(8,128)S(1)}, f32[16,256]{1,0:T(8,128)S(1)}, u32[]{:S(2)}, u32[]{:S(2)}) %collective-permute-start.20) | collective-permute-done | bytes 16416 | tf_op jit(solution)/shard_map/ppermute | solution.py:331
  125.4 1.2 collective-permute-done.21.after
  126.6 0.9 gather.1
  127.5 5.2 %all-to-all-start.4 = ((f32[8,64,256]{2,1,0:T(8,128)}), f32[8,64,256]{2,1,0:T(8,128)S(1)}, u32[]{:S(2)}, u32[]{:S(2)}) async-start(f32[8,64,256]{2,1,0:T(8,128)} %bitcast.15), calls=%async_computation.4 | async-start | bytes 1048576 | tf_op jit(solution)/shard_map/all_to_all | solution.py:319
  132.7 2.0 %collective-permute-start.23 = (f32[32,256]{1,0:T(8,128)S(1)}, f32[32,256]{1,0:T(8,128)S(1)}, u32[]{:S(2)}, u32[]{:S(2)}) collective-permute-start(f32[32,256]{1,0:T(8,128)S(1)} %pad_maximum_fusion), channel_id=1, source_target_pairs={{0,192},{64,128},{128,64},{192,0},{1,193},{65,129},{129,65},{193,1... | collective-permute-start | bytes 98312 | tf_op jit(solution)/shard_map/ppermute | solution.py:331
  134.8 0.6 collective-permute-start.24
  135.4 1.5 collective-permute-start.22
  136.8 0.0 collective-permute-start.28
  136.8 1.0 collective-permute-done.23
  137.9 2.3 %collective-permute-done.24 = f32[32,256]{1,0:T(8,128)S(1)} collective-permute-done((f32[32,256]{1,0:T(8,128)S(1)}, f32[32,256]{1,0:T(8,128)S(1)}, u32[]{:S(2)}, u32[]{:S(2)}) %collective-permute-start.24) | collective-permute-done | bytes 32800 | tf_op jit(solution)/shard_map/ppermute | solution.py:331
  140.2 3.5 %collective-permute-start.27 = (f32[32,256]{1,0:T(8,128)S(1)}, f32[32,256]{1,0:T(8,128)S(1)}, u32[]{:S(2)}, u32[]{:S(2)}) collective-permute-start(f32[32,256]{1,0:T(8,128)S(1)} %add_add_fusion.mixed_a), channel_id=1, source_target_pairs={{0,16},{8,24},{16,0},{24,8},{1,17},{9,25},{17,1},{25,9},{2,18},{10... | collective-permute-start | bytes 98312 | tf_op jit(solution)/shard_map/ppermute | solution.py:331
  143.7 1.2 collective-permute-start.26
  144.9 0.8 collective-permute-done.27.mixed_d
  145.7 3.1 %collective-permute-done.26.mixed_c = f32[32,256]{1,0:T(8,128)S(1)} collective-permute-done((f32[32,256]{1,0:T(8,128)S(1)}, f32[32,256]{1,0:T(8,128)S(1)}, u32[]{:S(2)}, u32[]{:S(2)}) %collective-permute-start.26) | collective-permute-done | bytes 32800 | tf_op jit(solution)/shard_map/ppermute | solution.py:331
  148.8 2.9 %final.1 = f32[1024,256]{1,0:T(8,128)} custom-call(f32[32,256]{1,0:T(8,128)S(1)} %add_add_fusion.mixed_a, f32[32,256]{1,0:T(8,128)S(1)} %collective-permute-done.25.mixed_b, f32[32,256]{1,0:T(8,128)S(1)} %collective-permute-done.26.mixed_c, f32[32,256]{1,0:T(8,128)S(1)} %collective-permute-done.27.mixed_d, f32[32,256]{1,0:T(8,128)S(1)} %get-tuple-element.41.basis_t, ...), custom_call_target="tpu_custom_call" | custom-call | tf_op jit(solution)/shard_map/final/pallas_call | solution.py:439
  151.7 0.7 reduce_sum.9
  (25 shorter events, 0.1 us)
Async XLA Ops:
  4.7 1.3 collective-permute-start
  6.0 7.8 %collective-permute-start.3 = (f32[8,128]{1,0:T(8,128)S(1)}, f32[8,128]{1,0:T(8,128)S(1)}, u32[]{:S(2)}, u32[]{:S(2)}) collective-permute-start(f32[8,128]{1,0:T(8,128)S(1)} %add.33.after), channel_id=1, source_target_pairs={{0,128},{64,192},{128,0},{192,64},{1,129},{65,193},{129,1},{193,65... | collective-permute-start | bytes 12296 | tf_op jit(solution)/shard_map/ppermute | solution.py:331
  9.0 4.8 %collective-permute-start.2 = (f32[8,128]{1,0:T(8,128)S(1)}, f32[8,128]{1,0:T(8,128)S(1)}, u32[]{:S(2)}, u32[]{:S(2)}) collective-permute-start(f32[8,128]{1,0:T(8,128)S(1)} %add.33.after), channel_id=1, source_target_pairs={{0,192},{64,128},{128,64},{192,0},{1,193},{65,129},{129,65},{193,1... | collective-permute-start | bytes 12296 | tf_op jit(solution)/shard_map/ppermute | solution.py:331
  10.1 3.7 %collective-permute-start.1 = (f32[8,128]{1,0:T(8,128)S(1)}, f32[8,128]{1,0:T(8,128)S(1)}, u32[]{:S(2)}, u32[]{:S(2)}) collective-permute-start(f32[8,128]{1,0:T(8,128)S(1)} %add.33.after), channel_id=1, source_target_pairs={{0,64},{64,0},{128,192},{192,128},{1,65},{65,1},{129,193},{193,129... | collective-permute-start | bytes 12296 | tf_op jit(solution)/shard_map/ppermute | solution.py:331
  39.3 1.3 collective-permute-start.4
  40.6 8.1 %collective-permute-start.7 = (f32[8,128]{1,0:T(8,128)S(1)}, f32[8,128]{1,0:T(8,128)S(1)}, u32[]{:S(2)}, u32[]{:S(2)}) collective-permute-start(f32[8,128]{1,0:T(8,128)S(1)} %add.34.after), channel_id=1, source_target_pairs={{0,128},{64,192},{128,0},{192,64},{1,129},{65,193},{129,1},{193,65... | collective-permute-start | bytes 12296 | tf_op jit(solution)/shard_map/ppermute | solution.py:331
  43.9 4.8 %collective-permute-start.6 = (f32[8,128]{1,0:T(8,128)S(1)}, f32[8,128]{1,0:T(8,128)S(1)}, u32[]{:S(2)}, u32[]{:S(2)}) collective-permute-start(f32[8,128]{1,0:T(8,128)S(1)} %add.34.after), channel_id=1, source_target_pairs={{0,192},{64,128},{128,64},{192,0},{1,193},{65,129},{129,65},{193,1... | collective-permute-start | bytes 12296 | tf_op jit(solution)/shard_map/ppermute | solution.py:331
  45.0 3.7 %collective-permute-start.5 = (f32[8,128]{1,0:T(8,128)S(1)}, f32[8,128]{1,0:T(8,128)S(1)}, u32[]{:S(2)}, u32[]{:S(2)}) collective-permute-start(f32[8,128]{1,0:T(8,128)S(1)} %add.34.after), channel_id=1, source_target_pairs={{0,64},{64,0},{128,192},{192,128},{1,65},{65,1},{129,193},{193,129... | collective-permute-start | bytes 12296 | tf_op jit(solution)/shard_map/ppermute | solution.py:331
  67.4 1.3 collective-permute-start.8
  68.7 5.1 %collective-permute-start.11 = (f32[8,128]{1,0:T(8,128)S(1)}, f32[8,128]{1,0:T(8,128)S(1)}, u32[]{:S(2)}, u32[]{:S(2)}) collective-permute-start(f32[8,128]{1,0:T(8,128)S(1)} %add.35), channel_id=1, source_target_pairs={{0,128},{64,192},{128,0},{192,64},{1,129},{65,193},{129,1},{193,65... | collective-permute-start | bytes 12296 | tf_op jit(solution)/shard_map/ppermute | solution.py:331
  71.9 4.8 %collective-permute-start.10 = (f32[8,128]{1,0:T(8,128)S(1)}, f32[8,128]{1,0:T(8,128)S(1)}, u32[]{:S(2)}, u32[]{:S(2)}) collective-permute-start(f32[8,128]{1,0:T(8,128)S(1)} %add.35), channel_id=1, source_target_pairs={{0,192},{64,128},{128,64},{192,0},{1,193},{65,129},{129,65},{193,1... | collective-permute-start | bytes 12296 | tf_op jit(solution)/shard_map/ppermute | solution.py:331
  73.1 3.7 %collective-permute-start.9 = (f32[8,128]{1,0:T(8,128)S(1)}, f32[8,128]{1,0:T(8,128)S(1)}, u32[]{:S(2)}, u32[]{:S(2)}) collective-permute-start(f32[8,128]{1,0:T(8,128)S(1)} %add.35), channel_id=1, source_target_pairs={{0,64},{64,0},{128,192},{192,128},{1,65},{65,1},{129,193},{193,129... | collective-permute-start | bytes 12296 | tf_op jit(solution)/shard_map/ppermute | solution.py:331
  98.5 28.1 %all-to-all-start.3 = ((f32[4,512,256]{2,1,0:T(8,128)}), f32[4,512,256]{2,1,0:T(8,128)S(1)}, u32[]{:S(2)}, u32[]{:S(2)}) async-start(f32[4,512,256]{2,1,0:T(8,128)} %bitcast.18), calls=%async_computation.3 | async-start | bytes 4194304 | tf_op jit(solution)/shard_map/all_to_all | solution.py:319
  102.1 1.3 collective-permute-start.12
  103.5 7.5 %collective-permute-start.16 = (f32[256,1024]{1,0:T(8,128)S(1)}, f32[256,1024]{1,0:T(8,128)S(1)}, u32[]{:S(2)}, u32[]{:S(2)}) collective-permute-start(f32[256,1024]{1,0:T(8,128)S(1)} %get-tuple-element.47.part_t), channel_id=1, source_target_pairs={{0,32},{32,0},{1,33},{33,1},{2,34},{34,2},{3,35},{35,3},{4,36},{36... | collective-permute-start | bytes 3145736 | tf_op jit(solution)/shard_map/ppermute | solution.py:331
  103.7 5.9 %collective-permute-start.15 = (f32[16,1024]{1,0:T(8,128)S(1)}, f32[16,1024]{1,0:T(8,128)S(1)}, u32[]{:S(2)}, u32[]{:S(2)}) collective-permute-start(f32[16,1024]{1,0:T(8,128)S(1)} %add.36.a), channel_id=1, source_target_pairs={{0,128},{64,192},{128,0},{192,64},{1,129},{65,193},{129,1},{193,65... | collective-permute-start | bytes 196616 | tf_op jit(solution)/shard_map/ppermute | solution.py:331
  105.4 5.6 %collective-permute-start.14 = (f32[16,1024]{1,0:T(8,128)S(1)}, f32[16,1024]{1,0:T(8,128)S(1)}, u32[]{:S(2)}, u32[]{:S(2)}) collective-permute-start(f32[16,1024]{1,0:T(8,128)S(1)} %add.36.a), channel_id=1, source_target_pairs={{0,192},{64,128},{128,64},{192,0},{1,193},{65,129},{129,65},{193,1... | collective-permute-start | bytes 196616 | tf_op jit(solution)/shard_map/ppermute | solution.py:331
  106.5 4.5 %collective-permute-start.13 = (f32[16,1024]{1,0:T(8,128)S(1)}, f32[16,1024]{1,0:T(8,128)S(1)}, u32[]{:S(2)}, u32[]{:S(2)}) collective-permute-start(f32[16,1024]{1,0:T(8,128)S(1)} %add.36.a), channel_id=1, source_target_pairs={{0,64},{64,0},{128,192},{192,128},{1,65},{65,1},{129,193},{193,129... | collective-permute-start | bytes 196616 | tf_op jit(solution)/shard_map/ppermute | solution.py:331
  111.4 4.8 %collective-permute-start.19 = (f32[16,256]{1,0:T(8,128)S(1)}, f32[16,256]{1,0:T(8,128)S(1)}, u32[]{:S(2)}, u32[]{:S(2)}) collective-permute-start(f32[16,256]{1,0:T(8,128)S(1)} %get-tuple-element.48), channel_id=1, source_target_pairs={{0,2},{1,3},{2,0},{3,1},{4,6},{5,7},{6,4},{7,5},{8,10},{9,11},{10,... | collective-permute-start | bytes 49160 | tf_op jit(solution)/shard_map/ppermute | solution.py:331
  112.2 4.0 %collective-permute-start.18 = (f32[16,256]{1,0:T(8,128)S(1)}, f32[16,256]{1,0:T(8,128)S(1)}, u32[]{:S(2)}, u32[]{:S(2)}) collective-permute-start(f32[16,256]{1,0:T(8,128)S(1)} %get-tuple-element.48), channel_id=1, source_target_pairs={{0,3},{1,2},{2,1},{3,0},{4,7},{5,6},{6,5},{7,4},{8,11},{9,10},{10,... | collective-permute-start | bytes 49160 | tf_op jit(solution)/shard_map/ppermute | solution.py:331
  113.2 4.5 %collective-permute-start.17 = (f32[16,256]{1,0:T(8,128)S(1)}, f32[16,256]{1,0:T(8,128)S(1)}, u32[]{:S(2)}, u32[]{:S(2)}) collective-permute-start(f32[16,256]{1,0:T(8,128)S(1)} %get-tuple-element.48), channel_id=1, source_target_pairs={{0,1},{1,0},{2,3},{3,2},{4,5},{5,4},{6,7},{7,6},{8,9},{9,8},{10,11... | collective-permute-start | bytes 49160 | tf_op jit(solution)/shard_map/ppermute | solution.py:331
  117.7 7.7 %collective-permute-start.20 = (f32[16,256]{1,0:T(8,128)S(1)}, f32[16,256]{1,0:T(8,128)S(1)}, u32[]{:S(2)}, u32[]{:S(2)}) collective-permute-start(f32[16,256]{1,0:T(8,128)S(1)} %add_add_fusion.1), channel_id=1, source_target_pairs={{0,4},{1,5},{2,6},{3,7},{4,0},{5,1},{6,2},{7,3},{8,12},{9,13},{10,... | collective-permute-start | bytes 49160 | tf_op jit(solution)/shard_map/ppermute | solution.py:331
  125.4 1.2 collective-permute-start.21
  127.5 24.2 %all-to-all-start.4 = ((f32[8,64,256]{2,1,0:T(8,128)}), f32[8,64,256]{2,1,0:T(8,128)S(1)}, u32[]{:S(2)}, u32[]{:S(2)}) async-start(f32[8,64,256]{2,1,0:T(8,128)} %bitcast.15), calls=%async_computation.4 | async-start | bytes 1048576 | tf_op jit(solution)/shard_map/all_to_all | solution.py:319
  132.7 5.1 %collective-permute-start.23 = (f32[32,256]{1,0:T(8,128)S(1)}, f32[32,256]{1,0:T(8,128)S(1)}, u32[]{:S(2)}, u32[]{:S(2)}) collective-permute-start(f32[32,256]{1,0:T(8,128)S(1)} %pad_maximum_fusion), channel_id=1, source_target_pairs={{0,192},{64,128},{128,64},{192,0},{1,193},{65,129},{129,65},{193,1... | collective-permute-start | bytes 98312 | tf_op jit(solution)/shard_map/ppermute | solution.py:331
  134.8 5.4 %collective-permute-start.24 = (f32[32,256]{1,0:T(8,128)S(1)}, f32[32,256]{1,0:T(8,128)S(1)}, u32[]{:S(2)}, u32[]{:S(2)}) collective-permute-start(f32[32,256]{1,0:T(8,128)S(1)} %pad_maximum_fusion), channel_id=1, source_target_pairs={{0,128},{64,192},{128,0},{192,64},{1,129},{65,193},{129,1},{193,65... | collective-permute-start | bytes 98312 | tf_op jit(solution)/shard_map/ppermute | solution.py:331
  135.4 4.8 %collective-permute-start.22 = (f32[32,256]{1,0:T(8,128)S(1)}, f32[32,256]{1,0:T(8,128)S(1)}, u32[]{:S(2)}, u32[]{:S(2)}) collective-permute-start(f32[32,256]{1,0:T(8,128)S(1)} %pad_maximum_fusion), channel_id=1, source_target_pairs={{0,64},{64,0},{128,192},{192,128},{1,65},{65,1},{129,193},{193,129... | collective-permute-start | bytes 98312 | tf_op jit(solution)/shard_map/ppermute | solution.py:331
  136.8 8.0 %collective-permute-start.28 = (f32[16,1024]{1,0:T(8,128)S(1)}, f32[16,1024]{1,0:T(8,128)S(1)}, u32[]{:S(2)}, u32[]{:S(2)}) collective-permute-start(f32[16,1024]{1,0:T(8,128)S(1)} %get-tuple-element.49.factor_mine), channel_id=1, source_target_pairs={{0,32},{32,0},{1,33},{33,1},{2,34},{34,2},{3,35},{35,3},{4,36},{36... | collective-permute-start | bytes 196616 | tf_op jit(solution)/shard_map/ppermute | solution.py:331
  140.2 5.5 %collective-permute-start.27 = (f32[32,256]{1,0:T(8,128)S(1)}, f32[32,256]{1,0:T(8,128)S(1)}, u32[]{:S(2)}, u32[]{:S(2)}) collective-permute-start(f32[32,256]{1,0:T(8,128)S(1)} %add_add_fusion.mixed_a), channel_id=1, source_target_pairs={{0,16},{8,24},{16,0},{24,8},{1,17},{9,25},{17,1},{25,9},{2,18},{10... | collective-permute-start | bytes 98312 | tf_op jit(solution)/shard_map/ppermute | solution.py:331
  143.7 5.1 %collective-permute-start.26 = (f32[32,256]{1,0:T(8,128)S(1)}, f32[32,256]{1,0:T(8,128)S(1)}, u32[]{:S(2)}, u32[]{:S(2)}) collective-permute-start(f32[32,256]{1,0:T(8,128)S(1)} %add_add_fusion.mixed_a), channel_id=1, source_target_pairs={{0,24},{8,16},{16,8},{24,0},{1,25},{9,17},{17,9},{25,1},{2,26},{10... | collective-permute-start | bytes 98312 | tf_op jit(solution)/shard_map/ppermute | solution.py:331
  144.9 4.0 %collective-permute-start.25 = (f32[32,256]{1,0:T(8,128)S(1)}, f32[32,256]{1,0:T(8,128)S(1)}, u32[]{:S(2)}, u32[]{:S(2)}) collective-permute-start(f32[32,256]{1,0:T(8,128)S(1)} %add_add_fusion.mixed_a), channel_id=1, source_target_pairs={{0,8},{8,0},{16,24},{24,16},{1,9},{9,1},{17,25},{25,17},{2,10},{10... | collective-permute-start | bytes 98312 | tf_op jit(solution)/shard_map/ppermute | solution.py:331

commit v6 on v5

--- a/solution.py
+++ b/solution.py
@@ -13,7 +13,7 @@
 F32, BF16 = jnp.float32, jnp.bfloat16
 LANES = 128
 BLOCK = 256
-PIVOTS = 4
+PIVOTS = 8
 MIB = 1 << 20
 
 nt = (((1,), (1,)), ((), ()))
@@ -124,8 +124,8 @@
     return jnp.concatenate([rows[i:i + 1] for i in range(rows.shape[0])], axis=1)
 
 
-def row_kernel(cols_in, like, rest, later, row_out):
-    factor = 1.0 / add4(*(cols_in[i] for i in range(4)))
+def row_kernel(a, b, c, d, like, rest, later, row_out):
+    factor = 1.0 / add4(a[...], b[...], c[...], d[...])
     rows, protos = like.shape
     sums = []
     for i in range(rows // BLOCK):
@@ -151,8 +151,9 @@
         row_out[q] = jnp.concatenate([result, tails[q]], axis=1)
 
 
-def last_row_kernel(cols_in, upper, lower, like, row_out, sums):
-    factor = 1.0 / add4(*(cols_in[i] for i in range(4)))
+def last_row_kernel(a, b, c, d, upper, lower, like, row_out, factor_out, sums):
+    factor = 1.0 / add4(a[...], b[...], c[...], d[...])
+    factor_out[...] = factor
     half, protos = upper.shape
     for number, table in enumerate((upper, lower)):
         for i in range(half // BLOCK):
@@ -195,9 +196,8 @@
         col_out[...] = result
 
 
-def gradient_kernel(ratio, like, upper, lower, cols_in, rows_in, like_scale, feat_t_a, feat_t_b, unit_proto, basis_t,
+def gradient_kernel(ratio, like, upper, lower, factor, rows_in, like_scale, feat_t_a, feat_t_b, unit_proto, basis_t,
                     row_grad, part_t, factor_mine, factor_other, code_scale, gradient, grads, sent):
-    factor = 1.0 / add4(*(cols_in[i] for i in range(4)))
     code_scale[...] = (10.0 / jnp.sum(rows_in[...], axis=0)).reshape(code_scale.shape)
     mine = factor_mine.shape[0]
     basis = basis_t[...].astype(BF16)
@@ -377,8 +377,8 @@
         )(unit_feat, unit_proto, sibling, seed_t, after)
 
     def row_step(cols, rest, later):
-        return call(row_kernel, shape(tall, 1, rows + LANES), name="rows", ins=(V, V, V, A))(
-            cols, stay(like), rest, stay(later)
+        return call(row_kernel, shape(tall, 1, rows + LANES), name="rows", ins=(V,) * 6 + (A,))(
+            *cols, stay(like), rest, stay(later)
         )
 
     def column_step(finish, sums, *outs):
@@ -388,21 +388,20 @@
 
     cols = sum_core(cols)
     upper, feat_t_a, basis_t = sibling_half(0, cols, shape(rank, feat))
-    cols = jnp.stack(fours(cols, "x"))
+    cols = fours(cols, "x")
     row_sums = exchange(row_step(cols, total, upper), proto)
     cols, piece = column_step(False, row_sums, shape(col_tiles, LANES), shape(1, LANES))
     cols = sum_core(cols)
     lower, feat_t_b = sibling_half(half, cols)
-    cols = jnp.stack(fours(cols, "x"))
+    cols = fours(cols, "x")
     row_sums = exchange(row_step(cols, piece, lower), proto)
     cols, like_scale = column_step(True, row_sums, shape(col_tiles, LANES), shape(*per_block))
-    cols = jnp.stack(fours(sum_core(cols), "x"))
-    row_sums = exchange(
-        call(last_row_kernel, shape(tall, row_tiles, LANES), row_scratch, name="rows", ins=(V, V, V, A))(
-            cols, stay(upper), stay(lower), stay(like)
-        ),
-        proto,
-    )
+    cols = fours(sum_core(cols), "x")
+    row_sums, factor = call(
+        last_row_kernel, (shape(tall, row_tiles, LANES), shape(col_tiles, LANES)), row_scratch,
+        name="rows", ins=(V,) * 6 + (A,),
+    )(*cols, stay(upper), stay(lower), stay(like))
+    row_sums = exchange(row_sums, proto)
 
     mine = rank // 2
     row_grad, part_t, factor_mine, factor_other = call(
@@ -417,7 +416,7 @@
         + (V((rows, protos), BF16), V((rows, feat), F32), pltpu.SemaphoreType.DMA((blocks,))),
         name="gradient", ins=(V,) * 10, out_specs=(H, V, V, V),
     )(
-        stay(like), stay(upper), stay(lower), cols, row_sums, like_scale, feat_t_a, feat_t_b, unit_proto,
+        stay(like), stay(upper), stay(lower), factor, row_sums, like_scale, feat_t_a, feat_t_b, unit_proto,
         basis_t,
     )
     factor_mine, part_t = lax.optimization_barrier((factor_mine + swap(factor_other, "c", 1), part_t))
@@ -427,8 +426,8 @@
         mixed_kernel, (shape(mine, protos), shape(mine, feat)), name="mixed",
     )(*fours(factor_mine, "x"), part_t, swap(part_t, "c", 1))
     factor_other = swap(factor_mine, "c", 1)
-    mixed_t = add4(*fours(mixed_t, "z"))
-    mixed_t = mixed_t + swap(mixed_t, "z", 4)
+    mixed_t = mixed_t + swap(mixed_t, "z", 1)
+    mixed_t = add4(mixed_t, *(swap(mixed_t, "z", m) for m in (2, 6, 4)))
     mixed_other = swap(mixed_t, "c", 1)
     grads = call(gather_kernel, shape(deep * rows // tall, feat), name="gather", ins=(V, A))(
         grads, mixed_other

time: 153 us -> 151 us (0.987)
  waiting for transfers between devices: 29 us -> 27.2 us
    ppermute x26, waiting for transfers between devices: 25.6 us -> 23.2 us  [swap(): lax.ppermute(value, axis, [(i, i ^ mask) for i in range(lax.axis_size(axi...]
  transfers between devices with their start and end apart: 31 -> 31, of which waited for: 16 -> 17; matrix products, arithmetic and copies ran while one was open for 0% -> 0% of each run, Pallas kernels for 7% -> 7%
where the time goes in v6:
time: 151 us; the launch traced here: 150 us
  blocking collectives  55.9 us (37%)
  starting transfers between devices  40.9 us (27%)
  waiting for transfers between devices  27.2 us (18%)
  Pallas kernels  25 us (17%)
    all_to_all x3, blocking collectives, exchange(): return lax.all_to_all(value, axes, 0, 0)  55.9 us
    ppermute x26, starting transfers between devices, swap(): lax.ppermute(value, axis, [(i, i ^ mask) for i in range(lax.axis_size(axi...  32.5 us
    ppermute x26, waiting for transfers between devices, swap(): lax.ppermute(value, axis, [(i, i ^ mask) for i in range(lax.axis_size(axi...  23.2 us
    all_to_all x2, starting transfers between devices, exchange(): return lax.all_to_all(value, axes, 0, 0)  8.12 us
    pallas_call x2, Pallas kernels, sibling_half(): call(functools.partial(sibling_kernel, first), (kept(half, protos), shape...  7.23 us
    pallas_call x1, Pallas kernels, on_device(): call(functools.partial(gradient_kernel, ratio), (pltpu.HBM((rows, feat),...  5.46 us
    pallas_call x1, Pallas kernels, on_device(): call(scores_kernel, (shape(rows, feat, dtype=BF16), shape(protos, feat, d...  3.91 us
    ppermute x3, waiting for transfers between devices, sum_core(): return value + lax.ppermute(value, 'c', [(0, 1), (1, 0)])  3.46 us
  transfers between devices with their start and end apart: 31, of which 17 were waited for; matrix products, arithmetic and copies ran while one was open for 0% of the time, Pallas kernels for 7%

profile of v6, /device:TPU:32, one launch (start us, length us, event | category | flops | bytes accessed | tf_op | source)
XLA Modules:
  0.0 150.4 jit_solution(6824135651110986877)
XLA Ops:
  0.6 3.9 %scores.1 = (bf16[2048,256]{1,0:T(8,128)(2,1)S(1)}, bf16[1024,256]{1,0:T(8,128)(2,1)S(1)}, f32[2048,1024]{1,0:T(8,128)S(1)}, f32[8,128]{1,0:T(8,128)S(1)}, f32[8...) custom-call(bf16[2048,256]{1,0:T(8,128)(2,1)} %feat_hbm.1, bf16[1024,256]{1,0:T(8,128)(2,1)} %proto_hbm.1, ...), custom_call_target="tpu_custom_call" | custom-call | tf_op jit(solution)/shard_map/scores/pallas_call | solution.py:352
  4.5 0.1 collective-permute-start
  4.6 1.2 collective-permute-done
  5.8 3.0 %collective-permute-start.3 = (f32[8,128]{1,0:T(8,128)S(1)}, f32[8,128]{1,0:T(8,128)S(1)}, u32[]{:S(2)}, u32[]{:S(2)}) collective-permute-start(f32[8,128]{1,0:T(8,128)S(1)} %add.33.after.a), channel_id=1, source_target_pairs={{0,128},{64,192},{128,0},{192,64},{1,129},{65,193},{129,1},{193,65... | collective-permute-start | bytes 12296 | tf_op jit(solution)/shard_map/ppermute | solution.py:331
  8.8 1.1 collective-permute-start.2
  10.0 0.0 collective-permute-start.1
  10.0 3.6 %sibling.2 = (f32[1024,1024]{1,0:T(8,128)S(1)}, bf16[256,1024]{1,0:T(8,128)(2,1)S(1)}, f32[32,256]{1,0:T(8,128)S(1)}) custom-call(bf16[2048,256]{1,0:T(8,128)(2,1)S(1)} %get-tuple-element.29.unit_feat, bf16[1024,256]{1,0:T(8,128)(2,1)S(1)} %get-tuple-element.30.unit_proto, s32[16,128]{1,0:T(8,128)S(1)} %get-tuple-element.31.sibling, ...), custom_call_target="tpu_custom_call" | custom-call | flops 2147483648 | tf_op jit(solution)/shard_map/sibling/pallas_call | solution.py:373
  13.6 0.0 collective-permute-done.2.c
  13.6 0.9 rows.3
  14.6 23.5 %all_to_all.25.rows_in = f32[32,1,2176]{2,1,0:T(1,128)S(1)} all-to-all(f32[32,1,2176]{2,1,0:T(1,128)S(1)} %rows.3), channel_id=1, replica_groups=mesh['x'=4,'c'=2,'y'=4,'z'=8] {'y','z'}, dimensions={0} | all-to-all | bytes 557056 | tf_op jit(solution)/shard_map/all_to_all | solution.py:319
  38.1 1.0 columns.2
  39.1 0.1 collective-permute-start.4
  39.2 1.2 collective-permute-done.4
  40.4 3.3 %collective-permute-start.7 = (f32[8,128]{1,0:T(8,128)S(1)}, f32[8,128]{1,0:T(8,128)S(1)}, u32[]{:S(2)}, u32[]{:S(2)}) collective-permute-start(f32[8,128]{1,0:T(8,128)S(1)} %add.34.after.a), channel_id=1, source_target_pairs={{0,128},{64,192},{128,0},{192,64},{1,129},{65,193},{129,1},{193,65... | collective-permute-start | bytes 12296 | tf_op jit(solution)/shard_map/ppermute | solution.py:331
  43.6 1.1 collective-permute-start.6
  44.8 0.0 collective-permute-start.5
  44.8 3.6 %sibling.3 = (f32[1024,1024]{1,0:T(8,128)S(1)}, bf16[256,1024]{1,0:T(8,128)(2,1)S(1)}) custom-call(bf16[2048,256]{1,0:T(8,128)(2,1)S(1)} %get-tuple-element.29.unit_feat, bf16[1024,256]{1,0:T(8,128)(2,1)S(1)} %get-tuple-element.30.unit_proto, s32[16,128]{1,0:T(8,128)S(1)} %get-tuple-element.31.sibling, s32[32,256]{1,0:T(8,128)S(1)} %get-tuple-element.32.seed_t, ...), custom_call_target="tpu_custom_call" | custom-call | flops 2147483648 | tf_op jit(solution)/shard_map/sibling/pallas_call | solution.py:373
  48.4 0.0 collective-permute-done.6.c
  48.5 0.9 rows.4
  49.4 16.8 %all_to_all.26.rows_in = f32[32,1,2176]{2,1,0:T(1,128)S(1)} all-to-all(f32[32,1,2176]{2,1,0:T(1,128)S(1)} %rows.4), channel_id=1, replica_groups=mesh['x'=4,'c'=2,'y'=4,'z'=8] {'y','z'}, dimensions={0} | all-to-all | bytes 557056 | tf_op jit(solution)/shard_map/all_to_all | solution.py:319
  66.1 1.0 columns.3
  67.1 0.1 collective-permute-start.8
  67.2 1.2 collective-permute-done.8
  68.4 3.3 %collective-permute-start.11 = (f32[8,128]{1,0:T(8,128)S(1)}, f32[8,128]{1,0:T(8,128)S(1)}, u32[]{:S(2)}, u32[]{:S(2)}) collective-permute-start(f32[8,128]{1,0:T(8,128)S(1)} %add.35.a), channel_id=1, source_target_pairs={{0,128},{64,192},{128,0},{192,64},{1,129},{65,193},{129,1},{193,65... | collective-permute-start | bytes 12296 | tf_op jit(solution)/shard_map/ppermute | solution.py:331
  71.7 1.1 collective-permute-start.10
  72.8 0.7 collective-permute-done.11.d
  73.5 3.0 %collective-permute-done.10.c = f32[8,128]{1,0:T(8,128)S(1)} collective-permute-done((f32[8,128]{1,0:T(8,128)S(1)}, f32[8,128]{1,0:T(8,128)S(1)}, u32[]{:S(2)}, u32[]{:S(2)}) %collective-permute-start.10) | collective-permute-done | bytes 4128 | tf_op jit(solution)/shard_map/ppermute | solution.py:331
  76.5 0.7 rows.5
  77.1 15.6 %all_to_all.27.rows_in = f32[32,16,128]{2,1,0:T(8,128)S(1)} all-to-all(f32[32,16,128]{2,1,0:T(8,128)S(1)} %get-tuple-element.41), channel_id=1, replica_groups=mesh['x'=4,'c'=2,'y'=4,'z'=8] {'y','z'}, dimensions={0} | all-to-all | bytes 524288 | tf_op jit(solution)/shard_map/all_to_all | solution.py:319
  92.7 5.5 %gradient.1 = (f32[2048,256]{1,0:T(8,128)}, f32[256,1024]{1,0:T(8,128)S(1)}, f32[16,1024]{1,0:T(8,128)S(1)}, f32[16,1024]{1,0:T(8,128)S(1)}) custom-call(f32[2048,1024]{1,0:T(8,128)S(1)} %get-tuple-element.28.like, f32[1024,1024]{1,0:T(8,128)S(1)} %get-tuple-element.34.later.upper, f32[1024,1024]{1,0:T(8,128)S(1)} %get-tuple-element.37.later.lower, ...), custom_call_target="tpu_custom_call" | custom-call | tf_op jit(solution)/shard_map/gradient/pallas_call | solution.py:407
  98.2 3.6 %all-to-all-start.3 = ((f32[4,512,256]{2,1,0:T(8,128)}), f32[4,512,256]{2,1,0:T(8,128)S(1)}, u32[]{:S(2)}, u32[]{:S(2)}) async-start(f32[4,512,256]{2,1,0:T(8,128)} %bitcast.4), calls=%async_computation.3 | async-start | bytes 4194304 | tf_op jit(solution)/shard_map/all_to_all | solution.py:319
  101.8 0.1 collective-permute-start.12
  101.9 1.2 collective-permute-done.12
  103.2 0.2 collective-permute-start.16
  103.4 1.7 %collective-permute-start.15 = (f32[16,1024]{1,0:T(8,128)S(1)}, f32[16,1024]{1,0:T(8,128)S(1)}, u32[]{:S(2)}, u32[]{:S(2)}) collective-permute-start(f32[16,1024]{1,0:T(8,128)S(1)} %add.36.a), channel_id=1, source_target_pairs={{0,128},{64,192},{128,0},{192,64},{1,129},{65,193},{129,1},{193,65... | collective-permute-start | bytes 196616 | tf_op jit(solution)/shard_map/ppermute | solution.py:331
  105.1 1.1 collective-permute-start.14
  106.2 0.7 collective-permute-start.13
  106.9 2.4 %collective-permute-done.15.d = f32[16,1024]{1,0:T(8,128)S(1)} collective-permute-done((f32[16,1024]{1,0:T(8,128)S(1)}, f32[16,1024]{1,0:T(8,128)S(1)}, u32[]{:S(2)}, u32[]{:S(2)}) %collective-permute-start.15) | collective-permute-done | bytes 65568 | tf_op jit(solution)/shard_map/ppermute | solution.py:331
  109.3 1.4 collective-permute-done.14.c
  110.7 0.4 mixed.1
  111.1 0.3 collective-permute-start.17
  111.4 3.4 %collective-permute-done.17 = f32[16,256]{1,0:T(8,128)S(1)} collective-permute-done((f32[16,256]{1,0:T(8,128)S(1)}, f32[16,256]{1,0:T(8,128)S(1)}, u32[]{:S(2)}, u32[]{:S(2)}) %collective-permute-start.17) | collective-permute-done | bytes 16416 | tf_op jit(solution)/shard_map/ppermute | solution.py:331
  114.8 0.9 collective-permute-start.20
  115.7 3.5 %collective-permute-start.19 = (f32[16,256]{1,0:T(8,128)S(1)}, f32[16,256]{1,0:T(8,128)S(1)}, u32[]{:S(2)}, u32[]{:S(2)}) collective-permute-start(f32[16,256]{1,0:T(8,128)S(1)} %add.37), channel_id=1, source_target_pairs={{0,6},{1,7},{2,4},{3,5},{4,2},{5,3},{6,0},{7,1},{8,14},{9,15},{10,... | collective-permute-start | bytes 49160 | tf_op jit(solution)/shard_map/ppermute | solution.py:331
  119.2 2.1 %collective-permute-start.18 = (f32[16,256]{1,0:T(8,128)S(1)}, f32[16,256]{1,0:T(8,128)S(1)}, u32[]{:S(2)}, u32[]{:S(2)}) collective-permute-start(f32[16,256]{1,0:T(8,128)S(1)} %add.37), channel_id=1, source_target_pairs={{0,2},{1,3},{2,0},{3,1},{4,6},{5,7},{6,4},{7,5},{8,10},{9,11},{10,... | collective-permute-start | bytes 49160 | tf_op jit(solution)/shard_map/ppermute | solution.py:331
  121.3 1.1 collective-permute-done.20
  122.5 1.4 collective-permute-done.18
  123.9 0.1 collective-permute-start.21
  123.9 1.2 collective-permute-done.21.after
  125.1 0.5 all-to-all-done.3.grads
  125.7 0.9 gather.1
  126.5 4.5 %all-to-all-start.4 = ((f32[8,64,256]{2,1,0:T(8,128)}), f32[8,64,256]{2,1,0:T(8,128)S(1)}, u32[]{:S(2)}, u32[]{:S(2)}) async-start(f32[8,64,256]{2,1,0:T(8,128)} %bitcast.3), calls=%async_computation.4 | async-start | bytes 1048576 | tf_op jit(solution)/shard_map/all_to_all | solution.py:319
  131.0 2.0 %collective-permute-start.23 = (f32[32,256]{1,0:T(8,128)S(1)}, f32[32,256]{1,0:T(8,128)S(1)}, u32[]{:S(2)}, u32[]{:S(2)}) collective-permute-start(f32[32,256]{1,0:T(8,128)S(1)} %pad_maximum_fusion), channel_id=1, source_target_pairs={{0,192},{64,128},{128,64},{192,0},{1,193},{65,129},{129,65},{193,1... | collective-permute-start | bytes 98312 | tf_op jit(solution)/shard_map/ppermute | solution.py:331
  133.1 0.5 collective-permute-start.24
  133.6 1.5 %collective-permute-start.22 = (f32[32,256]{1,0:T(8,128)S(1)}, f32[32,256]{1,0:T(8,128)S(1)}, u32[]{:S(2)}, u32[]{:S(2)}) collective-permute-start(f32[32,256]{1,0:T(8,128)S(1)} %pad_maximum_fusion), channel_id=1, source_target_pairs={{0,64},{64,0},{128,192},{192,128},{1,65},{65,1},{129,193},{193,129... | collective-permute-start | bytes 98312 | tf_op jit(solution)/shard_map/ppermute | solution.py:331
  135.1 0.0 collective-permute-start.28
  135.1 1.0 collective-permute-done.23
  136.2 2.3 %collective-permute-done.24 = f32[32,256]{1,0:T(8,128)S(1)} collective-permute-done((f32[32,256]{1,0:T(8,128)S(1)}, f32[32,256]{1,0:T(8,128)S(1)}, u32[]{:S(2)}, u32[]{:S(2)}) %collective-permute-start.24) | collective-permute-done | bytes 32800 | tf_op jit(solution)/shard_map/ppermute | solution.py:331
  138.5 3.5 %collective-permute-start.27 = (f32[32,256]{1,0:T(8,128)S(1)}, f32[32,256]{1,0:T(8,128)S(1)}, u32[]{:S(2)}, u32[]{:S(2)}) collective-permute-start(f32[32,256]{1,0:T(8,128)S(1)} %add_add_fusion.mixed_a), channel_id=1, source_target_pairs={{0,16},{8,24},{16,0},{24,8},{1,17},{9,25},{17,1},{25,9},{2,18},{10... | collective-permute-start | bytes 98312 | tf_op jit(solution)/shard_map/ppermute | solution.py:331
  142.0 1.2 collective-permute-start.26
  143.2 0.8 collective-permute-done.27.mixed_d
  144.0 3.1 %collective-permute-done.26.mixed_c = f32[32,256]{1,0:T(8,128)S(1)} collective-permute-done((f32[32,256]{1,0:T(8,128)S(1)}, f32[32,256]{1,0:T(8,128)S(1)}, u32[]{:S(2)}, u32[]{:S(2)}) %collective-permute-start.26) | collective-permute-done | bytes 32800 | tf_op jit(solution)/shard_map/ppermute | solution.py:331
  147.1 2.6 %final.1 = f32[1024,256]{1,0:T(8,128)} custom-call(f32[32,256]{1,0:T(8,128)S(1)} %add_add_fusion.mixed_a, f32[32,256]{1,0:T(8,128)S(1)} %collective-permute-done.25.mixed_b, f32[32,256]{1,0:T(8,128)S(1)} %collective-permute-done.26.mixed_c, f32[32,256]{1,0:T(8,128)S(1)} %collective-permute-done.27.mixed_d, f32[32,256]{1,0:T(8,128)S(1)} %get-tuple-element.45.basis_t, ...), custom_call_target="tpu_custom_call" | custom-call | tf_op jit(solution)/shard_map/final/pallas_call | solution.py:438
  149.8 0.7 reduce_sum.9
  (22 shorter events, 0.1 us)
Async XLA Ops:
  4.5 1.3 collective-permute-start
  5.8 7.8 %collective-permute-start.3 = (f32[8,128]{1,0:T(8,128)S(1)}, f32[8,128]{1,0:T(8,128)S(1)}, u32[]{:S(2)}, u32[]{:S(2)}) collective-permute-start(f32[8,128]{1,0:T(8,128)S(1)} %add.33.after.a), channel_id=1, source_target_pairs={{0,128},{64,192},{128,0},{192,64},{1,129},{65,193},{129,1},{193,65... | collective-permute-start | bytes 12296 | tf_op jit(solution)/shard_map/ppermute | solution.py:331
  8.8 4.8 %collective-permute-start.2 = (f32[8,128]{1,0:T(8,128)S(1)}, f32[8,128]{1,0:T(8,128)S(1)}, u32[]{:S(2)}, u32[]{:S(2)}) collective-permute-start(f32[8,128]{1,0:T(8,128)S(1)} %add.33.after.a), channel_id=1, source_target_pairs={{0,192},{64,128},{128,64},{192,0},{1,193},{65,129},{129,65},{193,1... | collective-permute-start | bytes 12296 | tf_op jit(solution)/shard_map/ppermute | solution.py:331
  10.0 3.7 %collective-permute-start.1 = (f32[8,128]{1,0:T(8,128)S(1)}, f32[8,128]{1,0:T(8,128)S(1)}, u32[]{:S(2)}, u32[]{:S(2)}) collective-permute-start(f32[8,128]{1,0:T(8,128)S(1)} %add.33.after.a), channel_id=1, source_target_pairs={{0,64},{64,0},{128,192},{192,128},{1,65},{65,1},{129,193},{193,129... | collective-permute-start | bytes 12296 | tf_op jit(solution)/shard_map/ppermute | solution.py:331
  39.1 1.3 collective-permute-start.4
  40.4 8.0 %collective-permute-start.7 = (f32[8,128]{1,0:T(8,128)S(1)}, f32[8,128]{1,0:T(8,128)S(1)}, u32[]{:S(2)}, u32[]{:S(2)}) collective-permute-start(f32[8,128]{1,0:T(8,128)S(1)} %add.34.after.a), channel_id=1, source_target_pairs={{0,128},{64,192},{128,0},{192,64},{1,129},{65,193},{129,1},{193,65... | collective-permute-start | bytes 12296 | tf_op jit(solution)/shard_map/ppermute | solution.py:331
  43.6 4.8 %collective-permute-start.6 = (f32[8,128]{1,0:T(8,128)S(1)}, f32[8,128]{1,0:T(8,128)S(1)}, u32[]{:S(2)}, u32[]{:S(2)}) collective-permute-start(f32[8,128]{1,0:T(8,128)S(1)} %add.34.after.a), channel_id=1, source_target_pairs={{0,192},{64,128},{128,64},{192,0},{1,193},{65,129},{129,65},{193,1... | collective-permute-start | bytes 12296 | tf_op jit(solution)/shard_map/ppermute | solution.py:331
  44.8 3.7 %collective-permute-start.5 = (f32[8,128]{1,0:T(8,128)S(1)}, f32[8,128]{1,0:T(8,128)S(1)}, u32[]{:S(2)}, u32[]{:S(2)}) collective-permute-start(f32[8,128]{1,0:T(8,128)S(1)} %add.34.after.a), channel_id=1, source_target_pairs={{0,64},{64,0},{128,192},{192,128},{1,65},{65,1},{129,193},{193,129... | collective-permute-start | bytes 12296 | tf_op jit(solution)/shard_map/ppermute | solution.py:331
  67.1 1.3 collective-permute-start.8
  68.4 5.1 %collective-permute-start.11 = (f32[8,128]{1,0:T(8,128)S(1)}, f32[8,128]{1,0:T(8,128)S(1)}, u32[]{:S(2)}, u32[]{:S(2)}) collective-permute-start(f32[8,128]{1,0:T(8,128)S(1)} %add.35.a), channel_id=1, source_target_pairs={{0,128},{64,192},{128,0},{192,64},{1,129},{65,193},{129,1},{193,65... | collective-permute-start | bytes 12296 | tf_op jit(solution)/shard_map/ppermute | solution.py:331
  71.7 4.8 %collective-permute-start.10 = (f32[8,128]{1,0:T(8,128)S(1)}, f32[8,128]{1,0:T(8,128)S(1)}, u32[]{:S(2)}, u32[]{:S(2)}) collective-permute-start(f32[8,128]{1,0:T(8,128)S(1)} %add.35.a), channel_id=1, source_target_pairs={{0,192},{64,128},{128,64},{192,0},{1,193},{65,129},{129,65},{193,1... | collective-permute-start | bytes 12296 | tf_op jit(solution)/shard_map/ppermute | solution.py:331
  72.8 3.7 %collective-permute-start.9 = (f32[8,128]{1,0:T(8,128)S(1)}, f32[8,128]{1,0:T(8,128)S(1)}, u32[]{:S(2)}, u32[]{:S(2)}) collective-permute-start(f32[8,128]{1,0:T(8,128)S(1)} %add.35.a), channel_id=1, source_target_pairs={{0,64},{64,0},{128,192},{192,128},{1,65},{65,1},{129,193},{193,129... | collective-permute-start | bytes 12296 | tf_op jit(solution)/shard_map/ppermute | solution.py:331
  98.2 27.5 %all-to-all-start.3 = ((f32[4,512,256]{2,1,0:T(8,128)}), f32[4,512,256]{2,1,0:T(8,128)S(1)}, u32[]{:S(2)}, u32[]{:S(2)}) async-start(f32[4,512,256]{2,1,0:T(8,128)} %bitcast.4), calls=%async_computation.3 | async-start | bytes 4194304 | tf_op jit(solution)/shard_map/all_to_all | solution.py:319
  101.8 1.3 collective-permute-start.12
  103.2 7.5 %collective-permute-start.16 = (f32[256,1024]{1,0:T(8,128)S(1)}, f32[256,1024]{1,0:T(8,128)S(1)}, u32[]{:S(2)}, u32[]{:S(2)}) collective-permute-start(f32[256,1024]{1,0:T(8,128)S(1)} %get-tuple-element.51.part_t), channel_id=1, source_target_pairs={{0,32},{32,0},{1,33},{33,1},{2,34},{34,2},{3,35},{35,3},{4,36},{36... | collective-permute-start | bytes 3145736 | tf_op jit(solution)/shard_map/ppermute | solution.py:331
  103.4 5.9 %collective-permute-start.15 = (f32[16,1024]{1,0:T(8,128)S(1)}, f32[16,1024]{1,0:T(8,128)S(1)}, u32[]{:S(2)}, u32[]{:S(2)}) collective-permute-start(f32[16,1024]{1,0:T(8,128)S(1)} %add.36.a), channel_id=1, source_target_pairs={{0,128},{64,192},{128,0},{192,64},{1,129},{65,193},{129,1},{193,65... | collective-permute-start | bytes 196616 | tf_op jit(solution)/shard_map/ppermute | solution.py:331
  105.1 5.6 %collective-permute-start.14 = (f32[16,1024]{1,0:T(8,128)S(1)}, f32[16,1024]{1,0:T(8,128)S(1)}, u32[]{:S(2)}, u32[]{:S(2)}) collective-permute-start(f32[16,1024]{1,0:T(8,128)S(1)} %add.36.a), channel_id=1, source_target_pairs={{0,192},{64,128},{128,64},{192,0},{1,193},{65,129},{129,65},{193,1... | collective-permute-start | bytes 196616 | tf_op jit(solution)/shard_map/ppermute | solution.py:331
  106.2 4.5 %collective-permute-start.13 = (f32[16,1024]{1,0:T(8,128)S(1)}, f32[16,1024]{1,0:T(8,128)S(1)}, u32[]{:S(2)}, u32[]{:S(2)}) collective-permute-start(f32[16,1024]{1,0:T(8,128)S(1)} %add.36.a), channel_id=1, source_target_pairs={{0,64},{64,0},{128,192},{192,128},{1,65},{65,1},{129,193},{193,129... | collective-permute-start | bytes 196616 | tf_op jit(solution)/shard_map/ppermute | solution.py:331
  111.1 3.8 %collective-permute-start.17 = (f32[16,256]{1,0:T(8,128)S(1)}, f32[16,256]{1,0:T(8,128)S(1)}, u32[]{:S(2)}, u32[]{:S(2)}) collective-permute-start(f32[16,256]{1,0:T(8,128)S(1)} %get-tuple-element.52), channel_id=1, source_target_pairs={{0,1},{1,0},{2,3},{3,2},{4,5},{5,4},{6,7},{7,6},{8,9},{9,8},{10,11... | collective-permute-start | bytes 49160 | tf_op jit(solution)/shard_map/ppermute | solution.py:331
  114.8 7.6 %collective-permute-start.20 = (f32[16,256]{1,0:T(8,128)S(1)}, f32[16,256]{1,0:T(8,128)S(1)}, u32[]{:S(2)}, u32[]{:S(2)}) collective-permute-start(f32[16,256]{1,0:T(8,128)S(1)} %add.37), channel_id=1, source_target_pairs={{0,4},{1,5},{2,6},{3,7},{4,0},{5,1},{6,2},{7,3},{8,12},{9,13},{10,... | collective-permute-start | bytes 49160 | tf_op jit(solution)/shard_map/ppermute | solution.py:331
  115.7 6.7 %collective-permute-start.19 = (f32[16,256]{1,0:T(8,128)S(1)}, f32[16,256]{1,0:T(8,128)S(1)}, u32[]{:S(2)}, u32[]{:S(2)}) collective-permute-start(f32[16,256]{1,0:T(8,128)S(1)} %add.37), channel_id=1, source_target_pairs={{0,6},{1,7},{2,4},{3,5},{4,2},{5,3},{6,0},{7,1},{8,14},{9,15},{10,... | collective-permute-start | bytes 49160 | tf_op jit(solution)/shard_map/ppermute | solution.py:331
  119.2 4.6 %collective-permute-start.18 = (f32[16,256]{1,0:T(8,128)S(1)}, f32[16,256]{1,0:T(8,128)S(1)}, u32[]{:S(2)}, u32[]{:S(2)}) collective-permute-start(f32[16,256]{1,0:T(8,128)S(1)} %add.37), channel_id=1, source_target_pairs={{0,2},{1,3},{2,0},{3,1},{4,6},{5,7},{6,4},{7,5},{8,10},{9,11},{10,... | collective-permute-start | bytes 49160 | tf_op jit(solution)/shard_map/ppermute | solution.py:331
  123.9 1.3 collective-permute-start.21
  126.5 23.2 %all-to-all-start.4 = ((f32[8,64,256]{2,1,0:T(8,128)}), f32[8,64,256]{2,1,0:T(8,128)S(1)}, u32[]{:S(2)}, u32[]{:S(2)}) async-start(f32[8,64,256]{2,1,0:T(8,128)} %bitcast.3), calls=%async_computation.4 | async-start | bytes 1048576 | tf_op jit(solution)/shard_map/all_to_all | solution.py:319
  131.0 5.1 %collective-permute-start.23 = (f32[32,256]{1,0:T(8,128)S(1)}, f32[32,256]{1,0:T(8,128)S(1)}, u32[]{:S(2)}, u32[]{:S(2)}) collective-permute-start(f32[32,256]{1,0:T(8,128)S(1)} %pad_maximum_fusion), channel_id=1, source_target_pairs={{0,192},{64,128},{128,64},{192,0},{1,193},{65,129},{129,65},{193,1... | collective-permute-start | bytes 98312 | tf_op jit(solution)/shard_map/ppermute | solution.py:331
  133.1 5.4 %collective-permute-start.24 = (f32[32,256]{1,0:T(8,128)S(1)}, f32[32,256]{1,0:T(8,128)S(1)}, u32[]{:S(2)}, u32[]{:S(2)}) collective-permute-start(f32[32,256]{1,0:T(8,128)S(1)} %pad_maximum_fusion), channel_id=1, source_target_pairs={{0,128},{64,192},{128,0},{192,64},{1,129},{65,193},{129,1},{193,65... | collective-permute-start | bytes 98312 | tf_op jit(solution)/shard_map/ppermute | solution.py:331
  133.6 4.9 %collective-permute-start.22 = (f32[32,256]{1,0:T(8,128)S(1)}, f32[32,256]{1,0:T(8,128)S(1)}, u32[]{:S(2)}, u32[]{:S(2)}) collective-permute-start(f32[32,256]{1,0:T(8,128)S(1)} %pad_maximum_fusion), channel_id=1, source_target_pairs={{0,64},{64,0},{128,192},{192,128},{1,65},{65,1},{129,193},{193,129... | collective-permute-start | bytes 98312 | tf_op jit(solution)/shard_map/ppermute | solution.py:331
  135.1 8.0 %collective-permute-start.28 = (f32[16,1024]{1,0:T(8,128)S(1)}, f32[16,1024]{1,0:T(8,128)S(1)}, u32[]{:S(2)}, u32[]{:S(2)}) collective-permute-start(f32[16,1024]{1,0:T(8,128)S(1)} %get-tuple-element.53.factor_mine), channel_id=1, source_target_pairs={{0,32},{32,0},{1,33},{33,1},{2,34},{34,2},{3,35},{35,3},{4,36},{36... | collective-permute-start | bytes 196616 | tf_op jit(solution)/shard_map/ppermute | solution.py:331
  138.5 5.5 %collective-permute-start.27 = (f32[32,256]{1,0:T(8,128)S(1)}, f32[32,256]{1,0:T(8,128)S(1)}, u32[]{:S(2)}, u32[]{:S(2)}) collective-permute-start(f32[32,256]{1,0:T(8,128)S(1)} %add_add_fusion.mixed_a), channel_id=1, source_target_pairs={{0,16},{8,24},{16,0},{24,8},{1,17},{9,25},{17,1},{25,9},{2,18},{10... | collective-permute-start | bytes 98312 | tf_op jit(solution)/shard_map/ppermute | solution.py:331
  142.0 5.1 %collective-permute-start.26 = (f32[32,256]{1,0:T(8,128)S(1)}, f32[32,256]{1,0:T(8,128)S(1)}, u32[]{:S(2)}, u32[]{:S(2)}) collective-permute-start(f32[32,256]{1,0:T(8,128)S(1)} %add_add_fusion.mixed_a), channel_id=1, source_target_pairs={{0,24},{8,16},{16,8},{24,0},{1,25},{9,17},{17,9},{25,1},{2,26},{10... | collective-permute-start | bytes 98312 | tf_op jit(solution)/shard_map/ppermute | solution.py:331
  143.2 4.0 %collective-permute-start.25 = (f32[32,256]{1,0:T(8,128)S(1)}, f32[32,256]{1,0:T(8,128)S(1)}, u32[]{:S(2)}, u32[]{:S(2)}) collective-permute-start(f32[32,256]{1,0:T(8,128)S(1)} %add_add_fusion.mixed_a), channel_id=1, source_target_pairs={{0,8},{8,0},{16,24},{24,16},{1,9},{9,1},{17,25},{25,17},{2,10},{10... | collective-permute-start | bytes 98312 | tf_op jit(solution)/shard_map/ppermute | solution.py:331

commit v7 on v6

--- a/solution.py
+++ b/solution.py
@@ -88,12 +88,12 @@
         unit = unit_rows(feat[here, :])
         unit_feat[here, :] = unit
         value = jnp.exp(dot16(unit, unit_proto[...], nt) * 10.0)
-        like[here, :] = value
         part = value[:, tile(0)]
         for j in range(1, tiles):
             part = part + value[:, tile(j)]
         total[i] = across(part)
         square = value * value
+        like[here, :] = square
         cols = [cols[j] + fold(square[:, tile(j)]) for j in range(tiles)]
     col_out[...] = jnp.concatenate([jnp.sum(c, axis=0, keepdims=True) for c in cols], axis=0)
     sibling_copy.wait()
@@ -132,7 +132,7 @@
         part = None
         for j in range(protos // LANES):
             value = like[i * BLOCK:(i + 1) * BLOCK, tile(j)]
-            value = value * value * factor[j:j + 1, :]
+            value = value * factor[j:j + 1, :]
             part = value if part is None else part + value
         sums.append(flat(across(part)))
     result = jnp.concatenate(sums, axis=1)
@@ -188,7 +188,7 @@
         weight = down(scale[i])
         for j in range(tiles):
             value = like[i * BLOCK:(i + 1) * BLOCK, tile(j)]
-            cols[j] = cols[j] + fold(value * value * weight)
+            cols[j] = cols[j] + fold(value * weight)
     result = jnp.concatenate([jnp.sum(c, axis=0, keepdims=True) for c in cols], axis=0)
     if len(col_out.shape) == 3:
         copies(col_out, result)
@@ -215,7 +215,8 @@
         first = down(like_scale[i])
         second = down(code_scale[i])
         for j in range(protos // LANES):
-            value = like[here, tile(j)] * first - table[there, tile(j)] * factor[j:j + 1, :] * second
+            square = like[here, tile(j)]
+            value = square * lax.rsqrt(square) * first - table[there, tile(j)] * factor[j:j + 1, :] * second
             gradient[here, tile(j)] = value.astype(BF16)
         grads[here, :] = dot16(gradient[here, :], unit_proto[...], nn)
         copy(i).start()
@@ -430,7 +431,7 @@
     mixed_t = add4(mixed_t, *(swap(mixed_t, "z", m) for m in (2, 6, 4)))
     mixed_other = swap(mixed_t, "c", 1)
     grads = call(gather_kernel, shape(deep * rows // tall, feat), name="gather", ins=(V, A))(
-        grads, mixed_other
+        grads, mixed_t
     )
     mixed_t = jnp.concatenate([mixed_t, mixed_other], axis=0)
     grads = exchange(grads.reshape(deep, rows // tall, feat), "z")

time: 151 us -> 150 us (level)
  transfers between devices with their start and end apart: 31 -> 31, of which waited for: 17 -> 18; matrix products, arithmetic and copies ran while one was open for 0% -> 0% of each run, Pallas kernels for 7% -> 7%
where the time goes in v7:
time: 150 us
  blocking collectives  55.8 us (37%)
  starting transfers between devices  39.5 us (26%)
  waiting for transfers between devices  28.5 us (19%)
  Pallas kernels  24.5 us (16%)
    all_to_all x3, blocking collectives, exchange(): return lax.all_to_all(value, axes, 0, 0)  55.8 us
    ppermute x26, starting transfers between devices, swap(): lax.ppermute(value, axis, [(i, i ^ mask) for i in range(lax.axis_size(axi...  31.5 us
    ppermute x26, waiting for transfers between devices, swap(): lax.ppermute(value, axis, [(i, i ^ mask) for i in range(lax.axis_size(axi...  23.3 us
    all_to_all x2, starting transfers between devices, exchange(): return lax.all_to_all(value, axes, 0, 0)  7.79 us
    pallas_call x2, Pallas kernels, sibling_half(): call(functools.partial(sibling_kernel, first), (kept(half, protos), shape...  7.23 us
    pallas_call x1, Pallas kernels, on_device(): call(functools.partial(gradient_kernel, ratio), (pltpu.HBM((rows, feat),...  6.05 us
    pallas_call x1, Pallas kernels, on_device(): call(scores_kernel, (shape(rows, feat, dtype=BF16), shape(protos, feat, d...  3.86 us
    ppermute x3, waiting for transfers between devices, sum_core(): return value + lax.ppermute(value, 'c', [(0, 1), (1, 0)])  3.46 us
  transfers between devices with their start and end apart: 31, of which 18 were waited for; matrix products, arithmetic and copies ran while one was open for 0% of the time, Pallas kernels for 7%

profile of v7, /device:TPU:32, one launch (start us, length us, event | category | flops | bytes accessed | tf_op | source)
XLA Modules:
  0.0 149.9 jit_solution(1166711434782731657)
XLA Ops:
  0.6 3.9 %scores.1 = (bf16[2048,256]{1,0:T(8,128)(2,1)S(1)}, bf16[1024,256]{1,0:T(8,128)(2,1)S(1)}, f32[2048,1024]{1,0:T(8,128)S(1)}, f32[8,128]{1,0:T(8,128)S(1)}, f32[8...) custom-call(bf16[2048,256]{1,0:T(8,128)(2,1)} %feat_hbm.1, bf16[1024,256]{1,0:T(8,128)(2,1)} %proto_hbm.1, ...), custom_call_target="tpu_custom_call" | custom-call | tf_op jit(solution)/shard_map/scores/pallas_call | solution.py:353
  4.5 0.1 collective-permute-start
  4.6 1.2 collective-permute-done
  5.8 3.0 %collective-permute-start.3 = (f32[8,128]{1,0:T(8,128)S(1)}, f32[8,128]{1,0:T(8,128)S(1)}, u32[]{:S(2)}, u32[]{:S(2)}) collective-permute-start(f32[8,128]{1,0:T(8,128)S(1)} %add.33.after.a), channel_id=1, source_target_pairs={{0,128},{64,192},{128,0},{192,64},{1,129},{65,193},{129,1},{193,65... | collective-permute-start | bytes 12296 | tf_op jit(solution)/shard_map/ppermute | solution.py:332
  8.8 1.1 collective-permute-start.2
  9.9 3.6 %sibling.2 = (f32[1024,1024]{1,0:T(8,128)S(1)}, bf16[256,1024]{1,0:T(8,128)(2,1)S(1)}, f32[32,256]{1,0:T(8,128)S(1)}) custom-call(bf16[2048,256]{1,0:T(8,128)(2,1)S(1)} %get-tuple-element.29.unit_feat, bf16[1024,256]{1,0:T(8,128)(2,1)S(1)} %get-tuple-element.30.unit_proto, s32[16,128]{1,0:T(8,128)S(1)} %get-tuple-element.31.sibling, ...), custom_call_target="tpu_custom_call" | custom-call | flops 2147483648 | tf_op jit(solution)/shard_map/sibling/pallas_call | solution.py:374
  13.5 0.0 collective-permute-done.3.d
  13.5 0.1 collective-permute-done.2.c
  13.6 0.0 collective-permute-done.1.b
  13.6 0.7 rows.3
  14.3 23.5 %all_to_all.25.rows_in = f32[32,1,2176]{2,1,0:T(1,128)S(1)} all-to-all(f32[32,1,2176]{2,1,0:T(1,128)S(1)} %rows.3), channel_id=1, replica_groups=mesh['x'=4,'c'=2,'y'=4,'z'=8] {'y','z'}, dimensions={0} | all-to-all | bytes 557056 | tf_op jit(solution)/shard_map/all_to_all | solution.py:320
  37.8 0.8 columns.2
  38.5 0.1 collective-permute-start.4
  38.6 1.2 collective-permute-done.4
  39.8 3.3 %collective-permute-start.7 = (f32[8,128]{1,0:T(8,128)S(1)}, f32[8,128]{1,0:T(8,128)S(1)}, u32[]{:S(2)}, u32[]{:S(2)}) collective-permute-start(f32[8,128]{1,0:T(8,128)S(1)} %add.34.after.a), channel_id=1, source_target_pairs={{0,128},{64,192},{128,0},{192,64},{1,129},{65,193},{129,1},{193,65... | collective-permute-start | bytes 12296 | tf_op jit(solution)/shard_map/ppermute | solution.py:332
  43.1 1.1 collective-permute-start.6
  44.2 0.0 collective-permute-start.5
  44.2 3.6 %sibling.3 = (f32[1024,1024]{1,0:T(8,128)S(1)}, bf16[256,1024]{1,0:T(8,128)(2,1)S(1)}) custom-call(bf16[2048,256]{1,0:T(8,128)(2,1)S(1)} %get-tuple-element.29.unit_feat, bf16[1024,256]{1,0:T(8,128)(2,1)S(1)} %get-tuple-element.30.unit_proto, s32[16,128]{1,0:T(8,128)S(1)} %get-tuple-element.31.sibling, s32[32,256]{1,0:T(8,128)S(1)} %get-tuple-element.32.seed_t, ...), custom_call_target="tpu_custom_call" | custom-call | flops 2147483648 | tf_op jit(solution)/shard_map/sibling/pallas_call | solution.py:374
  47.8 0.0 collective-permute-done.7.d
  47.9 0.0 collective-permute-done.6.c
  47.9 0.6 rows.4
  48.6 16.8 %all_to_all.26.rows_in = f32[32,1,2176]{2,1,0:T(1,128)S(1)} all-to-all(f32[32,1,2176]{2,1,0:T(1,128)S(1)} %rows.4), channel_id=1, replica_groups=mesh['x'=4,'c'=2,'y'=4,'z'=8] {'y','z'}, dimensions={0} | all-to-all | bytes 557056 | tf_op jit(solution)/shard_map/all_to_all | solution.py:320
  65.3 0.7 columns.3
  66.0 0.1 collective-permute-start.8
  66.1 1.2 collective-permute-done.8
  67.3 3.3 %collective-permute-start.11 = (f32[8,128]{1,0:T(8,128)S(1)}, f32[8,128]{1,0:T(8,128)S(1)}, u32[]{:S(2)}, u32[]{:S(2)}) collective-permute-start(f32[8,128]{1,0:T(8,128)S(1)} %add.35.a), channel_id=1, source_target_pairs={{0,128},{64,192},{128,0},{192,64},{1,129},{65,193},{129,1},{193,65... | collective-permute-start | bytes 12296 | tf_op jit(solution)/shard_map/ppermute | solution.py:332
  70.6 1.1 collective-permute-start.10
  71.7 0.7 collective-permute-done.11.d
  72.4 3.0 %collective-permute-done.10.c = f32[8,128]{1,0:T(8,128)S(1)} collective-permute-done((f32[8,128]{1,0:T(8,128)S(1)}, f32[8,128]{1,0:T(8,128)S(1)}, u32[]{:S(2)}, u32[]{:S(2)}) %collective-permute-start.10) | collective-permute-done | bytes 4128 | tf_op jit(solution)/shard_map/ppermute | solution.py:332
  75.4 0.7 rows.5
  76.1 15.6 %all_to_all.27.rows_in = f32[32,16,128]{2,1,0:T(8,128)S(1)} all-to-all(f32[32,16,128]{2,1,0:T(8,128)S(1)} %get-tuple-element.41), channel_id=1, replica_groups=mesh['x'=4,'c'=2,'y'=4,'z'=8] {'y','z'}, dimensions={0} | all-to-all | bytes 524288 | tf_op jit(solution)/shard_map/all_to_all | solution.py:320
  91.6 6.0 %gradient.1 = (f32[2048,256]{1,0:T(8,128)}, f32[256,1024]{1,0:T(8,128)S(1)}, f32[16,1024]{1,0:T(8,128)S(1)}, f32[16,1024]{1,0:T(8,128)S(1)}) custom-call(f32[2048,1024]{1,0:T(8,128)S(1)} %get-tuple-element.28.like, f32[1024,1024]{1,0:T(8,128)S(1)} %get-tuple-element.34.later.upper, f32[1024,1024]{1,0:T(8,128)S(1)} %get-tuple-element.37.later.lower, ...), custom_call_target="tpu_custom_call" | custom-call | tf_op jit(solution)/shard_map/gradient/pallas_call | solution.py:408
  97.7 3.6 %all-to-all-start.3 = ((f32[4,512,256]{2,1,0:T(8,128)}), f32[4,512,256]{2,1,0:T(8,128)S(1)}, u32[]{:S(2)}, u32[]{:S(2)}) async-start(f32[4,512,256]{2,1,0:T(8,128)} %bitcast.4), calls=%async_computation.3 | async-start | bytes 4194304 | tf_op jit(solution)/shard_map/all_to_all | solution.py:320
  101.3 0.1 collective-permute-start.12
  101.4 1.2 collective-permute-done.12
  102.7 0.2 collective-permute-start.16
  102.9 1.7 %collective-permute-start.15 = (f32[16,1024]{1,0:T(8,128)S(1)}, f32[16,1024]{1,0:T(8,128)S(1)}, u32[]{:S(2)}, u32[]{:S(2)}) collective-permute-start(f32[16,1024]{1,0:T(8,128)S(1)} %add.36.a), channel_id=1, source_target_pairs={{0,128},{64,192},{128,0},{192,64},{1,129},{65,193},{129,1},{193,65... | collective-permute-start | bytes 196616 | tf_op jit(solution)/shard_map/ppermute | solution.py:332
  104.6 1.1 collective-permute-start.14
  105.7 0.7 collective-permute-start.13
  106.4 2.4 %collective-permute-done.15.d = f32[16,1024]{1,0:T(8,128)S(1)} collective-permute-done((f32[16,1024]{1,0:T(8,128)S(1)}, f32[16,1024]{1,0:T(8,128)S(1)}, u32[]{:S(2)}, u32[]{:S(2)}) %collective-permute-start.15) | collective-permute-done | bytes 65568 | tf_op jit(solution)/shard_map/ppermute | solution.py:332
  108.8 1.4 collective-permute-done.14.c
  110.2 0.4 mixed.1
  110.6 0.3 collective-permute-start.17
  110.9 3.4 %collective-permute-done.17 = f32[16,256]{1,0:T(8,128)S(1)} collective-permute-done((f32[16,256]{1,0:T(8,128)S(1)}, f32[16,256]{1,0:T(8,128)S(1)}, u32[]{:S(2)}, u32[]{:S(2)}) %collective-permute-start.17) | collective-permute-done | bytes 16416 | tf_op jit(solution)/shard_map/ppermute | solution.py:332
  114.3 0.9 collective-permute-start.20
  115.3 3.5 %collective-permute-start.19 = (f32[16,256]{1,0:T(8,128)S(1)}, f32[16,256]{1,0:T(8,128)S(1)}, u32[]{:S(2)}, u32[]{:S(2)}) collective-permute-start(f32[16,256]{1,0:T(8,128)S(1)} %add.37), channel_id=1, source_target_pairs={{0,6},{1,7},{2,4},{3,5},{4,2},{5,3},{6,0},{7,1},{8,14},{9,15},{10,... | collective-permute-start | bytes 49160 | tf_op jit(solution)/shard_map/ppermute | solution.py:332
  118.7 2.1 %collective-permute-start.18 = (f32[16,256]{1,0:T(8,128)S(1)}, f32[16,256]{1,0:T(8,128)S(1)}, u32[]{:S(2)}, u32[]{:S(2)}) collective-permute-start(f32[16,256]{1,0:T(8,128)S(1)} %add.37), channel_id=1, source_target_pairs={{0,2},{1,3},{2,0},{3,1},{4,6},{5,7},{6,4},{7,5},{8,10},{9,11},{10,... | collective-permute-start | bytes 49160 | tf_op jit(solution)/shard_map/ppermute | solution.py:332
  120.8 1.1 collective-permute-done.20
  122.0 1.4 collective-permute-done.18
  123.4 1.8 %all-to-all-done.3.grads = f32[4,512,256]{2,1,0:T(8,128)S(1)} async-done(((f32[4,512,256]{2,1,0:T(8,128)}), f32[4,512,256]{2,1,0:T(8,128)S(1)}, u32[]{:S(2)}, u32[]{:S(2)}) %all-to-all-start.3) | async-done | bytes 2097184 | tf_op jit(solution)/shard_map/all_to_all | solution.py:320
  125.2 0.9 gather.1
  126.0 4.2 %all-to-all-start.4 = ((f32[8,64,256]{2,1,0:T(8,128)}), f32[8,64,256]{2,1,0:T(8,128)S(1)}, u32[]{:S(2)}, u32[]{:S(2)}) async-start(f32[8,64,256]{2,1,0:T(8,128)} %bitcast.3), calls=%async_computation.4 | async-start | bytes 1048576 | tf_op jit(solution)/shard_map/all_to_all | solution.py:320
  130.2 1.2 collective-permute-done.21
  131.4 2.1 %collective-permute-start.23 = (f32[32,256]{1,0:T(8,128)S(1)}, f32[32,256]{1,0:T(8,128)S(1)}, u32[]{:S(2)}, u32[]{:S(2)}) collective-permute-start(f32[32,256]{1,0:T(8,128)S(1)} %pad_maximum_fusion), channel_id=1, source_target_pairs={{0,192},{64,128},{128,64},{192,0},{1,193},{65,129},{129,65},{193,1... | collective-permute-start | bytes 98312 | tf_op jit(solution)/shard_map/ppermute | solution.py:332
  133.5 0.6 collective-permute-start.24
  134.1 1.4 collective-permute-start.22
  135.5 1.0 collective-permute-done.23
  136.5 2.3 %collective-permute-done.24 = f32[32,256]{1,0:T(8,128)S(1)} collective-permute-done((f32[32,256]{1,0:T(8,128)S(1)}, f32[32,256]{1,0:T(8,128)S(1)}, u32[]{:S(2)}, u32[]{:S(2)}) %collective-permute-start.24) | collective-permute-done | bytes 32800 | tf_op jit(solution)/shard_map/ppermute | solution.py:332
  138.9 2.5 %collective-permute-start.27 = (f32[32,256]{1,0:T(8,128)S(1)}, f32[32,256]{1,0:T(8,128)S(1)}, u32[]{:S(2)}, u32[]{:S(2)}) collective-permute-start(f32[32,256]{1,0:T(8,128)S(1)} %add_add_fusion.mixed_a), channel_id=1, source_target_pairs={{0,16},{8,24},{16,0},{24,8},{1,17},{9,25},{17,1},{25,9},{2,18},{10... | collective-permute-start | bytes 98312 | tf_op jit(solution)/shard_map/ppermute | solution.py:332
  141.4 1.2 collective-permute-start.26
  142.6 1.9 %collective-permute-done.27.mixed_d = f32[32,256]{1,0:T(8,128)S(1)} collective-permute-done((f32[32,256]{1,0:T(8,128)S(1)}, f32[32,256]{1,0:T(8,128)S(1)}, u32[]{:S(2)}, u32[]{:S(2)}) %collective-permute-start.27) | collective-permute-done | bytes 32800 | tf_op jit(solution)/shard_map/ppermute | solution.py:332
  144.5 2.0 %collective-permute-done.26.mixed_c = f32[32,256]{1,0:T(8,128)S(1)} collective-permute-done((f32[32,256]{1,0:T(8,128)S(1)}, f32[32,256]{1,0:T(8,128)S(1)}, u32[]{:S(2)}, u32[]{:S(2)}) %collective-permute-start.26) | collective-permute-done | bytes 32800 | tf_op jit(solution)/shard_map/ppermute | solution.py:332
  146.6 2.6 %final.1 = f32[1024,256]{1,0:T(8,128)} custom-call(f32[32,256]{1,0:T(8,128)S(1)} %add_add_fusion.mixed_a, f32[32,256]{1,0:T(8,128)S(1)} %collective-permute-done.25.mixed_b, f32[32,256]{1,0:T(8,128)S(1)} %collective-permute-done.26.mixed_c, f32[32,256]{1,0:T(8,128)S(1)} %collective-permute-done.27.mixed_d, f32[32,256]{1,0:T(8,128)S(1)} %get-tuple-element.45.basis_t, ...), custom_call_target="tpu_custom_call" | custom-call | tf_op jit(solution)/shard_map/final/pallas_call | solution.py:439
  149.2 0.7 reduce_sum.9
  (22 shorter events, 0.1 us)
Async XLA Ops:
  4.5 1.3 collective-permute-start
  5.8 7.8 %collective-permute-start.3 = (f32[8,128]{1,0:T(8,128)S(1)}, f32[8,128]{1,0:T(8,128)S(1)}, u32[]{:S(2)}, u32[]{:S(2)}) collective-permute-start(f32[8,128]{1,0:T(8,128)S(1)} %add.33.after.a), channel_id=1, source_target_pairs={{0,128},{64,192},{128,0},{192,64},{1,129},{65,193},{129,1},{193,65... | collective-permute-start | bytes 12296 | tf_op jit(solution)/shard_map/ppermute | solution.py:332
  8.8 4.8 %collective-permute-start.2 = (f32[8,128]{1,0:T(8,128)S(1)}, f32[8,128]{1,0:T(8,128)S(1)}, u32[]{:S(2)}, u32[]{:S(2)}) collective-permute-start(f32[8,128]{1,0:T(8,128)S(1)} %add.33.after.a), channel_id=1, source_target_pairs={{0,192},{64,128},{128,64},{192,0},{1,193},{65,129},{129,65},{193,1... | collective-permute-start | bytes 12296 | tf_op jit(solution)/shard_map/ppermute | solution.py:332
  9.9 3.7 %collective-permute-start.1 = (f32[8,128]{1,0:T(8,128)S(1)}, f32[8,128]{1,0:T(8,128)S(1)}, u32[]{:S(2)}, u32[]{:S(2)}) collective-permute-start(f32[8,128]{1,0:T(8,128)S(1)} %add.33.after.a), channel_id=1, source_target_pairs={{0,64},{64,0},{128,192},{192,128},{1,65},{65,1},{129,193},{193,129... | collective-permute-start | bytes 12296 | tf_op jit(solution)/shard_map/ppermute | solution.py:332
  38.5 1.3 collective-permute-start.4
  39.8 8.0 %collective-permute-start.7 = (f32[8,128]{1,0:T(8,128)S(1)}, f32[8,128]{1,0:T(8,128)S(1)}, u32[]{:S(2)}, u32[]{:S(2)}) collective-permute-start(f32[8,128]{1,0:T(8,128)S(1)} %add.34.after.a), channel_id=1, source_target_pairs={{0,128},{64,192},{128,0},{192,64},{1,129},{65,193},{129,1},{193,65... | collective-permute-start | bytes 12296 | tf_op jit(solution)/shard_map/ppermute | solution.py:332
  43.1 4.8 %collective-permute-start.6 = (f32[8,128]{1,0:T(8,128)S(1)}, f32[8,128]{1,0:T(8,128)S(1)}, u32[]{:S(2)}, u32[]{:S(2)}) collective-permute-start(f32[8,128]{1,0:T(8,128)S(1)} %add.34.after.a), channel_id=1, source_target_pairs={{0,192},{64,128},{128,64},{192,0},{1,193},{65,129},{129,65},{193,1... | collective-permute-start | bytes 12296 | tf_op jit(solution)/shard_map/ppermute | solution.py:332
  44.2 3.7 %collective-permute-start.5 = (f32[8,128]{1,0:T(8,128)S(1)}, f32[8,128]{1,0:T(8,128)S(1)}, u32[]{:S(2)}, u32[]{:S(2)}) collective-permute-start(f32[8,128]{1,0:T(8,128)S(1)} %add.34.after.a), channel_id=1, source_target_pairs={{0,64},{64,0},{128,192},{192,128},{1,65},{65,1},{129,193},{193,129... | collective-permute-start | bytes 12296 | tf_op jit(solution)/shard_map/ppermute | solution.py:332
  66.0 1.3 collective-permute-start.8
  67.3 5.1 %collective-permute-start.11 = (f32[8,128]{1,0:T(8,128)S(1)}, f32[8,128]{1,0:T(8,128)S(1)}, u32[]{:S(2)}, u32[]{:S(2)}) collective-permute-start(f32[8,128]{1,0:T(8,128)S(1)} %add.35.a), channel_id=1, source_target_pairs={{0,128},{64,192},{128,0},{192,64},{1,129},{65,193},{129,1},{193,65... | collective-permute-start | bytes 12296 | tf_op jit(solution)/shard_map/ppermute | solution.py:332
  70.6 4.8 %collective-permute-start.10 = (f32[8,128]{1,0:T(8,128)S(1)}, f32[8,128]{1,0:T(8,128)S(1)}, u32[]{:S(2)}, u32[]{:S(2)}) collective-permute-start(f32[8,128]{1,0:T(8,128)S(1)} %add.35.a), channel_id=1, source_target_pairs={{0,192},{64,128},{128,64},{192,0},{1,193},{65,129},{129,65},{193,1... | collective-permute-start | bytes 12296 | tf_op jit(solution)/shard_map/ppermute | solution.py:332
  71.7 3.7 %collective-permute-start.9 = (f32[8,128]{1,0:T(8,128)S(1)}, f32[8,128]{1,0:T(8,128)S(1)}, u32[]{:S(2)}, u32[]{:S(2)}) collective-permute-start(f32[8,128]{1,0:T(8,128)S(1)} %add.35.a), channel_id=1, source_target_pairs={{0,64},{64,0},{128,192},{192,128},{1,65},{65,1},{129,193},{193,129... | collective-permute-start | bytes 12296 | tf_op jit(solution)/shard_map/ppermute | solution.py:332
  97.7 27.5 %all-to-all-start.3 = ((f32[4,512,256]{2,1,0:T(8,128)}), f32[4,512,256]{2,1,0:T(8,128)S(1)}, u32[]{:S(2)}, u32[]{:S(2)}) async-start(f32[4,512,256]{2,1,0:T(8,128)} %bitcast.4), calls=%async_computation.3 | async-start | bytes 4194304 | tf_op jit(solution)/shard_map/all_to_all | solution.py:320
  101.3 1.3 collective-permute-start.12
  102.7 7.5 %collective-permute-start.16 = (f32[256,1024]{1,0:T(8,128)S(1)}, f32[256,1024]{1,0:T(8,128)S(1)}, u32[]{:S(2)}, u32[]{:S(2)}) collective-permute-start(f32[256,1024]{1,0:T(8,128)S(1)} %get-tuple-element.51.part_t), channel_id=1, source_target_pairs={{0,32},{32,0},{1,33},{33,1},{2,34},{34,2},{3,35},{35,3},{4,36},{36... | collective-permute-start | bytes 3145736 | tf_op jit(solution)/shard_map/ppermute | solution.py:332
  102.9 5.9 %collective-permute-start.15 = (f32[16,1024]{1,0:T(8,128)S(1)}, f32[16,1024]{1,0:T(8,128)S(1)}, u32[]{:S(2)}, u32[]{:S(2)}) collective-permute-start(f32[16,1024]{1,0:T(8,128)S(1)} %add.36.a), channel_id=1, source_target_pairs={{0,128},{64,192},{128,0},{192,64},{1,129},{65,193},{129,1},{193,65... | collective-permute-start | bytes 196616 | tf_op jit(solution)/shard_map/ppermute | solution.py:332
  104.6 5.6 %collective-permute-start.14 = (f32[16,1024]{1,0:T(8,128)S(1)}, f32[16,1024]{1,0:T(8,128)S(1)}, u32[]{:S(2)}, u32[]{:S(2)}) collective-permute-start(f32[16,1024]{1,0:T(8,128)S(1)} %add.36.a), channel_id=1, source_target_pairs={{0,192},{64,128},{128,64},{192,0},{1,193},{65,129},{129,65},{193,1... | collective-permute-start | bytes 196616 | tf_op jit(solution)/shard_map/ppermute | solution.py:332
  105.7 4.5 %collective-permute-start.13 = (f32[16,1024]{1,0:T(8,128)S(1)}, f32[16,1024]{1,0:T(8,128)S(1)}, u32[]{:S(2)}, u32[]{:S(2)}) collective-permute-start(f32[16,1024]{1,0:T(8,128)S(1)} %add.36.a), channel_id=1, source_target_pairs={{0,64},{64,0},{128,192},{192,128},{1,65},{65,1},{129,193},{193,129... | collective-permute-start | bytes 196616 | tf_op jit(solution)/shard_map/ppermute | solution.py:332
  110.6 3.8 %collective-permute-start.17 = (f32[16,256]{1,0:T(8,128)S(1)}, f32[16,256]{1,0:T(8,128)S(1)}, u32[]{:S(2)}, u32[]{:S(2)}) collective-permute-start(f32[16,256]{1,0:T(8,128)S(1)} %get-tuple-element.52), channel_id=1, source_target_pairs={{0,1},{1,0},{2,3},{3,2},{4,5},{5,4},{6,7},{7,6},{8,9},{9,8},{10,11... | collective-permute-start | bytes 49160 | tf_op jit(solution)/shard_map/ppermute | solution.py:332
  114.3 7.6 %collective-permute-start.20 = (f32[16,256]{1,0:T(8,128)S(1)}, f32[16,256]{1,0:T(8,128)S(1)}, u32[]{:S(2)}, u32[]{:S(2)}) collective-permute-start(f32[16,256]{1,0:T(8,128)S(1)} %add.37), channel_id=1, source_target_pairs={{0,4},{1,5},{2,6},{3,7},{4,0},{5,1},{6,2},{7,3},{8,12},{9,13},{10,... | collective-permute-start | bytes 49160 | tf_op jit(solution)/shard_map/ppermute | solution.py:332
  115.3 6.7 %collective-permute-start.19 = (f32[16,256]{1,0:T(8,128)S(1)}, f32[16,256]{1,0:T(8,128)S(1)}, u32[]{:S(2)}, u32[]{:S(2)}) collective-permute-start(f32[16,256]{1,0:T(8,128)S(1)} %add.37), channel_id=1, source_target_pairs={{0,6},{1,7},{2,4},{3,5},{4,2},{5,3},{6,0},{7,1},{8,14},{9,15},{10,... | collective-permute-start | bytes 49160 | tf_op jit(solution)/shard_map/ppermute | solution.py:332
  118.7 4.6 %collective-permute-start.18 = (f32[16,256]{1,0:T(8,128)S(1)}, f32[16,256]{1,0:T(8,128)S(1)}, u32[]{:S(2)}, u32[]{:S(2)}) collective-permute-start(f32[16,256]{1,0:T(8,128)S(1)} %add.37), channel_id=1, source_target_pairs={{0,2},{1,3},{2,0},{3,1},{4,6},{5,7},{6,4},{7,5},{8,10},{9,11},{10,... | collective-permute-start | bytes 49160 | tf_op jit(solution)/shard_map/ppermute | solution.py:332
  126.0 23.1 %all-to-all-start.4 = ((f32[8,64,256]{2,1,0:T(8,128)}), f32[8,64,256]{2,1,0:T(8,128)S(1)}, u32[]{:S(2)}, u32[]{:S(2)}) async-start(f32[8,64,256]{2,1,0:T(8,128)} %bitcast.3), calls=%async_computation.4 | async-start | bytes 1048576 | tf_op jit(solution)/shard_map/all_to_all | solution.py:320
  130.2 1.2 collective-permute-start.21
  131.4 5.1 %collective-permute-start.23 = (f32[32,256]{1,0:T(8,128)S(1)}, f32[32,256]{1,0:T(8,128)S(1)}, u32[]{:S(2)}, u32[]{:S(2)}) collective-permute-start(f32[32,256]{1,0:T(8,128)S(1)} %pad_maximum_fusion), channel_id=1, source_target_pairs={{0,192},{64,128},{128,64},{192,0},{1,193},{65,129},{129,65},{193,1... | collective-permute-start | bytes 98312 | tf_op jit(solution)/shard_map/ppermute | solution.py:332
  133.5 5.4 %collective-permute-start.24 = (f32[32,256]{1,0:T(8,128)S(1)}, f32[32,256]{1,0:T(8,128)S(1)}, u32[]{:S(2)}, u32[]{:S(2)}) collective-permute-start(f32[32,256]{1,0:T(8,128)S(1)} %pad_maximum_fusion), channel_id=1, source_target_pairs={{0,128},{64,192},{128,0},{192,64},{1,129},{65,193},{129,1},{193,65... | collective-permute-start | bytes 98312 | tf_op jit(solution)/shard_map/ppermute | solution.py:332
  134.1 4.8 %collective-permute-start.22 = (f32[32,256]{1,0:T(8,128)S(1)}, f32[32,256]{1,0:T(8,128)S(1)}, u32[]{:S(2)}, u32[]{:S(2)}) collective-permute-start(f32[32,256]{1,0:T(8,128)S(1)} %pad_maximum_fusion), channel_id=1, source_target_pairs={{0,64},{64,0},{128,192},{192,128},{1,65},{65,1},{129,193},{193,129... | collective-permute-start | bytes 98312 | tf_op jit(solution)/shard_map/ppermute | solution.py:332
  135.5 7.1 %collective-permute-start.28 = (f32[16,1024]{1,0:T(8,128)S(1)}, f32[16,1024]{1,0:T(8,128)S(1)}, u32[]{:S(2)}, u32[]{:S(2)}) collective-permute-start(f32[16,1024]{1,0:T(8,128)S(1)} %get-tuple-element.53.factor_mine), channel_id=1, source_target_pairs={{0,32},{32,0},{1,33},{33,1},{2,34},{34,2},{3,35},{35,3},{4,36},{36... | collective-permute-start | bytes 196616 | tf_op jit(solution)/shard_map/ppermute | solution.py:332
  138.9 5.6 %collective-permute-start.27 = (f32[32,256]{1,0:T(8,128)S(1)}, f32[32,256]{1,0:T(8,128)S(1)}, u32[]{:S(2)}, u32[]{:S(2)}) collective-permute-start(f32[32,256]{1,0:T(8,128)S(1)} %add_add_fusion.mixed_a), channel_id=1, source_target_pairs={{0,16},{8,24},{16,0},{24,8},{1,17},{9,25},{17,1},{25,9},{2,18},{10... | collective-permute-start | bytes 98312 | tf_op jit(solution)/shard_map/ppermute | solution.py:332
  141.4 5.1 %collective-permute-start.26 = (f32[32,256]{1,0:T(8,128)S(1)}, f32[32,256]{1,0:T(8,128)S(1)}, u32[]{:S(2)}, u32[]{:S(2)}) collective-permute-start(f32[32,256]{1,0:T(8,128)S(1)} %add_add_fusion.mixed_a), channel_id=1, source_target_pairs={{0,24},{8,16},{16,8},{24,0},{1,25},{9,17},{17,9},{25,1},{2,26},{10... | collective-permute-start | bytes 98312 | tf_op jit(solution)/shard_map/ppermute | solution.py:332
  142.6 4.0 %collective-permute-start.25 = (f32[32,256]{1,0:T(8,128)S(1)}, f32[32,256]{1,0:T(8,128)S(1)}, u32[]{:S(2)}, u32[]{:S(2)}) collective-permute-start(f32[32,256]{1,0:T(8,128)S(1)} %add_add_fusion.mixed_a), channel_id=1, source_target_pairs={{0,8},{8,0},{16,24},{24,16},{1,9},{9,1},{17,25},{25,17},{2,10},{10... | collective-permute-start | bytes 98312 | tf_op jit(solution)/shard_map/ppermute | solution.py:332

commit v8 on v7

--- a/solution.py
+++ b/solution.py
@@ -196,12 +196,21 @@
         col_out[...] = result
 
 
-def gradient_kernel(ratio, like, upper, lower, factor, rows_in, like_scale, feat_t_a, feat_t_b, unit_proto, basis_t,
+def predict_kernel(like, total_scale, after, predicted):
+    for i in range(like.shape[0] // BLOCK):
+        here = slice(i * BLOCK, (i + 1) * BLOCK)
+        scale = down(total_scale[i])
+        for j in range(like.shape[1] // LANES):
+            square = like[here, tile(j)]
+            predicted[here, tile(j)] = square * lax.rsqrt(square) * scale
+
+
+def gradient_kernel(ratio, predicted, upper, lower, factor, rows_in, feat_t_a, feat_t_b, unit_proto, basis_t,
                     row_grad, part_t, factor_mine, factor_other, code_scale, gradient, grads, sent):
     code_scale[...] = (10.0 / jnp.sum(rows_in[...], axis=0)).reshape(code_scale.shape)
     mine = factor_mine.shape[0]
     basis = basis_t[...].astype(BF16)
-    rows, protos = like.shape
+    rows, protos = predicted.shape
     blocks = rows // BLOCK
 
     def copy(i):
@@ -212,11 +221,9 @@
         here = slice(i * BLOCK, (i + 1) * BLOCK)
         table = upper if i < blocks // 2 else lower
         there = slice((i % (blocks // 2)) * BLOCK, (i % (blocks // 2) + 1) * BLOCK)
-        first = down(like_scale[i])
         second = down(code_scale[i])
         for j in range(protos // LANES):
-            square = like[here, tile(j)]
-            value = square * lax.rsqrt(square) * first - table[there, tile(j)] * factor[j:j + 1, :] * second
+            value = predicted[here, tile(j)] - table[there, tile(j)] * factor[j:j + 1, :] * second
             gradient[here, tile(j)] = value.astype(BF16)
         grads[here, :] = dot16(gradient[here, :], unit_proto[...], nn)
         copy(i).start()
@@ -397,11 +404,15 @@
     cols = fours(cols, "x")
     row_sums = exchange(row_step(cols, piece, lower), proto)
     cols, like_scale = column_step(True, row_sums, shape(col_tiles, LANES), shape(*per_block))
-    cols = fours(sum_core(cols), "x")
+    cols = sum_core(cols)
+    predicted = call(
+        predict_kernel, kept(rows, protos), name="predict", ins=(V, V, A), flops=rows * protos * feat
+    )(stay(like), like_scale, cols)
+    cols = fours(cols, "x")
     row_sums, factor = call(
         last_row_kernel, (shape(tall, row_tiles, LANES), shape(col_tiles, LANES)), row_scratch,
         name="rows", ins=(V,) * 6 + (A,),
-    )(*cols, stay(upper), stay(lower), stay(like))
+    )(*cols, stay(upper), stay(lower), stay(predicted))
     row_sums = exchange(row_sums, proto)
 
     mine = rank // 2
@@ -415,9 +426,9 @@
         ),
         row_scratch
         + (V((rows, protos), BF16), V((rows, feat), F32), pltpu.SemaphoreType.DMA((blocks,))),
-        name="gradient", ins=(V,) * 10, out_specs=(H, V, V, V),
+        name="gradient", ins=(V,) * 9, out_specs=(H, V, V, V),
     )(
-        stay(like), stay(upper), stay(lower), factor, row_sums, like_scale, feat_t_a, feat_t_b, unit_proto,
+        stay(predicted), stay(upper), stay(lower), factor, row_sums, feat_t_a, feat_t_b, unit_proto,
         basis_t,
     )
     factor_mine, part_t = lax.optimization_barrier((factor_mine + swap(factor_other, "c", 1), part_t))

time: 150 us -> 152 us (1.013)
  local copies, waits for them, and re-layouts: 0 us -> 2.19 us
    unnamed x0 -> x4, local copies, waits for them, and re-layouts: none -> 2.19 us
  transfers between devices with their start and end apart: 31 -> 31, of which waited for: 18 -> 16; matrix products, arithmetic and copies ran while one was open for 0% -> 0% of each run, Pallas kernels for 7% -> 8%
where the time goes in v8:
time: 152 us; the launch traced here: 151 us
  blocking collectives  55.9 us (37%)
  starting transfers between devices  39.5 us (26%)
  waiting for transfers between devices  27.4 us (18%)
  Pallas kernels  24.9 us (16%)
  local copies, waits for them, and re-layouts  2.19 us (1%)
    all_to_all x3, blocking collectives, exchange(): return lax.all_to_all(value, axes, 0, 0)  55.9 us
    ppermute x26, starting transfers between devices, swap(): lax.ppermute(value, axis, [(i, i ^ mask) for i in range(lax.axis_size(axi...  31.5 us
    ppermute x26, waiting for transfers between devices, swap(): lax.ppermute(value, axis, [(i, i ^ mask) for i in range(lax.axis_size(axi...  22.1 us
    all_to_all x2, starting transfers between devices, exchange(): return lax.all_to_all(value, axes, 0, 0)  7.79 us
    pallas_call x2, Pallas kernels, sibling_half(): call(functools.partial(sibling_kernel, first), (kept(half, protos), shape...  7.23 us
    pallas_call x1, Pallas kernels, on_device(): call(functools.partial(gradient_kernel, ratio), (pltpu.HBM((rows, feat),...  5.34 us
    pallas_call x1, Pallas kernels, on_device(): call(scores_kernel, (shape(rows, feat, dtype=BF16), shape(protos, feat, d...  3.86 us
    ppermute x3, waiting for transfers between devices, sum_core(): return value + lax.ppermute(value, 'c', [(0, 1), (1, 0)])  3.46 us
  transfers between devices with their start and end apart: 31, of which 16 were waited for; matrix products, arithmetic and copies ran while one was open for 0% of the time, Pallas kernels for 8%

profile of v8, /device:TPU:32, one launch (start us, length us, event | category | flops | bytes accessed | tf_op | source)
XLA Modules:
  0.0 151.4 jit_solution(13574508762185062189)
XLA Ops:
  0.6 3.9 %scores.1 = (bf16[2048,256]{1,0:T(8,128)(2,1)S(1)}, bf16[1024,256]{1,0:T(8,128)(2,1)S(1)}, f32[2048,1024]{1,0:T(8,128)S(1)}, f32[8,128]{1,0:T(8,128)S(1)}, f32[8...) custom-call(bf16[2048,256]{1,0:T(8,128)(2,1)} %feat_hbm.1, bf16[1024,256]{1,0:T(8,128)(2,1)} %proto_hbm.1, ...), custom_call_target="tpu_custom_call" | custom-call | tf_op jit(solution)/shard_map/scores/pallas_call | solution.py:360
  4.5 0.1 collective-permute-start
  4.6 1.2 collective-permute-done
  5.8 3.0 %collective-permute-start.3 = (f32[8,128]{1,0:T(8,128)S(1)}, f32[8,128]{1,0:T(8,128)S(1)}, u32[]{:S(2)}, u32[]{:S(2)}) collective-permute-start(f32[8,128]{1,0:T(8,128)S(1)} %add.33.after.a), channel_id=1, source_target_pairs={{0,128},{64,192},{128,0},{192,64},{1,129},{65,193},{129,1},{193,65... | collective-permute-start | bytes 12296 | tf_op jit(solution)/shard_map/ppermute | solution.py:339
  8.8 1.1 collective-permute-start.2
  9.9 0.0 collective-permute-start.1
  9.9 3.6 %sibling.2 = (f32[1024,1024]{1,0:T(8,128)S(1)}, bf16[256,1024]{1,0:T(8,128)(2,1)S(1)}, f32[32,256]{1,0:T(8,128)S(1)}) custom-call(bf16[2048,256]{1,0:T(8,128)(2,1)S(1)} %get-tuple-element.31.unit_feat, bf16[1024,256]{1,0:T(8,128)(2,1)S(1)} %get-tuple-element.32.unit_proto, s32[16,128]{1,0:T(8,128)S(1)} %get-tuple-element.33.sibling, ...), custom_call_target="tpu_custom_call" | custom-call | flops 2147483648 | tf_op jit(solution)/shard_map/sibling/pallas_call | solution.py:381
  13.6 0.0 collective-permute-done.2.c
  13.6 0.7 rows.3
  14.3 23.5 %all_to_all.25.rows_in = f32[32,1,2176]{2,1,0:T(1,128)S(1)} all-to-all(f32[32,1,2176]{2,1,0:T(1,128)S(1)} %rows.3), channel_id=1, replica_groups=mesh['x'=4,'c'=2,'y'=4,'z'=8] {'y','z'}, dimensions={0} | all-to-all | bytes 557056 | tf_op jit(solution)/shard_map/all_to_all | solution.py:327
  37.8 0.8 columns.2
  38.6 0.1 collective-permute-start.4
  38.7 1.2 collective-permute-done.4
  39.8 3.3 %collective-permute-start.7 = (f32[8,128]{1,0:T(8,128)S(1)}, f32[8,128]{1,0:T(8,128)S(1)}, u32[]{:S(2)}, u32[]{:S(2)}) collective-permute-start(f32[8,128]{1,0:T(8,128)S(1)} %add.34.after.a), channel_id=1, source_target_pairs={{0,128},{64,192},{128,0},{192,64},{1,129},{65,193},{129,1},{193,65... | collective-permute-start | bytes 12296 | tf_op jit(solution)/shard_map/ppermute | solution.py:339
  43.1 1.1 collective-permute-start.6
  44.2 0.0 collective-permute-start.5
  44.2 3.6 %sibling.3 = (f32[1024,1024]{1,0:T(8,128)S(1)}, bf16[256,1024]{1,0:T(8,128)(2,1)S(1)}) custom-call(bf16[2048,256]{1,0:T(8,128)(2,1)S(1)} %get-tuple-element.31.unit_feat, bf16[1024,256]{1,0:T(8,128)(2,1)S(1)} %get-tuple-element.32.unit_proto, s32[16,128]{1,0:T(8,128)S(1)} %get-tuple-element.33.sibling, s32[32,256]{1,0:T(8,128)S(1)} %get-tuple-element.34.seed_t, ...), custom_call_target="tpu_custom_call" | custom-call | flops 2147483648 | tf_op jit(solution)/shard_map/sibling/pallas_call | solution.py:381
  47.9 0.0 collective-permute-done.6.c
  47.9 0.6 rows.4
  48.6 16.8 %all_to_all.26.rows_in = f32[32,1,2176]{2,1,0:T(1,128)S(1)} all-to-all(f32[32,1,2176]{2,1,0:T(1,128)S(1)} %rows.4), channel_id=1, replica_groups=mesh['x'=4,'c'=2,'y'=4,'z'=8] {'y','z'}, dimensions={0} | all-to-all | bytes 557056 | tf_op jit(solution)/shard_map/all_to_all | solution.py:327
  65.3 0.7 columns.3
  66.1 0.1 collective-permute-start.8
  66.2 1.2 collective-permute-done.8
  67.3 3.3 %collective-permute-start.11 = (f32[8,128]{1,0:T(8,128)S(1)}, f32[8,128]{1,0:T(8,128)S(1)}, u32[]{:S(2)}, u32[]{:S(2)}) collective-permute-start(f32[8,128]{1,0:T(8,128)S(1)} %add.35.after.a), channel_id=1, source_target_pairs={{0,128},{64,192},{128,0},{192,64},{1,129},{65,193},{129,1},{193,65... | collective-permute-start | bytes 12296 | tf_op jit(solution)/shard_map/ppermute | solution.py:339
  70.6 1.1 collective-permute-start.10
  71.7 0.0 collective-permute-start.9
  71.7 1.1 predict.1.like.predicted
  72.9 2.5 %collective-permute-done.10.c = f32[8,128]{1,0:T(8,128)S(1)} collective-permute-done((f32[8,128]{1,0:T(8,128)S(1)}, f32[8,128]{1,0:T(8,128)S(1)}, u32[]{:S(2)}, u32[]{:S(2)}) %collective-permute-start.10) | collective-permute-done | bytes 4128 | tf_op jit(solution)/shard_map/ppermute | solution.py:339
  75.4 0.7 rows.5
  76.1 15.6 %all_to_all.27.rows_in = f32[32,16,128]{2,1,0:T(8,128)S(1)} all-to-all(f32[32,16,128]{2,1,0:T(8,128)S(1)} %get-tuple-element.42), channel_id=1, replica_groups=mesh['x'=4,'c'=2,'y'=4,'z'=8] {'y','z'}, dimensions={0} | all-to-all | bytes 524288 | tf_op jit(solution)/shard_map/all_to_all | solution.py:327
  91.7 2.2 %copy-done.1 = f32[1024,1024]{1,0:T(8,128)S(1)} copy-done((f32[1024,1024]{1,0:T(8,128)S(1)}, f32[1024,1024]{1,0:T(8,128)}, u32[]{:S(2)}) %copy-start.1) | copy-done | bytes 4194328
  93.8 5.3 %gradient.1 = (f32[2048,256]{1,0:T(8,128)}, f32[256,1024]{1,0:T(8,128)S(1)}, f32[16,1024]{1,0:T(8,128)S(1)}, f32[16,1024]{1,0:T(8,128)S(1)}) custom-call(f32[2048,1024]{1,0:T(8,128)S(1)} %predict.1.like.predicted, f32[1024,1024]{1,0:T(8,128)S(1)} %copy-done.1, f32[1024,1024]{1,0:T(8,128)S(1)} %get-tuple-element.38.later.lower, ...), custom_call_target="tpu_custom_call" | custom-call | tf_op jit(solution)/shard_map/gradient/pallas_call | solution.py:419
  99.2 3.6 %all-to-all-start.3 = ((f32[4,512,256]{2,1,0:T(8,128)}), f32[4,512,256]{2,1,0:T(8,128)S(1)}, u32[]{:S(2)}, u32[]{:S(2)}) async-start(f32[4,512,256]{2,1,0:T(8,128)} %bitcast.4), calls=%async_computation.3 | async-start | bytes 4194304 | tf_op jit(solution)/shard_map/all_to_all | solution.py:327
  102.8 0.1 collective-permute-start.12
  102.9 1.2 collective-permute-done.12
  104.2 0.2 collective-permute-start.16
  104.4 1.7 %collective-permute-start.15 = (f32[16,1024]{1,0:T(8,128)S(1)}, f32[16,1024]{1,0:T(8,128)S(1)}, u32[]{:S(2)}, u32[]{:S(2)}) collective-permute-start(f32[16,1024]{1,0:T(8,128)S(1)} %add.36.a), channel_id=1, source_target_pairs={{0,128},{64,192},{128,0},{192,64},{1,129},{65,193},{129,1},{193,65... | collective-permute-start | bytes 196616 | tf_op jit(solution)/shard_map/ppermute | solution.py:339
  106.1 1.1 collective-permute-start.14
  107.2 0.7 collective-permute-start.13
  107.9 2.4 %collective-permute-done.15.d = f32[16,1024]{1,0:T(8,128)S(1)} collective-permute-done((f32[16,1024]{1,0:T(8,128)S(1)}, f32[16,1024]{1,0:T(8,128)S(1)}, u32[]{:S(2)}, u32[]{:S(2)}) %collective-permute-start.15) | collective-permute-done | bytes 65568 | tf_op jit(solution)/shard_map/ppermute | solution.py:339
  110.3 1.4 collective-permute-done.14.c
  111.7 0.4 mixed.1
  112.1 0.3 collective-permute-start.17
  112.4 3.4 %collective-permute-done.17 = f32[16,256]{1,0:T(8,128)S(1)} collective-permute-done((f32[16,256]{1,0:T(8,128)S(1)}, f32[16,256]{1,0:T(8,128)S(1)}, u32[]{:S(2)}, u32[]{:S(2)}) %collective-permute-start.17) | collective-permute-done | bytes 16416 | tf_op jit(solution)/shard_map/ppermute | solution.py:339
  115.8 0.9 collective-permute-start.20
  116.8 3.5 %collective-permute-start.19 = (f32[16,256]{1,0:T(8,128)S(1)}, f32[16,256]{1,0:T(8,128)S(1)}, u32[]{:S(2)}, u32[]{:S(2)}) collective-permute-start(f32[16,256]{1,0:T(8,128)S(1)} %add.37), channel_id=1, source_target_pairs={{0,6},{1,7},{2,4},{3,5},{4,2},{5,3},{6,0},{7,1},{8,14},{9,15},{10,... | collective-permute-start | bytes 49160 | tf_op jit(solution)/shard_map/ppermute | solution.py:339
  120.2 2.1 %collective-permute-start.18 = (f32[16,256]{1,0:T(8,128)S(1)}, f32[16,256]{1,0:T(8,128)S(1)}, u32[]{:S(2)}, u32[]{:S(2)}) collective-permute-start(f32[16,256]{1,0:T(8,128)S(1)} %add.37), channel_id=1, source_target_pairs={{0,2},{1,3},{2,0},{3,1},{4,6},{5,7},{6,4},{7,5},{8,10},{9,11},{10,... | collective-permute-start | bytes 49160 | tf_op jit(solution)/shard_map/ppermute | solution.py:339
  122.3 1.1 collective-permute-done.20
  123.5 1.4 collective-permute-done.18
  124.9 1.8 %all-to-all-done.3.grads = f32[4,512,256]{2,1,0:T(8,128)S(1)} async-done(((f32[4,512,256]{2,1,0:T(8,128)}), f32[4,512,256]{2,1,0:T(8,128)S(1)}, u32[]{:S(2)}, u32[]{:S(2)}) %all-to-all-start.3) | async-done | bytes 2097184 | tf_op jit(solution)/shard_map/all_to_all | solution.py:327
  126.7 0.9 gather.1
  127.6 4.2 %all-to-all-start.4 = ((f32[8,64,256]{2,1,0:T(8,128)}), f32[8,64,256]{2,1,0:T(8,128)S(1)}, u32[]{:S(2)}, u32[]{:S(2)}) async-start(f32[8,64,256]{2,1,0:T(8,128)} %bitcast.3), calls=%async_computation.4 | async-start | bytes 1048576 | tf_op jit(solution)/shard_map/all_to_all | solution.py:327
  131.7 1.2 collective-permute-done.21
  132.9 2.1 %collective-permute-start.23 = (f32[32,256]{1,0:T(8,128)S(1)}, f32[32,256]{1,0:T(8,128)S(1)}, u32[]{:S(2)}, u32[]{:S(2)}) collective-permute-start(f32[32,256]{1,0:T(8,128)S(1)} %pad_maximum_fusion), channel_id=1, source_target_pairs={{0,192},{64,128},{128,64},{192,0},{1,193},{65,129},{129,65},{193,1... | collective-permute-start | bytes 98312 | tf_op jit(solution)/shard_map/ppermute | solution.py:339
  135.0 0.6 collective-permute-start.24
  135.6 1.4 collective-permute-start.22
  137.0 1.0 collective-permute-done.23
  138.0 2.3 %collective-permute-done.24 = f32[32,256]{1,0:T(8,128)S(1)} collective-permute-done((f32[32,256]{1,0:T(8,128)S(1)}, f32[32,256]{1,0:T(8,128)S(1)}, u32[]{:S(2)}, u32[]{:S(2)}) %collective-permute-start.24) | collective-permute-done | bytes 32800 | tf_op jit(solution)/shard_map/ppermute | solution.py:339
  140.4 2.5 %collective-permute-start.27 = (f32[32,256]{1,0:T(8,128)S(1)}, f32[32,256]{1,0:T(8,128)S(1)}, u32[]{:S(2)}, u32[]{:S(2)}) collective-permute-start(f32[32,256]{1,0:T(8,128)S(1)} %add_add_fusion.mixed_a), channel_id=1, source_target_pairs={{0,16},{8,24},{16,0},{24,8},{1,17},{9,25},{17,1},{25,9},{2,18},{10... | collective-permute-start | bytes 98312 | tf_op jit(solution)/shard_map/ppermute | solution.py:339
  142.9 1.2 collective-permute-start.26
  144.1 1.9 %collective-permute-done.27.mixed_d = f32[32,256]{1,0:T(8,128)S(1)} collective-permute-done((f32[32,256]{1,0:T(8,128)S(1)}, f32[32,256]{1,0:T(8,128)S(1)}, u32[]{:S(2)}, u32[]{:S(2)}) %collective-permute-start.27) | collective-permute-done | bytes 32800 | tf_op jit(solution)/shard_map/ppermute | solution.py:339
  146.0 2.1 %collective-permute-done.26.mixed_c = f32[32,256]{1,0:T(8,128)S(1)} collective-permute-done((f32[32,256]{1,0:T(8,128)S(1)}, f32[32,256]{1,0:T(8,128)S(1)}, u32[]{:S(2)}, u32[]{:S(2)}) %collective-permute-start.26) | collective-permute-done | bytes 32800 | tf_op jit(solution)/shard_map/ppermute | solution.py:339
  148.1 2.6 %final.1 = f32[1024,256]{1,0:T(8,128)} custom-call(f32[32,256]{1,0:T(8,128)S(1)} %add_add_fusion.mixed_a, f32[32,256]{1,0:T(8,128)S(1)} %collective-permute-done.25.mixed_b, f32[32,256]{1,0:T(8,128)S(1)} %collective-permute-done.26.mixed_c, f32[32,256]{1,0:T(8,128)S(1)} %collective-permute-done.27.mixed_d, f32[32,256]{1,0:T(8,128)S(1)} %get-tuple-element.45.basis_t, ...), custom_call_target="tpu_custom_call" | custom-call | tf_op jit(solution)/shard_map/final/pallas_call | solution.py:450
  150.7 0.7 reduce_sum.9
  (27 shorter events, 0.1 us)
Async XLA Ops:
  4.5 1.3 collective-permute-start
  5.8 7.8 %collective-permute-start.3 = (f32[8,128]{1,0:T(8,128)S(1)}, f32[8,128]{1,0:T(8,128)S(1)}, u32[]{:S(2)}, u32[]{:S(2)}) collective-permute-start(f32[8,128]{1,0:T(8,128)S(1)} %add.33.after.a), channel_id=1, source_target_pairs={{0,128},{64,192},{128,0},{192,64},{1,129},{65,193},{129,1},{193,65... | collective-permute-start | bytes 12296 | tf_op jit(solution)/shard_map/ppermute | solution.py:339
  8.8 4.8 %collective-permute-start.2 = (f32[8,128]{1,0:T(8,128)S(1)}, f32[8,128]{1,0:T(8,128)S(1)}, u32[]{:S(2)}, u32[]{:S(2)}) collective-permute-start(f32[8,128]{1,0:T(8,128)S(1)} %add.33.after.a), channel_id=1, source_target_pairs={{0,192},{64,128},{128,64},{192,0},{1,193},{65,129},{129,65},{193,1... | collective-permute-start | bytes 12296 | tf_op jit(solution)/shard_map/ppermute | solution.py:339
  9.9 3.7 %collective-permute-start.1 = (f32[8,128]{1,0:T(8,128)S(1)}, f32[8,128]{1,0:T(8,128)S(1)}, u32[]{:S(2)}, u32[]{:S(2)}) collective-permute-start(f32[8,128]{1,0:T(8,128)S(1)} %add.33.after.a), channel_id=1, source_target_pairs={{0,64},{64,0},{128,192},{192,128},{1,65},{65,1},{129,193},{193,129... | collective-permute-start | bytes 12296 | tf_op jit(solution)/shard_map/ppermute | solution.py:339
  13.5 61.9 %copy-start = (f32[1024,1024]{1,0:T(8,128)}, f32[1024,1024]{1,0:T(8,128)S(1)}, u32[]{:S(2)}) copy-start(f32[1024,1024]{1,0:T(8,128)S(1)} %get-tuple-element.35.later.upper) | copy-start | bytes 12582916
  38.6 1.3 collective-permute-start.4
  39.8 8.0 %collective-permute-start.7 = (f32[8,128]{1,0:T(8,128)S(1)}, f32[8,128]{1,0:T(8,128)S(1)}, u32[]{:S(2)}, u32[]{:S(2)}) collective-permute-start(f32[8,128]{1,0:T(8,128)S(1)} %add.34.after.a), channel_id=1, source_target_pairs={{0,128},{64,192},{128,0},{192,64},{1,129},{65,193},{129,1},{193,65... | collective-permute-start | bytes 12296 | tf_op jit(solution)/shard_map/ppermute | solution.py:339
  43.1 4.8 %collective-permute-start.6 = (f32[8,128]{1,0:T(8,128)S(1)}, f32[8,128]{1,0:T(8,128)S(1)}, u32[]{:S(2)}, u32[]{:S(2)}) collective-permute-start(f32[8,128]{1,0:T(8,128)S(1)} %add.34.after.a), channel_id=1, source_target_pairs={{0,192},{64,128},{128,64},{192,0},{1,193},{65,129},{129,65},{193,1... | collective-permute-start | bytes 12296 | tf_op jit(solution)/shard_map/ppermute | solution.py:339
  44.2 3.7 %collective-permute-start.5 = (f32[8,128]{1,0:T(8,128)S(1)}, f32[8,128]{1,0:T(8,128)S(1)}, u32[]{:S(2)}, u32[]{:S(2)}) collective-permute-start(f32[8,128]{1,0:T(8,128)S(1)} %add.34.after.a), channel_id=1, source_target_pairs={{0,64},{64,0},{128,192},{192,128},{1,65},{65,1},{129,193},{193,129... | collective-permute-start | bytes 12296 | tf_op jit(solution)/shard_map/ppermute | solution.py:339
  66.1 1.3 collective-permute-start.8
  67.3 5.6 %collective-permute-start.11 = (f32[8,128]{1,0:T(8,128)S(1)}, f32[8,128]{1,0:T(8,128)S(1)}, u32[]{:S(2)}, u32[]{:S(2)}) collective-permute-start(f32[8,128]{1,0:T(8,128)S(1)} %add.35.after.a), channel_id=1, source_target_pairs={{0,128},{64,192},{128,0},{192,64},{1,129},{65,193},{129,1},{193,65... | collective-permute-start | bytes 12296 | tf_op jit(solution)/shard_map/ppermute | solution.py:339
  70.6 4.8 %collective-permute-start.10 = (f32[8,128]{1,0:T(8,128)S(1)}, f32[8,128]{1,0:T(8,128)S(1)}, u32[]{:S(2)}, u32[]{:S(2)}) collective-permute-start(f32[8,128]{1,0:T(8,128)S(1)} %add.35.after.a), channel_id=1, source_target_pairs={{0,192},{64,128},{128,64},{192,0},{1,193},{65,129},{129,65},{193,1... | collective-permute-start | bytes 12296 | tf_op jit(solution)/shard_map/ppermute | solution.py:339
  71.7 3.7 %collective-permute-start.9 = (f32[8,128]{1,0:T(8,128)S(1)}, f32[8,128]{1,0:T(8,128)S(1)}, u32[]{:S(2)}, u32[]{:S(2)}) collective-permute-start(f32[8,128]{1,0:T(8,128)S(1)} %add.35.after.a), channel_id=1, source_target_pairs={{0,64},{64,0},{128,192},{192,128},{1,65},{65,1},{129,193},{193,129... | collective-permute-start | bytes 12296 | tf_op jit(solution)/shard_map/ppermute | solution.py:339
  91.7 2.2 %copy-start.1 = (f32[1024,1024]{1,0:T(8,128)S(1)}, f32[1024,1024]{1,0:T(8,128)}, u32[]{:S(2)}) copy-start(f32[1024,1024]{1,0:T(8,128)} %copy-done) | copy-start | bytes 12582916
  99.2 27.5 %all-to-all-start.3 = ((f32[4,512,256]{2,1,0:T(8,128)}), f32[4,512,256]{2,1,0:T(8,128)S(1)}, u32[]{:S(2)}, u32[]{:S(2)}) async-start(f32[4,512,256]{2,1,0:T(8,128)} %bitcast.4), calls=%async_computation.3 | async-start | bytes 4194304 | tf_op jit(solution)/shard_map/all_to_all | solution.py:327
  102.8 1.3 collective-permute-start.12
  104.2 7.5 %collective-permute-start.16 = (f32[256,1024]{1,0:T(8,128)S(1)}, f32[256,1024]{1,0:T(8,128)S(1)}, u32[]{:S(2)}, u32[]{:S(2)}) collective-permute-start(f32[256,1024]{1,0:T(8,128)S(1)} %get-tuple-element.51.part_t), channel_id=1, source_target_pairs={{0,32},{32,0},{1,33},{33,1},{2,34},{34,2},{3,35},{35,3},{4,36},{36... | collective-permute-start | bytes 3145736 | tf_op jit(solution)/shard_map/ppermute | solution.py:339
  104.4 5.9 %collective-permute-start.15 = (f32[16,1024]{1,0:T(8,128)S(1)}, f32[16,1024]{1,0:T(8,128)S(1)}, u32[]{:S(2)}, u32[]{:S(2)}) collective-permute-start(f32[16,1024]{1,0:T(8,128)S(1)} %add.36.a), channel_id=1, source_target_pairs={{0,128},{64,192},{128,0},{192,64},{1,129},{65,193},{129,1},{193,65... | collective-permute-start | bytes 196616 | tf_op jit(solution)/shard_map/ppermute | solution.py:339
  106.1 5.6 %collective-permute-start.14 = (f32[16,1024]{1,0:T(8,128)S(1)}, f32[16,1024]{1,0:T(8,128)S(1)}, u32[]{:S(2)}, u32[]{:S(2)}) collective-permute-start(f32[16,1024]{1,0:T(8,128)S(1)} %add.36.a), channel_id=1, source_target_pairs={{0,192},{64,128},{128,64},{192,0},{1,193},{65,129},{129,65},{193,1... | collective-permute-start | bytes 196616 | tf_op jit(solution)/shard_map/ppermute | solution.py:339
  107.2 4.5 %collective-permute-start.13 = (f32[16,1024]{1,0:T(8,128)S(1)}, f32[16,1024]{1,0:T(8,128)S(1)}, u32[]{:S(2)}, u32[]{:S(2)}) collective-permute-start(f32[16,1024]{1,0:T(8,128)S(1)} %add.36.a), channel_id=1, source_target_pairs={{0,64},{64,0},{128,192},{192,128},{1,65},{65,1},{129,193},{193,129... | collective-permute-start | bytes 196616 | tf_op jit(solution)/shard_map/ppermute | solution.py:339
  112.1 3.8 %collective-permute-start.17 = (f32[16,256]{1,0:T(8,128)S(1)}, f32[16,256]{1,0:T(8,128)S(1)}, u32[]{:S(2)}, u32[]{:S(2)}) collective-permute-start(f32[16,256]{1,0:T(8,128)S(1)} %get-tuple-element.52), channel_id=1, source_target_pairs={{0,1},{1,0},{2,3},{3,2},{4,5},{5,4},{6,7},{7,6},{8,9},{9,8},{10,11... | collective-permute-start | bytes 49160 | tf_op jit(solution)/shard_map/ppermute | solution.py:339
  115.8 7.6 %collective-permute-start.20 = (f32[16,256]{1,0:T(8,128)S(1)}, f32[16,256]{1,0:T(8,128)S(1)}, u32[]{:S(2)}, u32[]{:S(2)}) collective-permute-start(f32[16,256]{1,0:T(8,128)S(1)} %add.37), channel_id=1, source_target_pairs={{0,4},{1,5},{2,6},{3,7},{4,0},{5,1},{6,2},{7,3},{8,12},{9,13},{10,... | collective-permute-start | bytes 49160 | tf_op jit(solution)/shard_map/ppermute | solution.py:339
  116.8 6.7 %collective-permute-start.19 = (f32[16,256]{1,0:T(8,128)S(1)}, f32[16,256]{1,0:T(8,128)S(1)}, u32[]{:S(2)}, u32[]{:S(2)}) collective-permute-start(f32[16,256]{1,0:T(8,128)S(1)} %add.37), channel_id=1, source_target_pairs={{0,6},{1,7},{2,4},{3,5},{4,2},{5,3},{6,0},{7,1},{8,14},{9,15},{10,... | collective-permute-start | bytes 49160 | tf_op jit(solution)/shard_map/ppermute | solution.py:339
  120.2 4.6 %collective-permute-start.18 = (f32[16,256]{1,0:T(8,128)S(1)}, f32[16,256]{1,0:T(8,128)S(1)}, u32[]{:S(2)}, u32[]{:S(2)}) collective-permute-start(f32[16,256]{1,0:T(8,128)S(1)} %add.37), channel_id=1, source_target_pairs={{0,2},{1,3},{2,0},{3,1},{4,6},{5,7},{6,4},{7,5},{8,10},{9,11},{10,... | collective-permute-start | bytes 49160 | tf_op jit(solution)/shard_map/ppermute | solution.py:339
  127.6 23.1 %all-to-all-start.4 = ((f32[8,64,256]{2,1,0:T(8,128)}), f32[8,64,256]{2,1,0:T(8,128)S(1)}, u32[]{:S(2)}, u32[]{:S(2)}) async-start(f32[8,64,256]{2,1,0:T(8,128)} %bitcast.3), calls=%async_computation.4 | async-start | bytes 1048576 | tf_op jit(solution)/shard_map/all_to_all | solution.py:327
  131.7 1.2 collective-permute-start.21
  132.9 5.1 %collective-permute-start.23 = (f32[32,256]{1,0:T(8,128)S(1)}, f32[32,256]{1,0:T(8,128)S(1)}, u32[]{:S(2)}, u32[]{:S(2)}) collective-permute-start(f32[32,256]{1,0:T(8,128)S(1)} %pad_maximum_fusion), channel_id=1, source_target_pairs={{0,192},{64,128},{128,64},{192,0},{1,193},{65,129},{129,65},{193,1... | collective-permute-start | bytes 98312 | tf_op jit(solution)/shard_map/ppermute | solution.py:339
  135.0 5.4 %collective-permute-start.24 = (f32[32,256]{1,0:T(8,128)S(1)}, f32[32,256]{1,0:T(8,128)S(1)}, u32[]{:S(2)}, u32[]{:S(2)}) collective-permute-start(f32[32,256]{1,0:T(8,128)S(1)} %pad_maximum_fusion), channel_id=1, source_target_pairs={{0,128},{64,192},{128,0},{192,64},{1,129},{65,193},{129,1},{193,65... | collective-permute-start | bytes 98312 | tf_op jit(solution)/shard_map/ppermute | solution.py:339
  135.6 4.8 %collective-permute-start.22 = (f32[32,256]{1,0:T(8,128)S(1)}, f32[32,256]{1,0:T(8,128)S(1)}, u32[]{:S(2)}, u32[]{:S(2)}) collective-permute-start(f32[32,256]{1,0:T(8,128)S(1)} %pad_maximum_fusion), channel_id=1, source_target_pairs={{0,64},{64,0},{128,192},{192,128},{1,65},{65,1},{129,193},{193,129... | collective-permute-start | bytes 98312 | tf_op jit(solution)/shard_map/ppermute | solution.py:339
  137.0 7.1 %collective-permute-start.28 = (f32[16,1024]{1,0:T(8,128)S(1)}, f32[16,1024]{1,0:T(8,128)S(1)}, u32[]{:S(2)}, u32[]{:S(2)}) collective-permute-start(f32[16,1024]{1,0:T(8,128)S(1)} %get-tuple-element.53.factor_mine), channel_id=1, source_target_pairs={{0,32},{32,0},{1,33},{33,1},{2,34},{34,2},{3,35},{35,3},{4,36},{36... | collective-permute-start | bytes 196616 | tf_op jit(solution)/shard_map/ppermute | solution.py:339
  140.4 5.6 %collective-permute-start.27 = (f32[32,256]{1,0:T(8,128)S(1)}, f32[32,256]{1,0:T(8,128)S(1)}, u32[]{:S(2)}, u32[]{:S(2)}) collective-permute-start(f32[32,256]{1,0:T(8,128)S(1)} %add_add_fusion.mixed_a), channel_id=1, source_target_pairs={{0,16},{8,24},{16,0},{24,8},{1,17},{9,25},{17,1},{25,9},{2,18},{10... | collective-permute-start | bytes 98312 | tf_op jit(solution)/shard_map/ppermute | solution.py:339
  142.9 5.1 %collective-permute-start.26 = (f32[32,256]{1,0:T(8,128)S(1)}, f32[32,256]{1,0:T(8,128)S(1)}, u32[]{:S(2)}, u32[]{:S(2)}) collective-permute-start(f32[32,256]{1,0:T(8,128)S(1)} %add_add_fusion.mixed_a), channel_id=1, source_target_pairs={{0,24},{8,16},{16,8},{24,0},{1,25},{9,17},{17,9},{25,1},{2,26},{10... | collective-permute-start | bytes 98312 | tf_op jit(solution)/shard_map/ppermute | solution.py:339
  144.1 4.0 %collective-permute-start.25 = (f32[32,256]{1,0:T(8,128)S(1)}, f32[32,256]{1,0:T(8,128)S(1)}, u32[]{:S(2)}, u32[]{:S(2)}) collective-permute-start(f32[32,256]{1,0:T(8,128)S(1)} %add_add_fusion.mixed_a), channel_id=1, source_target_pairs={{0,8},{8,0},{16,24},{24,16},{1,9},{9,1},{17,25},{25,17},{2,10},{10... | collective-permute-start | bytes 98312 | tf_op jit(solution)/shard_map/ppermute | solution.py:339
